TPU v7x, 32 devices: a whole 2x2x4 slice. The times are simulated.
32 devices in a mesh: dp: 8 (over z, x), tensor: 4 (over y, core).
Axes of the slice: x: 2, y: 2, z: 4, core: 2. Of those that a mesh axis runs over, the one named last changes fastest.
Arguments:
- tokens: bfloat16 [16384, 768], P(('dp', 'tensor')), may hold values from -6 to 6
- seg_lengths: int32 [8, 13], P('dp'), may hold values from 32 to 1024, as said below
- parents: int32 [8, 13], P('dp'), may hold values from 0 to 4, as said below
- qkv_latent: float32 [768, 3, 768], P(None, None, 'tensor'), may hold values from -0.3125 to 0.3125
- qv_bias: bfloat16 [2, 768], P(None, 'tensor'), may hold values from -3 to 3
- out_latent: float32 [768, 768], P('tensor'), may hold values from -1.75 to 1.75
- out_bias: bfloat16 [768], replicated, may hold values from -3 to 3
- norm1_gain: bfloat16 [768], replicated, may hold values from 0.5 to 1.5
- norm1_shift: bfloat16 [768], replicated, may hold values from -3 to 3
- up_latent: float32 [768, 3072], P(None, 'tensor'), may hold values from -0.21875 to 0.21875
- up_bias: bfloat16 [3072], P('tensor'), may hold values from -3 to 3
- down_latent: float32 [3072, 768], P('tensor'), may hold values from -0.109375 to 0.109375
- down_bias: bfloat16 [768], replicated, may hold values from -3 to 3
- norm2_gain: bfloat16 [768], replicated, may hold values from 0.5 to 1.5
- norm2_shift: bfloat16 [768], replicated, may hold values from -3 to 3
- teacher_qkv: bfloat16 [768, 3, 768], P(None, None, 'tensor'), may hold values from -0.3125 to 0.3125
- teacher_qv_bias: bfloat16 [2, 768], P(None, 'tensor'), may hold values from -3 to 3
- teacher_out: bfloat16 [768, 768], P('tensor'), may hold values from -1.75 to 1.75
- teacher_out_bias: bfloat16 [768], replicated, may hold values from -3 to 3
- teacher_norm1_gain: bfloat16 [768], replicated, may hold values from 0.5 to 1.5
- teacher_norm1_shift: bfloat16 [768], replicated, may hold values from -3 to 3
- teacher_up: bfloat16 [768, 3072], P(None, 'tensor'), may hold values from -0.21875 to 0.21875
- teacher_up_bias: bfloat16 [3072], P('tensor'), may hold values from -3 to 3
- teacher_down: bfloat16 [3072, 768], P('tensor'), may hold values from -0.109375 to 0.109375
- teacher_down_bias: bfloat16 [768], replicated, may hold values from -3 to 3
- teacher_norm2_gain: bfloat16 [768], replicated, may hold values from 0.5 to 1.5
- teacher_norm2_shift: bfloat16 [768], replicated, may hold values from -3 to 3
Outputs:
- output: bfloat16 [16384, 768], P(('dp', 'tensor'))
- loss: float32 [8], P('dp')
- input_grad: float32 [16384, 768], P(('dp', 'tensor'))
- qkv_latent_grad: float32 [768, 3, 768], P(None, None, 'tensor')
- qv_bias_grad: float32 [2, 768], P(None, 'tensor')
- out_latent_grad: float32 [768, 768], P('tensor')
- out_bias_grad: float32 [768], replicated
- norm1_gain_grad: float32 [768], replicated
- norm1_shift_grad: float32 [768], replicated
- up_latent_grad: float32 [768, 3072], P(None, 'tensor')
- up_bias_grad: float32 [3072], P('tensor')
- down_latent_grad: float32 [3072, 768], P('tensor')
- down_bias_grad: float32 [768], replicated
- norm2_gain_grad: float32 [768], replicated
- norm2_shift_grad: float32 [768], replicated
Inputs may be any that keep to these rules, and one draw needn't show every extreme that they name: `seg_lengths`: segments of a tree lie in order: segment 0 is the trunk with exactly 1024 tokens, then 4 branches whose lengths taken in pairs sum to 256, then 4 * 2 leaves whose lengths taken in pairs sum to 128; the lengths of a tree sum to 2048. `parents`: the trunk's and every branch's parent is 0; every leaf's parent is a branch, and each branch is the parent of exactly 2 leaves.
All inputs are finite; a program needn't handle non-finite values.
Results may differ from a plain program's by a relative error of at most 0.014.
The roundings to bfloat16 on the way count: a program that leaves them out, or rounds other values in their place, can miss the bound.
Values may be sent and summed in bfloat16 or wider, within the bound.
A program may use at most 128 MiB of HBM per device.

v0:
```python
import jax
import jax.numpy as jnp
from jax import lax
from jax.sharding import PartitionSpec as P

HEAD_DIM = 64


CLIP_RANGE = 3.0
NORM_EPSILON = 1e-05
MASKED_SCORE = -1e30


def clip_act(values):
    return CLIP_RANGE * jnp.tanh(values / CLIP_RANGE)


def clip_slope(values):
    level = jnp.tanh(values / CLIP_RANGE)
    return 1.0 - level * level


def gelu_slope(upward):
    normal_cdf = 0.5 * (1.0 + lax.erf(upward * 0.7071067811865476))
    density = jnp.exp(-0.5 * upward * upward) * 0.3989422804014327
    return normal_cdf + upward * density


def norm_forward(hidden, gain, shift):
    row_mean = jnp.mean(hidden, axis=-1, keepdims=True)
    centred = hidden - row_mean
    inv_std = lax.rsqrt(jnp.mean(centred * centred, axis=-1, keepdims=True) + NORM_EPSILON)
    normed = centred * inv_std
    return (normed * gain + shift, normed, inv_std)


def norm_backward(grad_out, normed, inv_std, gain):
    grad_normed = grad_out * gain
    centre = jnp.mean(grad_normed, axis=-1, keepdims=True)
    inner_sum = jnp.mean(grad_normed * normed, axis=-1, keepdims=True)
    grad_in = inv_std * (grad_normed - centre - normed * inner_sum)
    return (grad_in, jnp.sum(grad_out * normed, axis=0), jnp.sum(grad_out, axis=0))


def lookup(indices, lookup_table):
    labels = jnp.arange(lookup_table.shape[0], dtype=jnp.int32)
    picked = jnp.where(indices[:, None] == labels[None, :], lookup_table[None, :], 0)
    return jnp.sum(picked, axis=1)


def token_links(lengths, parent, all_rows):
    seg_ends = jnp.cumsum(lengths)
    starts = seg_ends - lengths
    positions = jnp.arange(all_rows, dtype=jnp.int32)
    seg_ids = jnp.sum((positions[:, None] >= starts[None, :]).astype(jnp.int32), axis=1) - 1
    grand_parent = lookup(parent, parent)
    return (seg_ids, lookup(seg_ids, parent), lookup(seg_ids, grand_parent))


def path_mask(row_links, col_links):
    row_seg, row_one, row_two = row_links
    col_seg, col_one, col_two = col_links
    allowed = (col_seg[None, :] == row_seg[:, None]) | (col_seg[None, :] == row_one[:, None])
    allowed = (
        allowed | (col_seg[None, :] == row_two[:, None]) | (col_one[None, :] == row_seg[:, None])
    )
    return allowed | (col_two[None, :] == row_seg[:, None])


def contract_rows(left, right):
    return lax.dot_general(
        left, right, (((0,), (0,)), ((), ())), preferred_element_type=jnp.float32
    )


def contract_cols(left, right):
    return lax.dot_general(
        left, right, (((1,), (1,)), ((), ())), preferred_element_type=jnp.float32
    )


def block_scores(query_block, key_rows, row_links, path_links):
    scores = (
        jnp.einsum("qhd,khd->hqk", query_block, key_rows, preferred_element_type=jnp.float32)
        * 0.125
    )
    allowed = path_mask(row_links, path_links)
    return jnp.where(allowed[None], scores, MASKED_SCORE)


def attend_forward(queries, key_rows, values, path_links, row_block):
    all_rows, local_heads, head_dim = queries.shape
    blocks = all_rows // row_block
    query_blocks = queries.reshape(blocks, row_block, local_heads, head_dim)
    row_parts = tuple((element.reshape(blocks, row_block) for element in path_links))

    def one_block(inputs):
        query_block, row_seg, row_one, row_two = inputs
        scores = block_scores(query_block, key_rows, (row_seg, row_one, row_two), path_links)
        peak = jnp.max(scores, axis=-1, keepdims=True)
        raised = jnp.exp(scores - peak)
        total = jnp.sum(raised, axis=-1, keepdims=True)
        weights = (raised / total).astype(jnp.bfloat16)
        context = jnp.einsum("hqk,khd->qhd", weights, values, preferred_element_type=jnp.float32)
        return (context, (peak + jnp.log(total))[..., 0])

    context, log_sums = lax.map(one_block, (query_blocks,) + row_parts)
    return (context.reshape(all_rows, local_heads * head_dim), log_sums)


def attend_backward(queries, key_rows, values, grad_context, log_sums, path_links, row_block):
    all_rows, local_heads, head_dim = queries.shape
    blocks = all_rows // row_block
    query_blocks = queries.reshape(blocks, row_block, local_heads, head_dim)
    grad_blocks = grad_context.reshape(blocks, row_block, local_heads, head_dim)
    row_parts = tuple((element.reshape(blocks, row_block) for element in path_links))

    def one_block(carry, inputs):
        grad_keys, grad_values = carry
        query_block, grad_block, log_block, row_seg, row_one, row_two = inputs
        scores = block_scores(query_block, key_rows, (row_seg, row_one, row_two), path_links)
        weights = jnp.exp(scores - log_block[..., None])
        grad_weights = jnp.einsum(
            "qhd,khd->hqk", grad_block, values, preferred_element_type=jnp.float32
        )
        inner_sum = jnp.sum(weights * grad_weights, axis=-1, keepdims=True)
        grad_scores = (weights * (grad_weights - inner_sum)).astype(jnp.bfloat16)
        grad_queries = (
            jnp.einsum("hqk,khd->qhd", grad_scores, key_rows, preferred_element_type=jnp.float32)
            * 0.125
        )
        grad_keys = (
            grad_keys
            + jnp.einsum(
                "hqk,qhd->khd", grad_scores, query_block, preferred_element_type=jnp.float32
            )
            * 0.125
        )
        grad_values = grad_values + jnp.einsum(
            "hqk,qhd->khd",
            weights.astype(jnp.bfloat16),
            grad_block,
            preferred_element_type=jnp.float32,
        )
        return ((grad_keys, grad_values), grad_queries)

    zero_grads = jnp.zeros((all_rows, local_heads, head_dim), jnp.float32)
    (grad_keys, grad_values), grad_queries = lax.scan(
        one_block, (zero_grads, zero_grads), (query_blocks, grad_blocks, log_sums) + row_parts
    )
    return (
        grad_queries.reshape(all_rows, local_heads * head_dim),
        grad_keys.reshape(all_rows, -1),
        grad_values.reshape(all_rows, -1),
    )


def project_heads(source, weight, bias, all_rows, local_heads):
    projected = jnp.einsum("td,dcf->tcf", source, weight, preferred_element_type=jnp.float32)
    wide_bias = bias.astype(jnp.float32)
    queries = (
        (projected[:, 0] + wide_bias[0])
        .astype(jnp.bfloat16)
        .reshape(all_rows, local_heads, HEAD_DIM)
    )
    key_rows = projected[:, 1].astype(jnp.bfloat16).reshape(all_rows, local_heads, HEAD_DIM)
    values = (
        (projected[:, 2] + wide_bias[1])
        .astype(jnp.bfloat16)
        .reshape(all_rows, local_heads, HEAD_DIM)
    )
    return (queries, key_rows, values)


def body(
    tokens,
    seg_lengths,
    parents,
    qkv_latent,
    qv_bias,
    out_latent,
    out_bias,
    norm1_gain,
    norm1_shift,
    up_latent,
    up_bias,
    down_latent,
    down_bias,
    norm2_gain,
    norm2_shift,
    teacher_qkv,
    teacher_qv_bias,
    teacher_out,
    teacher_out_bias,
    teacher_norm1_gain,
    teacher_norm1_shift,
    teacher_up,
    teacher_up_bias,
    teacher_down,
    teacher_down_bias,
    teacher_norm2_gain,
    teacher_norm2_shift,
):
    own_rows, model_width = tokens.shape
    tensor_size = lax.axis_size("tensor")
    all_rows = own_rows * tensor_size
    row_block = all_rows // max(1, all_rows // 512)
    local_cols = qkv_latent.shape[2]
    local_heads = local_cols // HEAD_DIM
    hidden_all = up_latent.shape[1] * tensor_size
    out_sums, down_sums = lax.psum(
        (jnp.sum(jnp.abs(out_latent), axis=0), jnp.sum(jnp.abs(down_latent), axis=0)), "tensor"
    )
    w_qkv = (jnp.mean(jnp.abs(qkv_latent), axis=0) * jnp.sign(qkv_latent)).astype(jnp.bfloat16)
    w_out = (out_sums / model_width * jnp.sign(out_latent)).astype(jnp.bfloat16)
    w_up = (jnp.mean(jnp.abs(up_latent), axis=0) * jnp.sign(up_latent)).astype(jnp.bfloat16)
    w_down = (down_sums / hidden_all * jnp.sign(down_latent)).astype(jnp.bfloat16)
    path_links = token_links(seg_lengths[0], parents[0], all_rows)
    x_own = tokens.astype(jnp.float32)
    x_in = clip_act(x_own).astype(jnp.bfloat16)
    x_in_all, x_all = (
        lax.all_gather(x_in, "tensor", axis=0, tiled=True),
        lax.all_gather(tokens, "tensor", axis=0, tiled=True),
    )
    queries, key_rows, values = project_heads(x_in_all, w_qkv, qv_bias, all_rows, local_heads)
    t_queries, t_keys, t_values = project_heads(
        x_all, teacher_qkv, teacher_qv_bias, all_rows, local_heads
    )
    context, log_sums = attend_forward(queries, key_rows, values, path_links, row_block)
    t_context, unused = attend_forward(t_queries, t_keys, t_values, path_links, row_block)
    attn_in = clip_act(context).astype(jnp.bfloat16)
    t_context_in = t_context.astype(jnp.bfloat16)
    attn_part = jnp.dot(attn_in, w_out, preferred_element_type=jnp.float32)
    t_attn_part = jnp.dot(t_context_in, teacher_out, preferred_element_type=jnp.float32)
    attn_own, t_attn_own = (
        lax.psum_scatter(
            attn_part.astype(jnp.bfloat16), "tensor", scatter_dimension=0, tiled=True
        ).astype(jnp.float32),
        lax.psum_scatter(
            t_attn_part.astype(jnp.bfloat16), "tensor", scatter_dimension=0, tiled=True
        ).astype(jnp.float32),
    )
    gain_one = norm1_gain.astype(jnp.float32)
    gain_two = norm2_gain.astype(jnp.float32)
    y_one, normed_one, inv_one = norm_forward(
        x_own + attn_own + out_bias.astype(jnp.float32), gain_one, norm1_shift.astype(jnp.float32)
    )
    t_y_one, unused_n, unused_s = norm_forward(
        x_own + t_attn_own + teacher_out_bias.astype(jnp.float32),
        teacher_norm1_gain.astype(jnp.float32),
        teacher_norm1_shift.astype(jnp.float32),
    )
    y_one_in = clip_act(y_one).astype(jnp.bfloat16)
    t_y_one_in = t_y_one.astype(jnp.bfloat16)
    y_one_all, t_y_one_all = (
        lax.all_gather(y_one_in, "tensor", axis=0, tiled=True),
        lax.all_gather(t_y_one_in, "tensor", axis=0, tiled=True),
    )
    upward = jnp.dot(y_one_all, w_up, preferred_element_type=jnp.float32) + up_bias.astype(
        jnp.float32
    )
    t_upward = jnp.dot(
        t_y_one_all, teacher_up, preferred_element_type=jnp.float32
    ) + teacher_up_bias.astype(jnp.float32)
    gelu_vals = jax.nn.gelu(upward, approximate=False)
    gelu_in = clip_act(gelu_vals).astype(jnp.bfloat16)
    t_gelu_in = jax.nn.gelu(t_upward, approximate=False).astype(jnp.bfloat16)
    ffn_part = jnp.dot(gelu_in, w_down, preferred_element_type=jnp.float32)
    t_ffn_part = jnp.dot(t_gelu_in, teacher_down, preferred_element_type=jnp.float32)
    ffn_own, t_ffn_own = (
        lax.psum_scatter(
            ffn_part.astype(jnp.bfloat16), "tensor", scatter_dimension=0, tiled=True
        ).astype(jnp.float32),
        lax.psum_scatter(
            t_ffn_part.astype(jnp.bfloat16), "tensor", scatter_dimension=0, tiled=True
        ).astype(jnp.float32),
    )
    out_own, normed_two, inv_two = norm_forward(
        y_one + ffn_own + down_bias.astype(jnp.float32), gain_two, norm2_shift.astype(jnp.float32)
    )
    t_out_own, unused_a, unused_b = norm_forward(
        t_y_one + t_ffn_own + teacher_down_bias.astype(jnp.float32),
        teacher_norm2_gain.astype(jnp.float32),
        teacher_norm2_shift.astype(jnp.float32),
    )
    mismatch = out_own - t_out_own
    loss_part = jnp.sum(mismatch * mismatch)[None]
    grad_two, gain_two_grad, shift_two_grad = norm_backward(mismatch, normed_two, inv_two, gain_two)
    grad_ffn = grad_two.astype(jnp.bfloat16)
    down_bias_grad = jnp.sum(grad_ffn.astype(jnp.float32), axis=0)
    grad_ffn_all = lax.all_gather(grad_ffn, "tensor", axis=0, tiled=True)
    down_grad = contract_rows(gelu_in, grad_ffn_all)
    grad_gelu = contract_cols(grad_ffn_all, w_down)
    grad_up = (grad_gelu * clip_slope(gelu_vals) * gelu_slope(upward)).astype(jnp.bfloat16)
    up_bias_grad = jnp.sum(grad_up.astype(jnp.float32), axis=0)
    up_grad = contract_rows(y_one_all, grad_up)
    grad_y_in = lax.psum_scatter(
        contract_cols(grad_up, w_up).astype(jnp.bfloat16), "tensor", scatter_dimension=0, tiled=True
    ).astype(jnp.float32)
    grad_y_one = grad_two + grad_y_in * clip_slope(y_one)
    grad_h, gain_one_grad, shift_one_grad = norm_backward(grad_y_one, normed_one, inv_one, gain_one)
    grad_attn = grad_h.astype(jnp.bfloat16)
    out_bias_grad = jnp.sum(grad_attn.astype(jnp.float32), axis=0)
    grad_attn_all = lax.all_gather(grad_attn, "tensor", axis=0, tiled=True)
    out_grad = contract_rows(attn_in, grad_attn_all)
    grad_context = (contract_cols(grad_attn_all, w_out) * clip_slope(context)).astype(jnp.bfloat16)
    grad_context = grad_context.reshape(all_rows, local_heads, HEAD_DIM)
    grad_queries, grad_keys, grad_values = attend_backward(
        queries, key_rows, values, grad_context, log_sums, path_links, row_block
    )
    grad_proj = jnp.stack([grad_queries, grad_keys, grad_values], axis=1).astype(jnp.bfloat16)
    qv_bias_grad = jnp.stack(
        [
            jnp.sum(grad_proj[:, 0].astype(jnp.float32), axis=0),
            jnp.sum(grad_proj[:, 2].astype(jnp.float32), axis=0),
        ]
    )
    qkv_grad = jnp.einsum("td,tcf->dcf", x_in_all, grad_proj, preferred_element_type=jnp.float32)
    grad_x_in = lax.psum_scatter(
        jnp.einsum("tcf,dcf->td", grad_proj, w_qkv, preferred_element_type=jnp.float32).astype(
            jnp.bfloat16
        ),
        "tensor",
        scatter_dimension=0,
        tiled=True,
    ).astype(jnp.float32)
    input_grad = grad_h + grad_x_in * clip_slope(x_own)
    shared_grads = jnp.stack(
        [
            out_bias_grad,
            gain_one_grad,
            shift_one_grad,
            down_bias_grad,
            gain_two_grad,
            shift_two_grad,
        ]
    )
    loss_sum, shared_grads = lax.psum((loss_part, shared_grads), "tensor")
    qkv_grad, qv_bias_grad, out_grad, up_grad, up_bias_grad, down_grad, shared_grads = lax.psum(
        (qkv_grad, qv_bias_grad, out_grad, up_grad, up_bias_grad, down_grad, shared_grads), "dp"
    )
    tree_loss = loss_sum / (all_rows * model_width)
    return (
        out_own.astype(jnp.bfloat16),
        tree_loss,
        input_grad,
        qkv_grad,
        qv_bias_grad,
        out_grad,
        shared_grads[0],
        shared_grads[1],
        shared_grads[2],
        up_grad,
        up_bias_grad,
        down_grad,
        shared_grads[3],
        shared_grads[4],
        shared_grads[5],
    )


def solution(mesh):
    in_specs = (
        P(("dp", "tensor"), None),
        P("dp", None),
        P("dp", None),
        P(None, None, "tensor"),
        P(None, "tensor"),
        P("tensor", None),
        P(),
        P(),
        P(),
        P(None, "tensor"),
        P("tensor"),
        P("tensor", None),
        P(),
        P(),
        P(),
        P(None, None, "tensor"),
        P(None, "tensor"),
        P("tensor", None),
        P(),
        P(),
        P(),
        P(None, "tensor"),
        P("tensor"),
        P("tensor", None),
        P(),
        P(),
        P(),
    )
    out_specs = (
        P(("dp", "tensor"), None),
        P("dp"),
        P(("dp", "tensor"), None),
        P(None, None, "tensor"),
        P(None, "tensor"),
        P("tensor", None),
        P(),
        P(),
        P(),
        P(None, "tensor"),
        P("tensor"),
        P("tensor", None),
        P(),
        P(),
        P(),
    )
    return jax.shard_map(body, mesh=mesh, in_specs=in_specs, out_specs=out_specs, check_vma=False)
```

profile of v0, /device:TPU:0, one launch (start us, length us, event | category | flops | bytes accessed | tf_op | source)
XLA Modules:
  0.0 1056.2 jit_solution(15064911923213269148)
XLA Ops:
  23.7 9.7 all-reduce.3
  47.7 24.2 %all-gather.7.cloned.1.call-done = bf16[2048,768]{1,0:T(8,128)(2,1)} async-done(((bf16[512,768]{1,0:T(8,128)(2,1)}), bf16[2048,768]{1,0:T(8,128)(2,1)}) %all-gather.7.cloned.1.call-update) | async-done | bytes 3145744 | tf_op jit(solution)/shard_map/all_gather | solution.py:222
  84.9 86.4 %while.41 = (s32[]{:T(128)}, bf16[4,512,3,64]{1,3,2,0:T(8,128)(2,1)}, s32[2048]{0:T(1024)S(1)}, s32[4,512]{1,0:T(4,128)}, s32[4,512]{1,0:T(4,128)}, /*index=5*/s...) while((s32[]{:T(128)}, ...), condition=%wide.region_24.25_spmd.clone, body=%wide.region_21.24_spmd.sunk.clone | while | flops 833619968 | bytes 29481092 | solution.py:107
  89.3 10.1 fusion.248
  99.3 7.5 fusion.249
  110.7 10.1 fusion.248
  120.8 7.5 fusion.249
  132.2 10.1 fusion.248
  142.3 7.5 fusion.249
  153.7 10.1 fusion.248
  163.7 7.5 fusion.249
  182.7 102.0 %while.40 = (s32[]{:T(128)}, f32[4,512,3,64]{1,3,2,0:T(8,128)}, f32[4,3,512]{2,1,0:T(4,128)}, s32[2048]{0:T(1024)S(1)}, s32[4,512]{1,0:T(4,128)}, /*index=5*/s32...) while((s32[]{:T(128)}, f32[4,512,3,64]{1,3,2,0:T(8,128)}, ...), condition=%wide.region_9.10_spmd.clone, body=%wide.region_6.9_spmd.sunk.clone | while | flops 852490752 | bytes 44200080 | solution.py:107
  200.6 7.4 fusion.244
  226.0 7.3 fusion.244
  251.3 7.3 fusion.244
  276.7 7.3 fusion.244
  296.3 34.6 %reduce-scatter.7.cloned.1.call-done = bf16[512,768]{1,0:T(8,128)(2,1)} async-done(((bf16[2048,768]{1,0:T(8,128)(2,1)}), bf16[512,768]{1,0:T(8,128)(2,1)}) %reduce-scatter.7.cloned.1.call-update) | async-done | bytes 786448 | tf_op jit(solution)/shard_map/reduce_scatter | solution.py:236
  339.8 26.8 %all-gather.13.cloned.1.call-done = bf16[2048,768]{1,0:T(8,128)(2,1)} async-done(((bf16[512,768]{1,0:T(8,128)(2,1)}), bf16[2048,768]{1,0:T(8,128)(2,1)}) %all-gather.13.cloned.1.call-update) | async-done | bytes 3145744 | tf_op jit(solution)/shard_map/all_gather | solution.py:257
  366.6 20.7 %convolution_convert_fusion.1 = bf16[2048,768]{1,0:T(8,128)(2,1)} fusion(bf16[768,768]{1,0:T(8,128)(2,1)S(1)} %copy-done, bf16[2048,768]{1,0:T(8,128)(2,1)} %all-gather.13.cloned.1.call-done, bf16[768,768]{1,0:T(8,128)(2,1)} %param.54, f32[768]{0:T(1024)} %convert_element_type.239), kind=kOutput, calls=%fused_computation.129 | convolution fusion | flops 4937220096 | bytes 8653824 | tf_op jit(solution)/shard_map/dot_general | solution.py:269
  389.9 7.3 all-gather.9.cloned.1.call-done
  397.1 20.9 %fusion.71 = (f32[2048,768]{1,0:T(8,128)S(1)}, f32[2048,768]{1,0:T(8,128)}) fusion(f32[768]{0:T(1024)S(1)} %convert_element_type.218, bf16[2048,768]{1,0:T(8,128)(2,1)} %all-gather.9.cloned.1.call-done, f32[768,768]{1,0:T(8,128)} %param.42, f32[768]{0:T(1024)S(1)} %broadcast_multiply_fusion.1), kind=kOutput, calls=%fused_computation.85 | convolution fusion | flops 2521497600 | bytes 18094080 | tf_op jit(solution)/shard_map/dot_general | solution.py:259
  425.7 12.0 %reduce-scatter.13.cloned.1.call-done = bf16[512,768]{1,0:T(8,128)(2,1)} async-done(((bf16[2048,768]{1,0:T(8,128)(2,1)}), bf16[512,768]{1,0:T(8,128)(2,1)}) %reduce-scatter.13.cloned.1.call-update) | async-done | bytes 786448 | tf_op jit(solution)/shard_map/reduce_scatter | solution.py:274
  437.7 40.7 %reduce-scatter.9.cloned.1.call-done = bf16[512,768]{1,0:T(8,128)(2,1)} async-done(((bf16[2048,768]{1,0:T(8,128)(2,1)}), bf16[512,768]{1,0:T(8,128)(2,1)}) %reduce-scatter.9.cloned.1.call-update) | async-done | bytes 786448 | tf_op jit(solution)/shard_map/reduce_scatter | solution.py:271
  487.4 28.6 %all-gather.15.cloned.1.call-done = bf16[2048,768]{1,0:T(8,128)(2,1)} async-done(((bf16[512,768]{1,0:T(8,128)(2,1)}), bf16[2048,768]{1,0:T(8,128)(2,1)}) %all-gather.15.cloned.1.call-update) | async-done | bytes 3145744 | tf_op jit(solution)/shard_map/all_gather | solution.py:291
  516.1 11.5 %convert_reduce_fusion = (f32[768]{0:T(1024)}, bf16[2048,768]{1,0:T(8,128)(2,1)S(1)}) fusion(f32[2048,768]{1,0:T(8,128)} %get-tuple-element.462, f32[768]{0:T(1024)S(1)} %convert_element_type.218, f32[2048,768]{1,0:T(8,128)} %copy-done.24, bf16[2048,768]{1,0:T(8,128)(2,1)} %all-gather.15.cloned.1.call-done, f32[768,768]{1,0:T(8,128)} %param.44, ...), kind=kOutput, calls=%fused_computation.96 | convolution fusion | flops 2442853632 | bytes 21242880 | tf_op jit(solution)/shard_map/dot_general | solution.py:77
  533.6 38.1 %reduce-scatter.15.cloned.1.call-done = bf16[512,768]{1,0:T(8,128)(2,1)} async-done(((bf16[2048,768]{1,0:T(8,128)(2,1)}), bf16[512,768]{1,0:T(8,128)(2,1)}) %reduce-scatter.15.cloned.1.call-update) | async-done | bytes 786448 | tf_op jit(solution)/shard_map/reduce_scatter | solution.py:297
  580.7 25.5 %all-gather.17.cloned.1.call-done = bf16[2048,768]{1,0:T(8,128)(2,1)} async-done(((bf16[512,768]{1,0:T(8,128)(2,1)}), bf16[2048,768]{1,0:T(8,128)(2,1)}) %all-gather.17.cloned.1.call-update) | async-done | bytes 3145744 | tf_op jit(solution)/shard_map/all_gather | solution.py:304
  610.2 141.5 %while.42 = (s32[]{:T(128)}, f32[2048,3,64]{0,2,1:T(8,128)}, f32[2048,3,64]{0,2,1:T(8,128)}, bf16[4,512,3,64]{1,3,2,0:T(8,128)(2,1)}, bf16[4,512,3,64]{1,3,2,0:T...) while((s32[]{:T(128)}, f32[2048,3,64]{0,2,1:T(8,128)}, ...), condition=%wide.region_40.41_spmd.clone.clone, body=%wide.region_38.40_spmd.clone.sunk.clone | while | flops 2071951872 | bytes 150460816 | solution.py:148
  768.4 7.7 fusion.110
  784.8 12.9 %all-reduce.2 = (f32[1]{0:T(128)}, f32[6,768]{1,0:T(8,128)S(1)}) all-reduce(f32[1]{0:T(128)} %bitcast.23, f32[6,768]{1,0:T(8,128)S(1)} %stack.44), channel_id=1, replica_groups=mesh['dp'=8,'tensor'=4] {'tensor'}, use_global_device_ids=true, to_apply=%region_32.33 | all-reduce | flops 4609 | bytes 36872 | tf_op jit(solution)/shard_map/psum | solution.py:338
  801.0 38.9 %all-reduce = (f32[2,192]{1,0:T(2,128)}, f32[6,768]{1,0:T(8,128)S(1)}, f32[768]{0:T(1024)}) all-reduce(f32[2,192]{1,0:T(2,128)S(1)} %pad_maximum_fusion.1, f32[6,768]{1,0:T(8,128)S(1)} %get-tuple-element.422, f32[768]{0:T(1024)S(1)} %copy-done.81), channel_id=1, replica_groups=mesh['dp'=8,'tensor'=4] {'dp'}, use_global_device_ids=true, to_apply=%region_45.46 | all-reduce | flops 5760 | bytes 46080 | tf_op jit(solution)/shard_map/psum | solution.py:339
  843.9 197.9 %all-reduce.6.cloned.1.call-done = (f32[768,3,192]{0,2,1:T(8,128)}, f32[192,768]{1,0:T(8,128)}, f32[768,768]{1,0:T(8,128)}, f32[768,768]{1,0:T(8,128)}) async-done(((f32[768,3,192]{0,2,1:T(8,128)}, f32[192,768]{1,0:T(8,128)}, f32[768,768]{1,0:T(8,128)}, f32[768,768]{1,0:T(8,128)}), (f32[768,3,192]{0,2,1:T(8,128)}, f32[192,768]{1,0:T(8,128)}, f32[768,768]{1,0:T(8,128)}, ...) | async-done | bytes 7077904 | tf_op jit(solution)/shard_map/psum | solution.py:339
  (468 shorter events, 380.1 us)
Async XLA Ops:
  7.2 359.4 %copy-start = (bf16[768,768]{1,0:T(8,128)(2,1)S(1)}, bf16[768,768]{1,0:T(8,128)(2,1)}, u32[]{:S(2)}) copy-start(bf16[768,768]{1,0:T(8,128)(2,1)} %param.56) | copy-start | bytes 3538948
  7.2 33.9 %all-gather.11.cloned.1.call-start = ((), (), s32[]{:S(2)}) async-start(), calls=%async_computation.10 | async-start | bytes 3932160 | tf_op jit(solution)/shard_map/all_gather | solution.py:223
  8.0 63.9 %all-gather.7.cloned.1.call-start = ((), (), s32[]{:S(2)}) async-start(), calls=%async_computation.6 | async-start | bytes 3932160 | tf_op jit(solution)/shard_map/all_gather | solution.py:222
  10.3 286.0 %reduce-scatter.11.cloned.1.call-start = ((), (), s32[]{:S(2)}) async-start(), calls=%async_computation.11 | async-start | bytes 3932160 | tf_op jit(solution)/shard_map/reduce_scatter | solution.py:239
  175.9 155.0 %reduce-scatter.7.cloned.1.call-start = ((), (), s32[]{:S(2)}) async-start(), calls=%async_computation.7 | async-start | bytes 3932160 | tf_op jit(solution)/shard_map/reduce_scatter | solution.py:236
  292.7 73.9 %all-gather.13.cloned.1.call-start = ((), (), s32[]{:S(2)}) async-start(), calls=%async_computation.12 | async-start | bytes 3932160 | tf_op jit(solution)/shard_map/all_gather | solution.py:257
  337.9 59.3 %all-gather.9.cloned.1.call-start = ((), (), s32[]{:S(2)}) async-start(), calls=%async_computation.8 | async-start | bytes 3932160 | tf_op jit(solution)/shard_map/all_gather | solution.py:256
  338.5 99.2 %reduce-scatter.13.cloned.1.call-start = ((), (), s32[]{:S(2)}) async-start(), calls=%async_computation.13 | async-start | bytes 3932160 | tf_op jit(solution)/shard_map/reduce_scatter | solution.py:274
  387.3 91.1 %reduce-scatter.9.cloned.1.call-start = ((), (), s32[]{:S(2)}) async-start(), calls=%async_computation.9 | async-start | bytes 3932160 | tf_op jit(solution)/shard_map/reduce_scatter | solution.py:271
  424.9 53.4 %copy-start.16 = (bf16[512,768]{1,0:T(8,128)(2,1)S(1)}, bf16[512,768]{1,0:T(8,128)(2,1)}, u32[]{:S(2)}) copy-start(bf16[512,768]{1,0:T(8,128)(2,1)} %reduce-scatter.11.cloned.1.call-done) | copy-start | bytes 2359300
  424.9 53.4 %copy-start.46 = (f32[768]{0:T(1024)S(1)}, f32[768]{0:T(1024)}, u32[]{:S(2)}) copy-start(f32[768]{0:T(1024)} %convert_element_type.213) | copy-start | bytes 9220
  424.9 53.4 %copy-start.49 = (f32[768]{0:T(1024)S(1)}, f32[768]{0:T(1024)}, u32[]{:S(2)}) copy-start(f32[768]{0:T(1024)} %convert_element_type.214) | copy-start | bytes 9220
  425.0 53.4 %copy-start.52 = (f32[768]{0:T(1024)S(1)}, f32[768]{0:T(1024)}, u32[]{:S(2)}) copy-start(f32[768]{0:T(1024)} %convert_element_type.235) | copy-start | bytes 9220
  425.0 53.4 %copy-start.54 = (f32[512]{0:T(512)S(1)}, f32[512]{0:T(512)}, u32[]{:S(2)}) copy-start(f32[512]{0:T(512)} %copy-done.53) | copy-start | bytes 6148
  425.0 53.4 %copy-start.57 = (f32[512]{0:T(512)S(1)}, f32[512]{0:T(512)}, u32[]{:S(2)}) copy-start(f32[512]{0:T(512)} %copy-done.56) | copy-start | bytes 6148
  425.0 53.4 %copy-start.60 = (f32[768]{0:T(1024)S(1)}, f32[768]{0:T(1024)}, u32[]{:S(2)}) copy-start(f32[768]{0:T(1024)} %convert_element_type.215) | copy-start | bytes 9220
  425.0 53.4 %copy-start.64 = (f32[768]{0:T(1024)S(1)}, f32[768]{0:T(1024)}, u32[]{:S(2)}) copy-start(f32[768]{0:T(1024)} %convert_element_type.236) | copy-start | bytes 9220
  425.0 53.4 %copy-start.66 = (f32[768]{0:T(1024)S(1)}, f32[768]{0:T(1024)}, u32[]{:S(2)}) copy-start(f32[768]{0:T(1024)} %convert_element_type.237) | copy-start | bytes 9220
  425.1 91.0 %all-gather.15.cloned.1.call-start = ((), (), s32[]{:S(2)}) async-start(), calls=%async_computation.14 | async-start | bytes 3932160 | tf_op jit(solution)/shard_map/all_gather | solution.py:291
  487.4 84.3 %reduce-scatter.15.cloned.1.call-start = ((), (), s32[]{:S(2)}) async-start(), calls=%async_computation.15 | async-start | bytes 3932160 | tf_op jit(solution)/shard_map/reduce_scatter | solution.py:297
  533.5 72.7 %all-gather.17.cloned.1.call-start = ((), (), s32[]{:S(2)}) async-start(), calls=%async_computation.16 | async-start | bytes 3932160 | tf_op jit(solution)/shard_map/all_gather | solution.py:304
  577.6 263.0 %reduce-scatter.17.cloned.1.call-start = ((), (), s32[]{:S(2)}) async-start(), calls=%async_computation.17 | async-start | bytes 3932160 | tf_op jit(solution)/shard_map/reduce_scatter | solution.py:319
  761.3 280.5 %all-reduce.6.cloned.1.call-start = ((), (), s32[]{:S(2)}) async-start(), calls=%async_computation.18 | async-start | bytes 14155776 | tf_op jit(solution)/shard_map/psum | solution.py:339
  784.0 56.5 %copy-start.7 = (bf16[512,768]{1,0:T(8,128)(2,1)S(1)}, bf16[512,768]{1,0:T(8,128)(2,1)}, u32[]{:S(2)}) copy-start(bf16[512,768]{1,0:T(8,128)(2,1)} %param.33) | copy-start | bytes 2359300
  784.1 56.5 %copy-start.11 = (bf16[512,768]{1,0:T(8,128)(2,1)S(1)}, bf16[512,768]{1,0:T(8,128)(2,1)}, u32[]{:S(2)}) copy-start(bf16[512,768]{1,0:T(8,128)(2,1)} %reduce-scatter.7.cloned.1.call-done) | copy-start | bytes 2359300
  784.1 56.5 %copy-start.14 = (f32[512,768]{1,0:T(8,128)S(1)}, f32[512,768]{1,0:T(8,128)}, u32[]{:S(2)}) copy-start(f32[512,768]{1,0:T(8,128)} %copy-done.13) | copy-start | bytes 4718596
  784.1 56.5 %copy-start.47 = (f32[768]{0:T(1024)S(1)}, f32[768]{0:T(1024)}, u32[]{:S(2)}) copy-start(f32[768]{0:T(1024)} %convert_element_type.213) | copy-start | bytes 9220
  784.1 56.5 %copy-start.50 = (f32[768]{0:T(1024)S(1)}, f32[768]{0:T(1024)}, u32[]{:S(2)}) copy-start(f32[768]{0:T(1024)} %convert_element_type.214) | copy-start | bytes 9220
  784.1 56.5 %copy-start.55 = (f32[512]{0:T(512)S(1)}, f32[512]{0:T(512)}, u32[]{:S(2)}) copy-start(f32[512]{0:T(512)} %copy-done.53) | copy-start | bytes 6148
  784.1 56.5 %copy-start.58 = (f32[512]{0:T(512)S(1)}, f32[512]{0:T(512)}, u32[]{:S(2)}) copy-start(f32[512]{0:T(512)} %copy-done.56) | copy-start | bytes 6148
  784.1 56.5 %copy-start.70 = (f32[512]{0:T(512)S(1)}, f32[512]{0:T(512)}, u32[]{:S(2)}) copy-start(f32[512]{0:T(512)} %copy-done.69) | copy-start | bytes 6148
  784.1 56.5 %copy-start.72 = (f32[512]{0:T(512)S(1)}, f32[512]{0:T(512)}, u32[]{:S(2)}) copy-start(f32[512]{0:T(512)} %copy-done.71) | copy-start | bytes 6148
  (103 other events, 644.8 us)
Sparse Core Ops, SparseCore 0:
  9.6 31.4 all-gather.10
  43.3 28.5 all-gather.6
  176.1 37.9 reduce-scatter.10
  292.8 38.0 reduce-scatter.6
  338.0 28.5 all-gather.12
  368.6 28.5 all-gather.8
  399.7 37.9 reduce-scatter.12
  440.4 37.9 reduce-scatter.8
  487.5 28.5 all-gather.14
  533.6 37.9 reduce-scatter.14
  577.7 28.5 all-gather.16
  761.4 38.4 reduce-scatter.16
  805.5 236.2 all-reduce.5
where the time goes:
time: 1060 us
  waiting for transfers between devices  443 us (42%)
  matrix products  323 us (30%)
  other arithmetic  146 us (14%)
  local copies, waits for them, and re-layouts  64.7 us (6%)
  blocking collectives  61.4 us (6%)
  between operations  17 us (2%)
    psum x1, waiting for transfers between devices, body(): lax.psum((qkv_grad, qv_bias_grad, out_grad, up_grad, up_bias_grad, down_g...  198 us
    dot_general x8, matrix products, one_block(): jnp.einsum('hqk,khd->qhd', weights, values, preferred_element_type=jnp.fl...  59.4 us
    reduce_scatter x1, waiting for transfers between devices, body(): lax.psum_scatter(ffn_part.astype(jnp.bfloat16), 'tensor', scatter_dimensi...  40.7 us
    sub x4, matrix products, one_block(): raised = jnp.exp(scores - peak)  40.2 us
    psum x1, blocking collectives, body(): lax.psum((qkv_grad, qv_bias_grad, out_grad, up_grad, up_bias_grad, down_g...  38.9 us
    reduce_scatter x1, waiting for transfers between devices, body(): lax.psum_scatter(contract_cols(grad_up, w_up).astype(jnp.bfloat16), 'tens...  38.1 us
    dot_general x8, matrix products, block_scores(): jnp.einsum('qhd,khd->hqk', query_block, key_rows, preferred_element_type=...  36 us
    reduce_scatter x1, waiting for transfers between devices, body(): lax.psum_scatter(attn_part.astype(jnp.bfloat16), 'tensor', scatter_dimens...  34.6 us
  transfers between devices with their start and end apart: 13, of which 11 were waited for; matrix products, arithmetic and copies ran while one was open for 21% of the time, Pallas kernels for 0%

commit v1 on v0

v1 whole, which is shorter than its diff:
```python
import functools

import jax
import jax.numpy as jnp
from jax import lax
from jax.experimental import pallas as pl
from jax.experimental.pallas import tpu as pltpu
from jax.sharding import PartitionSpec as P

HEAD_DIM = 64
LANES = 128
CLIP_RANGE = 3.0
NORM_EPSILON = 1e-05
MASKED_SCORE = -1e30
SEG_LANE = HEAD_DIM
ROW_TERM = HEAD_DIM + 16
Q_BLOCK = 256
BF16, F32 = jnp.bfloat16, jnp.float32
ROWS_ROWS = (((0,), (0,)), ((), ()))
COLS_COLS = (((1,), (1,)), ((), ()))


def clip_act(values):
    return CLIP_RANGE * jnp.tanh(values / CLIP_RANGE)


def clip_slope(values):
    level = jnp.tanh(values / CLIP_RANGE)
    return 1.0 - level * level


def gelu_slope(upward):
    normal_cdf = 0.5 * (1.0 + lax.erf(upward * 0.7071067811865476))
    density = jnp.exp(-0.5 * upward * upward) * 0.3989422804014327
    return normal_cdf + upward * density


def norm_forward(hidden, gain, shift):
    row_mean = jnp.mean(hidden, axis=-1, keepdims=True)
    centred = hidden - row_mean
    inv_std = lax.rsqrt(jnp.mean(centred * centred, axis=-1, keepdims=True) + NORM_EPSILON)
    normed = centred * inv_std
    return (normed * gain + shift, normed, inv_std)


def norm_backward(grad_out, normed, inv_std, gain):
    grad_normed = grad_out * gain
    centre = jnp.mean(grad_normed, axis=-1, keepdims=True)
    inner_sum = jnp.mean(grad_normed * normed, axis=-1, keepdims=True)
    grad_in = inv_std * (grad_normed - centre - normed * inner_sum)
    return (grad_in, jnp.sum(grad_out * normed, axis=0), jnp.sum(grad_out, axis=0))


def dot(left, right):
    return jnp.dot(left, right, preferred_element_type=F32)


def dot_rows(left, right):
    return lax.dot_general(left, right, ROWS_ROWS, preferred_element_type=F32)


def dot_cols(left, right):
    return lax.dot_general(left, right, COLS_COLS, preferred_element_type=F32)


def swap(array, bit):
    size = lax.axis_size("tensor")
    return lax.ppermute(array, "tensor", [(i, i ^ bit) for i in range(size)])


def gather_blocks(own):
    far = swap(own, 2)
    near = swap(own, 1)
    return [own, near, far, swap(far, 1)]


def exchange_blocks(blocks):
    far = swap(jnp.stack([blocks[2], blocks[3]]), 2)
    near = swap(jnp.stack([blocks[1], far[1]]), 1)
    return [blocks[0], near[0], far[0], near[1]]


def reduce_blocks(blocks):
    near = swap(jnp.stack([blocks[1], blocks[3]]).astype(BF16), 1).astype(F32)
    far = swap((blocks[2] + near[1]).astype(BF16), 2).astype(F32)
    return blocks[0] + near[0] + far


def sum_small(array):
    array = array + swap(array, 1)
    return array + swap(array, 2)


def lookup(indices, lookup_table):
    labels = jnp.arange(lookup_table.shape[0], dtype=jnp.int32)
    picked = jnp.where(indices[:, None] == labels[None, :], lookup_table[None, :], 0)
    return jnp.sum(picked, axis=1)


def segment_features(lengths, parent, positions):
    count = lengths.shape[0]
    labels = jnp.arange(count, dtype=jnp.int32)
    starts = jnp.sum(jnp.where(labels[None, :] < labels[:, None], lengths[None, :], 0), axis=1)
    seg_ids = jnp.sum((positions[:, None] >= starts[None, :]).astype(jnp.int32), axis=1) - 1
    grand_parent = lookup(parent, parent)
    one, two = parent, grand_parent
    row, col = labels[:, None], labels[None, :]
    allowed = (col == row) | (col == one[:, None]) | (col == two[:, None])
    allowed = allowed | (one[None, :] == row) | (two[None, :] == row)
    blocked = (~allowed).astype(F32)
    onehot = (seg_ids[:, None] == labels[None, :]).astype(F32)
    query_part = onehot * MASKED_SCORE
    key_part = dot(onehot.astype(BF16), blocked.astype(BF16))
    rows = positions.shape[0]
    pad = jnp.zeros((rows, 16 - count), F32)
    left = jnp.zeros((rows, HEAD_DIM), F32)
    right = jnp.zeros((rows, LANES - HEAD_DIM - 16), F32)
    ones = jnp.ones((rows, 3), F32)
    none = jnp.zeros((rows, LANES - HEAD_DIM - 19), F32)
    return jnp.concatenate(
        [
            left, query_part, pad, right,
            left, key_part, pad, ones, none,
            left, pad * 0.0, jnp.zeros((rows, count), F32), ones, none,
        ],
        axis=1,
    ).astype(BF16)


def split_three(values, rounded=lambda part: part.astype(BF16).astype(F32)):
    first = rounded(values)
    second = rounded(values - first)
    return first, second, rounded(values - first - second)


def to_bf16_grid(values):
    return lax.reduce_precision(values, exponent_bits=8, mantissa_bits=7)


def forward_kernel(x_ref, w_ref, b_ref, f_ref, qkv_ref, ctx_ref, keys, vals_t, *, keep):
    rows = x_ref.shape[0]
    proj = dot(x_ref[...], w_ref[0])
    proj = (proj + b_ref[0]).astype(BF16) + f_ref[...]
    queries = proj[:, :LANES]
    qkv_ref[...] = proj
    keys[...] = proj[:, LANES : 2 * LANES]
    vals_t[...] = proj[:, 2 * LANES :].T
    scores = []
    for start in range(0, rows, Q_BLOCK):
        scores.append(dot_cols(keys[...], queries[start : start + Q_BLOCK]))
    for index, block in enumerate(scores):
        part = slice(index * Q_BLOCK, (index + 1) * Q_BLOCK)
        peak = jnp.max(block, axis=0, keepdims=True)
        raised = jnp.exp(block - peak)
        total = jnp.sum(raised, axis=0, keepdims=True)
        weights = (raised * (1.0 / total)).astype(BF16)
        context = dot(vals_t[...], weights)
        ctx_ref[0, part, :] = context[:HEAD_DIM].T
        if keep:
            first, second, third = split_three(-(peak + jnp.log(total)))
            lane = lax.broadcasted_iota(jnp.int32, (LANES, Q_BLOCK), 0)
            spread = jnp.where(lane == ROW_TERM, first, 0.0)
            spread = jnp.where(lane == ROW_TERM + 1, second, spread)
            spread = jnp.where(lane == ROW_TERM + 2, third, spread)
            qkv_ref[part, :LANES] = queries[part] + spread.T.astype(BF16)


def attend_forward(source, weight, bias, features, keep):
    rows, width = source.shape
    heads = weight.shape[0]
    cols = 3 * LANES
    return pl.pallas_call(
        functools.partial(forward_kernel, keep=keep),
        grid=(heads,),
        in_specs=[
            pl.BlockSpec((rows, width), lambda h: (0, 0)),
            pl.BlockSpec((1, width, cols), lambda h: (h, 0, 0)),
            pl.BlockSpec((1, 1, cols), lambda h: (h, 0, 0)),
            pl.BlockSpec((rows, cols), lambda h: (0, 0)),
        ],
        out_specs=[
            pl.BlockSpec((rows, cols), lambda h: (0, h)),
            pl.BlockSpec((1, rows, HEAD_DIM), lambda h: (h, 0, 0)),
        ],
        out_shape=[
            jax.ShapeDtypeStruct((rows, heads * cols), BF16),
            jax.ShapeDtypeStruct((heads, rows, HEAD_DIM), F32),
        ],
        scratch_shapes=[pltpu.VMEM((rows, LANES), BF16), pltpu.VMEM((LANES, rows), BF16)],
        compiler_params=pltpu.CompilerParams(vmem_limit_bytes=56 * 2**20),
        cost_estimate=pl.CostEstimate(
            flops=16 * heads * rows * rows * HEAD_DIM,
            bytes_accessed=2 * rows * (width + 2 * heads * cols),
            transcendentals=heads * rows * rows,
        ),
        name="attend_forward",
    )(source, weight, bias, features)


def backward_kernel(qkv_ref, g_ref, dq_ref, dk_ref, dv_ref, keys_t, *, key_block):
    rows = g_ref.shape[0]
    queries = qkv_ref[:, :LANES]
    grads = g_ref[...]
    keys_t[...] = qkv_ref[:, LANES : 2 * LANES].T
    total = None
    for start in range(0, rows, key_block):
        part = slice(start, start + key_block)
        weights = jnp.exp(dot_cols(qkv_ref[part, LANES : 2 * LANES], queries))
        grad_weights = dot_cols(qkv_ref[part, 2 * LANES :], grads)
        grad_scores = (weights * grad_weights).astype(BF16)
        step = dot(keys_t[:, part], grad_scores)
        total = step if total is None else total + step
        dk_ref[0, part, :] = dot(grad_scores, queries)[:, :HEAD_DIM]
        dv_ref[0, part, :] = dot(weights.astype(BF16), grads)[:, :HEAD_DIM]
    dq_ref[0] = total[:HEAD_DIM].T * 0.125


def attend_backward(qkv, grads):
    rows = qkv.shape[0]
    cols = 3 * LANES
    heads = qkv.shape[1] // cols
    one_head = jax.ShapeDtypeStruct((heads, rows, HEAD_DIM), F32)
    head_spec = pl.BlockSpec((1, rows, HEAD_DIM), lambda h: (h, 0, 0))
    return pl.pallas_call(
        functools.partial(backward_kernel, key_block=256),
        grid=(heads,),
        in_specs=[
            pl.BlockSpec((rows, cols), lambda h: (0, h)),
            pl.BlockSpec((rows, LANES), lambda h: (0, h)),
        ],
        out_specs=[head_spec] * 3,
        out_shape=[one_head] * 3,
        scratch_shapes=[pltpu.VMEM((LANES, rows), BF16)],
        compiler_params=pltpu.CompilerParams(vmem_limit_bytes=56 * 2**20),
        cost_estimate=pl.CostEstimate(
            flops=40 * heads * rows * rows * HEAD_DIM,
            bytes_accessed=2 * rows * heads * (cols + 7 * LANES),
            transcendentals=heads * rows * rows,
        ),
        name="attend_backward",
    )(qkv, grads)


def padded_heads(weight, bias):
    width, _, cols = weight.shape
    heads = cols // HEAD_DIM
    scale = jnp.array([0.125, 1.0, 1.0], F32)
    weight = weight.reshape(width, 3, heads, HEAD_DIM).transpose(2, 0, 1, 3)
    weight = weight * scale[None, None, :, None].astype(weight.dtype)
    weight = jnp.pad(weight, ((0, 0), (0, 0), (0, 0), (0, LANES - HEAD_DIM)))
    full = jnp.stack([bias[0] * 0.125, jnp.zeros_like(bias[0]), bias[1]]).astype(F32)
    full = full.reshape(3, heads, HEAD_DIM).transpose(1, 0, 2)
    full = jnp.pad(full, ((0, 0), (0, 0), (0, LANES - HEAD_DIM)))
    return (
        weight.reshape(heads, width, 3 * LANES).astype(BF16),
        full.reshape(heads, 1, 3 * LANES),
    )


def join_heads(parts):
    heads, rows, width = parts.shape
    return parts.transpose(1, 0, 2).reshape(rows, heads * width)


def reduce_dp(array):
    share = lax.psum_scatter(array.astype(BF16), "dp", scatter_dimension=0, tiled=True)
    return lax.all_gather(share, "dp", axis=0, tiled=True).astype(F32)


def body(
    tokens,
    seg_lengths,
    parents,
    qkv_latent,
    qv_bias,
    out_latent,
    out_bias,
    norm1_gain,
    norm1_shift,
    up_latent,
    up_bias,
    down_latent,
    down_bias,
    norm2_gain,
    norm2_shift,
    teacher_qkv,
    teacher_qv_bias,
    teacher_out,
    teacher_out_bias,
    teacher_norm1_gain,
    teacher_norm1_shift,
    teacher_up,
    teacher_up_bias,
    teacher_down,
    teacher_down_bias,
    teacher_norm2_gain,
    teacher_norm2_shift,
):
    own_rows, model_width = tokens.shape
    group = lax.axis_size("tensor")
    me = lax.axis_index("tensor")
    all_rows = own_rows * group
    local_cols = qkv_latent.shape[2]
    local_heads = local_cols // HEAD_DIM
    hidden_all = up_latent.shape[1] * group
    x_all = jnp.concatenate(gather_blocks(tokens))
    sums = sum_small(
        jnp.stack([jnp.sum(jnp.abs(out_latent), axis=0), jnp.sum(jnp.abs(down_latent), axis=0)])
    )
    w_qkv = (jnp.mean(jnp.abs(qkv_latent), axis=0) * jnp.sign(qkv_latent)).astype(BF16)
    w_out = (sums[0] / model_width * jnp.sign(out_latent)).astype(BF16)
    w_up = (jnp.mean(jnp.abs(up_latent), axis=0) * jnp.sign(up_latent)).astype(BF16)
    w_down = (sums[1] / hidden_all * jnp.sign(down_latent)).astype(BF16)
    block_rows = jnp.arange(own_rows, dtype=jnp.int32)
    positions = jnp.concatenate([(me ^ j) * own_rows + block_rows for j in range(group)])
    features = segment_features(seg_lengths[0], parents[0], positions)
    x_own = tokens.astype(F32)
    x_in_all = clip_act(x_all.astype(F32)).astype(BF16)

    qkv, context = attend_forward(
        x_in_all, *padded_heads(w_qkv, qv_bias), features, True
    )
    _, t_context = attend_forward(
        x_all, *padded_heads(teacher_qkv, teacher_qv_bias), features, False
    )
    context = join_heads(context)
    attn_in = clip_act(context).astype(BF16)
    t_attn_in = join_heads(t_context).astype(BF16)

    def own_rows_all_heads(array):
        return jnp.concatenate(exchange_blocks(list(array.reshape(group, own_rows, -1))), axis=1)

    w_out_all = jnp.concatenate(gather_blocks(w_out))
    t_weights = jnp.concatenate(
        [teacher_up, teacher_down, teacher_out, jnp.tile(teacher_up_bias[None], (16, 1))]
    )
    t_blocks = gather_blocks(t_weights)
    hid = teacher_up.shape[1]
    t_up = [block[:model_width] for block in t_blocks]
    t_down = [block[model_width : model_width + hid] for block in t_blocks]
    t_out_all = jnp.concatenate(
        [block[model_width + hid : model_width + hid + local_cols] for block in t_blocks]
    )
    t_up_bias = [block[-1].astype(F32) for block in t_blocks]

    attn_in_own = own_rows_all_heads(attn_in)
    attn_own = dot(attn_in_own, w_out_all)
    gain_one = norm1_gain.astype(F32)
    gain_two = norm2_gain.astype(F32)
    y_one, normed_one, inv_one = norm_forward(
        x_own + attn_own + out_bias.astype(F32), gain_one, norm1_shift.astype(F32)
    )
    y_one_in = clip_act(y_one).astype(BF16)
    y_one_all = jnp.concatenate(gather_blocks(y_one_in))

    t_attn_own = dot(own_rows_all_heads(t_attn_in), t_out_all)
    t_y_one, _, _ = norm_forward(
        x_own + t_attn_own + teacher_out_bias.astype(F32),
        teacher_norm1_gain.astype(F32),
        teacher_norm1_shift.astype(F32),
    )
    t_y_one_in = t_y_one.astype(BF16)
    t_ffn_own = teacher_down_bias.astype(F32)
    for up, down, bias in zip(t_up, t_down, t_up_bias):
        t_hidden = jax.nn.gelu(dot(t_y_one_in, up) + bias, approximate=False).astype(BF16)
        t_ffn_own = t_ffn_own + dot(t_hidden, down)
    t_out_own, _, _ = norm_forward(
        t_y_one + t_ffn_own,
        teacher_norm2_gain.astype(F32),
        teacher_norm2_shift.astype(F32),
    )

    upward = dot(y_one_all, w_up) + up_bias.astype(F32)
    gelu_vals = jax.nn.gelu(upward, approximate=False)
    gelu_in = clip_act(gelu_vals).astype(BF16)
    ffn_part = dot(gelu_in, w_down)
    ffn_own = reduce_blocks(list(ffn_part.reshape(group, own_rows, -1)))
    out_own, normed_two, inv_two = norm_forward(
        y_one + ffn_own + down_bias.astype(F32), gain_two, norm2_shift.astype(F32)
    )
    mismatch = out_own - t_out_own
    loss_part = jnp.sum(mismatch * mismatch)
    grad_two, gain_two_grad, shift_two_grad = norm_backward(mismatch, normed_two, inv_two, gain_two)
    grad_ffn = grad_two.astype(BF16)
    down_bias_grad = jnp.sum(grad_ffn.astype(F32), axis=0)
    grad_ffn_all = jnp.concatenate(gather_blocks(grad_ffn))
    down_grad = dot_rows(gelu_in, grad_ffn_all)
    grad_gelu = dot_cols(grad_ffn_all, w_down)
    grad_up = (grad_gelu * clip_slope(gelu_vals) * gelu_slope(upward)).astype(BF16)
    up_bias_grad = jnp.sum(grad_up.astype(F32), axis=0)
    up_grad = dot_rows(y_one_all, grad_up)
    ffn_grads = reduce_dp(jnp.concatenate([up_grad, down_grad]))
    grad_y_in = reduce_blocks(list(dot_cols(grad_up, w_up).reshape(group, own_rows, -1)))
    grad_y_one = grad_two + grad_y_in * clip_slope(y_one)
    grad_h, gain_one_grad, shift_one_grad = norm_backward(grad_y_one, normed_one, inv_one, gain_one)
    grad_attn = grad_h.astype(BF16)
    out_bias_grad = jnp.sum(grad_attn.astype(F32), axis=0)
    out_grad = reduce_blocks(
        list(dot_rows(attn_in_own, grad_attn).reshape(group, local_cols, -1))
    )
    level = attn_in_own.astype(F32) / CLIP_RANGE
    grad_context = (dot_cols(grad_attn, w_out_all) * (1.0 - level * level)).astype(BF16)
    grad_context = jnp.concatenate(
        exchange_blocks([grad_context[:, j * local_cols : (j + 1) * local_cols] for j in range(group)])
    )
    grad_heads = grad_context.reshape(all_rows, local_heads, HEAD_DIM)
    inner = -jnp.sum(
        grad_heads.astype(F32) * context.reshape(all_rows, local_heads, HEAD_DIM),
        axis=-1,
        keepdims=True,
    )
    grad_wide = jnp.concatenate(
        [
            grad_heads,
            jnp.zeros((all_rows, local_heads, ROW_TERM - HEAD_DIM), BF16),
            *(part.astype(BF16) for part in split_three(inner, to_bf16_grid)),
            jnp.zeros((all_rows, local_heads, LANES - ROW_TERM - 3), BF16),
        ],
        axis=-1,
    ).reshape(all_rows, local_heads * LANES)
    grad_queries, grad_keys, grad_values = attend_backward(qkv, grad_wide)
    grad_proj = jnp.concatenate(
        [join_heads(grad_queries), join_heads(grad_keys), join_heads(grad_values)], axis=1
    ).astype(BF16)
    proj_bias_grad = jnp.sum(grad_proj.astype(F32), axis=0)
    qkv_grad = dot_rows(x_in_all, grad_proj)
    grad_x_in = reduce_blocks(
        list(
            dot_cols(grad_proj, w_qkv.reshape(model_width, -1)).reshape(group, own_rows, -1)
        )
    )
    input_grad = grad_h + grad_x_in * clip_slope(x_own)

    shared = jnp.stack(
        [
            out_bias_grad,
            gain_one_grad,
            shift_one_grad,
            down_bias_grad,
            gain_two_grad,
            shift_two_grad,
            jnp.full((model_width,), loss_part),
        ]
    )
    shared = sum_small(shared)
    tree_loss = shared[6, :1] / (all_rows * model_width)
    small = jnp.concatenate(
        [shared[:6].reshape(-1), up_bias_grad, proj_bias_grad]
    )
    small = lax.psum(small, "dp")
    shared, up_bias_grad, proj_bias_grad = (
        small[: 6 * model_width].reshape(6, model_width),
        small[6 * model_width : 6 * model_width + hid],
        small[6 * model_width + hid :].reshape(3, local_cols),
    )
    late = reduce_dp(
        jnp.concatenate([qkv_grad.reshape(-1, model_width), out_grad.astype(F32)])
    )
    qkv_rows = 3 * local_cols
    return (
        out_own.astype(BF16),
        tree_loss,
        input_grad,
        late[:qkv_rows].reshape(model_width, 3, local_cols),
        jnp.stack([proj_bias_grad[0], proj_bias_grad[2]]),
        late[qkv_rows:],
        shared[0],
        shared[1],
        shared[2],
        ffn_grads[:model_width],
        up_bias_grad,
        ffn_grads[model_width:],
        shared[3],
        shared[4],
        shared[5],
    )


def solution(mesh):
    rows, cols = ("dp", "tensor"), "tensor"
    vec = P()
    params = (
        P(None, None, cols),
        P(None, cols),
        P(cols, None),
        vec,
        vec,
        vec,
        P(None, cols),
        P(cols),
        P(cols, None),
        vec,
        vec,
        vec,
    )
    in_specs = (P(rows, None), P("dp", None), P("dp", None)) + params + params
    out_specs = (P(rows, None), P("dp"), P(rows, None)) + params
    return jax.shard_map(body, mesh=mesh, in_specs=in_specs, out_specs=out_specs, check_vma=False)
```

time: 1060 us -> 759 us (0.72)
  matrix products: 323 us -> 112 us
  waiting for transfers between devices: 443 us -> 299 us
  Pallas kernels: 0 us -> 88.3 us
  other arithmetic: 146 us -> 82.1 us
  local copies, waits for them, and re-layouts: 64.7 us -> 93.3 us
  blocking collectives: 61.4 us -> 35.1 us
  starting transfers between devices: 0.53 us -> 24.4 us
    psum x1 -> x0, waiting for transfers between devices: 198 us -> none  [body(): lax.psum((qkv_grad, qv_bias_grad, out_grad, up_grad, up_bias_grad, down_g...]
    dot_general x44 -> x17, matrix products: 271 us -> 112 us  [the longest x9 65.1 us: dot(): return jnp.dot(left, right, preferred_element_type=F32)]
    ppermute x0 -> x33, waiting for transfers between devices: none -> 154 us  [swap(): return lax.ppermute(array, 'tensor', [(i, i ^ bit) for i in range(size)])]
    all_gather x6 -> x2, waiting for transfers between devices: 118 us -> 21.2 us  [reduce_dp(): return lax.all_gather(share, 'dp', axis=0, tiled=True).astype(F32)]
    pallas_call x0 -> x3, Pallas kernels: none -> 88.3 us  [the longest x2 54.4 us: attend_forward(): pl.pallas_call(functools.partial(forward_kernel, keep=keep), grid=(heads,...]
    sub x4 -> x0, matrix products: 40.2 us -> none  [one_block(): raised = jnp.exp(scores - peak)]
    or x12 -> x0, other arithmetic: 32.7 us -> none  [path_mask(): return allowed | (col_two[None, :] == row_seg[:, None])]
    reduce_sum x9 -> x7, other arithmetic: 34.7 us -> 7.32 us  [the longest x1 2.87 us: body(): loss_part = jnp.sum(mismatch * mismatch)]
  transfers between devices with their start and end apart: 13 -> 37, of which waited for: 11 -> 13; matrix products, arithmetic and copies ran while one was open for 21% -> 32% of each run, Pallas kernels for 0% -> 12%
where the time goes in v1:
time: 759 us; the launch traced here: 751 us
  waiting for transfers between devices  299 us (39%)
  matrix products  112 us (15%)
  local copies, waits for them, and re-layouts  93.3 us (12%)
  Pallas kernels  88.3 us (12%)
  other arithmetic  82.1 us (11%)
  blocking collectives  35.1 us (5%)
  starting transfers between devices  24.4 us (3%)
  between operations  17.3 us (2%)
    ppermute x33, waiting for transfers between devices, swap(): return lax.ppermute(array, 'tensor', [(i, i ^ bit) for i in range(size)])  154 us
    reduce_scatter x2, waiting for transfers between devices, reduce_dp(): lax.psum_scatter(array.astype(BF16), 'dp', scatter_dimension=0, tiled=True)  123 us
    dot_general x9, matrix products, dot(): return jnp.dot(left, right, preferred_element_type=F32)  65.1 us
    pallas_call x2, Pallas kernels, attend_forward(): pl.pallas_call(functools.partial(forward_kernel, keep=keep), grid=(heads,...  54.4 us
    psum x1, blocking collectives, body(): small = lax.psum(small, 'dp')  35.1 us
    pallas_call x1, Pallas kernels, attend_backward(): pl.pallas_call(functools.partial(backward_kernel, key_block=256), grid=(h...  33.9 us
    dot_general x4, matrix products, dot_cols(): return lax.dot_general(left, right, COLS_COLS, preferred_element_type=F32)  27.5 us
    ppermute x33, starting transfers between devices, swap(): return lax.ppermute(array, 'tensor', [(i, i ^ bit) for i in range(size)])  24 us
  transfers between devices with their start and end apart: 37, of which 13 were waited for; matrix products, arithmetic and copies ran while one was open for 32% of the time, Pallas kernels for 12%

profile of v1, /device:TPU:0, one launch (start us, length us, event | category | flops | bytes accessed | tf_op | source)
XLA Modules:
  0.0 751.3 jit_solution(802392822770425059)
XLA Ops:
  22.0 63.6 %collective-permute-done.6 = f32[2,768]{1,0:T(2,128)S(1)} collective-permute-done((f32[2,768]{1,0:T(2,128)S(1)}, f32[2,768]{1,0:T(2,128)S(1)}, u32[]{:S(2)}, u32[]{:S(2)}) %collective-permute-start.6) | collective-permute-done | bytes 6176 | tf_op jit(solution)/shard_map/ppermute | solution.py:68
  97.4 9.0 %concatenate.65.f_ref = bf16[2048,384]{1,0:T(8,128)(2,1)} concatenate(bf16[2048,64]{1,0:T(8,128)(2,1)S(1)} %broadcast_in_dim.32, bf16[2048,13]{1,0:T(8,128)(2,1)S(1)} %copy-done.20, bf16[2048,3]{1,0:T(8,128)(2,1)S(1)} %broadcast.328, bf16[2048,48]{1,0:T(8,128)(2,1)} %broadcast_in_dim.36, bf16[2048,64]{1,0:T(8,128)(2,1)S(1)} %broadcast_in_dim.32, bf16[2048,13]{1,0:T(8,128)(2,1)S(1)} %copy.167, ...), dimensions={1} | concatenate | bytes 3145728 | tf_op jit(solution)/shard_map/concatenate | solution.py:120
  114.3 27.5 %attend_forward.2 = (bf16[2048,1152]{1,0:T(8,128)(2,1)}, f32[3,2048,64]{2,1,0:T(8,128)}) custom-call(bf16[2048,768]{1,0:T(8,128)(2,1)} %multiply_convert_fusion.1.x_ref, bf16[3,768,384]{2,1,0:T(8,128)(2,1)} %copy.168.w_ref, f32[3,1,384]{2,1,0:T(1,128)} %reshape.352.b_ref, bf16[2048,384]{1,0:T(8,128)(2,1)} %concatenate.65.f_ref), custom_call_target="tpu_custom_call" | custom-call | flops 12884901888 | bytes 12582912 | tf_op jit(solution)/shard_map/attend_forward/pallas_call | solution.py:172
  146.8 26.9 %attend_forward.3 = (bf16[2048,1152]{1,0:T(8,128)(2,1)}, f32[3,2048,64]{2,1,0:T(8,128)}) custom-call(bf16[2048,768]{1,0:T(8,128)(2,1)} %copy-done.7, bf16[3,768,384]{2,1,0:T(8,128)(2,1)} %copy.180.w_ref, f32[3,1,384]{2,1,0:T(1,128)} %reshape.354.b_ref, bf16[2048,384]{1,0:T(8,128)(2,1)} %concatenate.65.f_ref), custom_call_target="tpu_custom_call" | custom-call | flops 12884901888 | bytes 12582912 | tf_op jit(solution)/shard_map/attend_forward/pallas_call | solution.py:172
  191.8 25.7 %collective-permute-done.15 = bf16[2,512,192]{1,2,0:T(8,128)(2,1)} collective-permute-done((bf16[2,512,192]{1,2,0:T(8,128)(2,1)}, bf16[2,512,192]{1,2,0:T(8,128)(2,1)}, u32[]{:S(2)}, u32[]{:S(2)}) %collective-permute-start.15) | collective-permute-done | bytes 393248 | tf_op jit(solution)/shard_map/ppermute | solution.py:68
  234.6 23.8 %fusion.3 = (f32[2048,768]{1,0:T(8,128)S(1)}, f32[2048,768]{1,0:T(8,128)}) fusion(f32[768]{0:T(1024)S(1)} %copy-done.47, f32[768,768]{1,0:T(8,128)} %param.38, f32[768]{0:T(1024)S(1)} %copy-done.56, bf16[512,768]{1,0:T(8,128)(2,1)} %collective-permute-done.12, bf16[512,768]{1,0:T(8,128)(2,1)} %collective-permute-done.11, ...), kind=kOutput, calls=%fused_computation.5 | convolution fusion | flops 2534080512 | bytes 18094080 | tf_op jit(solution)/shard_map/dot_general | solution.py:55
  258.4 5.0 fusion.417
  267.9 8.1 %fusion.90 = f32[512,768]{1,0:T(8,128)} fusion(bf16[1744,768]{1,0:T(8,128)(2,1)} %collective-permute-done.17, f32[768]{0:T(1024)S(1)} %copy-done.46, f32[512,768]{1,0:T(8,128)} %copy-done.21, f32[768]{0:T(1024)S(1)} %copy-done.50, f32[768]{0:T(1024)S(1)} %copy-done.49, f32[512]{0:T(512)S(1)} %add_rsqrt_fusion.1, f32[512]{0:T(512)S(1)} %broadcast_multiply_fusion.7), kind=kOutput, calls=%fused_computation.201 | convolution fusion | flops 1235877888 | bytes 5518336 | tf_op jit(solution)/shard_map/dot_general | solution.py:55
  275.9 7.5 fusion.91
  284.2 8.0 %fusion.89 = f32[512,768]{1,0:T(8,128)} fusion(bf16[1744,768]{1,0:T(8,128)(2,1)} %collective-permute-done.18, f32[768]{0:T(1024)S(1)} %copy-done.45, f32[512,768]{1,0:T(8,128)S(1)} %copy-done.22, f32[768]{0:T(1024)S(1)} %copy-done.50, f32[768]{0:T(1024)S(1)} %copy-done.49, f32[512]{0:T(512)S(1)} %add_rsqrt_fusion.1, f32[512]{0:T(512)S(1)} %broadcast_multiply_fusion.7), kind=kOutput, calls=%fused_computation.200 | convolution fusion | flops 1235877888 | bytes 5518336 | tf_op jit(solution)/shard_map/dot_general | solution.py:55
  293.8 3.6 fusion.53
  299.1 9.0 %fusion.419 = (f32[512]{0:T(512)S(1)}, f32[512,768]{1,0:T(8,128)S(1)}) fusion(bf16[1744,768]{1,0:T(8,128)(2,1)} %copy-done.37, f32[768]{0:T(1024)S(1)} %fusion.257, f32[512,768]{1,0:T(8,128)} %copy-done.21, f32[768]{0:T(1024)S(1)} %copy-done.50, f32[768]{0:T(1024)S(1)} %copy-done.49, f32[512]{0:T(512)S(1)} %add_rsqrt_fusion.1, ...), kind=kOutput, calls=%fused_computation.605 | convolution fusion | flops 1239809536 | bytes 11831296 | tf_op jit(solution)/shard_map/dot_general | solution.py:55
  308.5 9.2 %collective-permute-done.14 = bf16[512,768]{1,0:T(8,128)(2,1)} collective-permute-done((bf16[512,768]{1,0:T(8,128)(2,1)}, bf16[512,768]{1,0:T(8,128)(2,1)}, u32[]{:S(2)}, u32[]{:S(2)}) %collective-permute-start.14) | collective-permute-done | bytes 786464 | tf_op jit(solution)/shard_map/ppermute | solution.py:68
  326.6 17.4 %collective-permute-done.21 = bf16[512,768]{1,0:T(8,128)(2,1)S(1)} collective-permute-done((bf16[512,768]{1,0:T(8,128)(2,1)S(1)}, bf16[512,768]{1,0:T(8,128)(2,1)S(1)}, u32[]{:S(2)}, u32[]{:S(2)}) %collective-permute-start.21) | collective-permute-done | bytes 786464 | tf_op jit(solution)/shard_map/ppermute | solution.py:68
  346.4 14.0 %convert_reduce_fusion = (f32[768]{0:T(1024)S(1)}, bf16[2048,768]{1,0:T(8,128)(2,1)}) fusion(f32[2048,768]{1,0:T(8,128)} %get-tuple-element.169, f32[768]{0:T(1024)S(1)} %copy-done.48, f32[2048,768]{1,0:T(8,128)S(1)} %bitcast.159, f32[768,768]{1,0:T(8,128)S(1)} %copy-done.5, f32[768]{0:T(1024)S(1)} %copy-done.39, ...), kind=kOutput, calls=%fused_computation.12 | convolution fusion | flops 2455436544 | bytes 21242880 | tf_op jit(solution)/shard_map/dot_general | solution.py:63
  360.5 4.7 fusion.424
  371.2 17.8 %collective-permute-done.24 = bf16[512,768]{1,0:T(8,128)(2,1)S(1)} collective-permute-done((bf16[512,768]{1,0:T(8,128)(2,1)S(1)}, bf16[512,768]{1,0:T(8,128)(2,1)S(1)}, u32[]{:S(2)}, u32[]{:S(2)}) %collective-permute-start.24) | collective-permute-done | bytes 786464 | tf_op jit(solution)/shard_map/ppermute | solution.py:68
  399.5 10.5 %collective-permute-done.27 = bf16[2,512,192]{2,1,0:T(8,128)(2,1)S(1)} collective-permute-done((bf16[2,512,192]{2,1,0:T(8,128)(2,1)S(1)}, bf16[2,512,192]{2,1,0:T(8,128)(2,1)S(1)}, u32[]{:S(2)}, u32[]{:S(2)}) %collective-permute-start.27) | collective-permute-done | bytes 393248 | tf_op jit(solution)/shard_map/ppermute | solution.py:68
  428.4 4.6 fusion.18
  435.8 9.7 %concatenate.78 = bf16[2048,3,128]{2,0,1:T(8,128)(2,1)} concatenate(bf16[2048,3,64]{2,0,1:T(8,128)(2,1)} %pad_maximum_fusion.7, bf16[2048,3,16]{2,0,1:T(8,128)(2,1)} %broadcast_in_dim.40, bf16[2048,3,1]{2,0,1:T(8,128)(2,1)} %copy.196, bf16[2048,3,1]{2,0,1:T(8,128)(2,1)} %get-tuple-element.117, bf16[2048,3,1]{2,0,1:T(8,128)(2,1)S(1)} %get-tuple-element.116, ...), dimensions={2} | concatenate | bytes 3145728 | tf_op jit(solution)/shard_map/concatenate | solution.py:412
  448.8 33.9 %attend_backward.1 = (f32[3,2048,64]{2,1,0:T(8,128)}, f32[3,2048,64]{2,1,0:T(8,128)}, f32[3,2048,64]{2,1,0:T(8,128)}) custom-call(bf16[2048,1152]{1,0:T(8,128)(2,1)} %get-tuple-element.23.qkv_ref, bf16[2048,384]{1,0:T(8,128)(2,1)} %copy.198.g_ref), custom_call_target="tpu_custom_call" | custom-call | flops 32212254720 | bytes 15728640 | tf_op jit(solution)/shard_map/attend_backward/pallas_call | solution.py:224
  493.7 5.6 convolution_convert_fusion.3
  507.4 5.7 convolution_convert_fusion.2
  513.1 5.6 convolution_convert_fusion.1
  520.4 51.4 %reduce-scatter.3.cloned.1.call-done = bf16[96,768]{1,0:T(8,128)(2,1)} async-done(((bf16[768,768]{1,0:T(8,128)(2,1)}), bf16[96,768]{1,0:T(8,128)(2,1)}) %reduce-scatter.3.cloned.1.call-update) | async-done | bytes 147472 | tf_op jit(solution)/shard_map/reduce_scatter | solution.py:266
  572.0 71.8 %reduce-scatter.5.cloned.1.call-done = bf16[192,768]{1,0:T(8,128)(2,1)} async-done(((bf16[1536,768]{1,0:T(8,128)(2,1)}), bf16[192,768]{1,0:T(8,128)(2,1)}) %reduce-scatter.5.cloned.1.call-update) | async-done | bytes 294928 | tf_op jit(solution)/shard_map/reduce_scatter | solution.py:266
  643.8 6.7 fusion.425
  662.1 3.6 fusion.43
  667.6 35.1 %psum.7 = f32[5952]{0:T(1024)S(1)} all-reduce(f32[5952]{0:T(1024)S(1)} %pad_maximum_fusion.25), channel_id=1, replica_groups=mesh['dp'=8,'tensor'=4] {'dp'}, use_global_device_ids=true, to_apply=%region_30.31 | all-reduce | flops 5952 | bytes 47616 | tf_op jit(solution)/shard_map/psum | solution.py:450
  703.9 4.0 fusion.29
  718.0 21.2 %all-gather.5.cloned.1.call-done = bf16[1536,768]{1,0:T(8,128)(2,1)} async-done(((bf16[192,768]{1,0:T(8,128)(2,1)}), bf16[1536,768]{1,0:T(8,128)(2,1)}) %all-gather.5.cloned.1.call-update) | async-done | bytes 2359312 | tf_op jit(solution)/shard_map/all_gather | solution.py:267
  739.3 4.2 fusion.408
  (430 shorter events, 179.7 us)
Async XLA Ops:
  7.2 564.6 %reduce-scatter.3.cloned.1.call-start = ((), (), s32[]{:S(2)}) async-start(), calls=%async_computation.2 | async-start | bytes 1327104 | tf_op jit(solution)/shard_map/reduce_scatter | solution.py:266
  7.2 79.0 %collective-permute-start.1 = (bf16[512,768]{1,0:T(8,128)(2,1)}, bf16[512,768]{1,0:T(8,128)(2,1)}, u32[]{:S(2)}, u32[]{:S(2)}) collective-permute-start(bf16[512,768]{1,0:T(8,128)(2,1)} %param.29), channel_id=1, source_target_pairs={{0,2},{1,3},{2,0},{3,1},{4,6},{5,7},{6,4},{7,5},{8,10},{9,11},{10,... | collective-permute-start | bytes 2359304 | tf_op jit(solution)/shard_map/ppermute | solution.py:68
  10.3 97.6 %collective-permute-start = (bf16[512,768]{1,0:T(8,128)(2,1)}, bf16[512,768]{1,0:T(8,128)(2,1)}, u32[]{:S(2)}, u32[]{:S(2)}) collective-permute-start(bf16[512,768]{1,0:T(8,128)(2,1)} %param.29), channel_id=1, source_target_pairs={{0,1},{1,0},{2,3},{3,2},{4,5},{5,4},{6,7},{7,6},{8,9},{9,8},{10,11... | collective-permute-start | bytes 2359304 | tf_op jit(solution)/shard_map/ppermute | solution.py:68
  14.2 215.1 %collective-permute-start.18 = (bf16[1744,768]{1,0:T(8,128)(2,1)}, bf16[1744,768]{1,0:T(8,128)(2,1)}, u32[]{:S(2)}, u32[]{:S(2)}) collective-permute-start(bf16[1744,768]{1,0:T(8,128)(2,1)} %pad_maximum_fusion.2), channel_id=1, source_target_pairs={{0,2},{1,3},{2,0},{3,1},{4,6},{5,7},{6,4},{7,5},{8,10},{9,11},{10,... | collective-permute-start | bytes 8036360 | tf_op jit(solution)/shard_map/ppermute | solution.py:68
  14.3 216.6 %collective-permute-start.17 = (bf16[1744,768]{1,0:T(8,128)(2,1)}, bf16[1744,768]{1,0:T(8,128)(2,1)}, u32[]{:S(2)}, u32[]{:S(2)}) collective-permute-start(bf16[1744,768]{1,0:T(8,128)(2,1)} %pad_maximum_fusion.2), channel_id=1, source_target_pairs={{0,1},{1,0},{2,3},{3,2},{4,5},{5,4},{6,7},{7,6},{8,9},{9,8},{10,11... | collective-permute-start | bytes 8036360 | tf_op jit(solution)/shard_map/ppermute | solution.py:68
  15.2 4.7 collective-permute-start.5
  19.9 65.6 %collective-permute-start.6 = (f32[2,768]{1,0:T(2,128)S(1)}, f32[2,768]{1,0:T(2,128)S(1)}, u32[]{:S(2)}, u32[]{:S(2)}) collective-permute-start(f32[2,768]{1,0:T(2,128)S(1)} %fusion.394), channel_id=1, source_target_pairs={{0,2},{1,3},{2,0},{3,1},{4,6},{5,7},{6,4},{7,5},{8,10},{9,11},{10,... | collective-permute-start | bytes 18440 | tf_op jit(solution)/shard_map/ppermute | solution.py:68
  86.2 24.3 %collective-permute-start.2 = (bf16[512,768]{1,0:T(8,128)(2,1)}, bf16[512,768]{1,0:T(8,128)(2,1)}, u32[]{:S(2)}, u32[]{:S(2)}) collective-permute-start(bf16[512,768]{1,0:T(8,128)(2,1)} %collective-permute-done.1), channel_id=1, source_target_pairs={{0,1},{1,0},{2,3},{3,2},{4,5},{5,4},{6,7},{7,6},{8,9},{9,8},{10,11... | collective-permute-start | bytes 2359304 | tf_op jit(solution)/shard_map/ppermute | solution.py:68
  87.1 20.4 %collective-permute-start.8 = (bf16[192,768]{1,0:T(8,128)(2,1)}, bf16[192,768]{1,0:T(8,128)(2,1)}, u32[]{:S(2)}, u32[]{:S(2)}) collective-permute-start(bf16[192,768]{1,0:T(8,128)(2,1)} %multiply_convert_fusion.9), channel_id=1, source_target_pairs={{0,2},{1,3},{2,0},{3,1},{4,6},{5,7},{6,4},{7,5},{8,10},{9,11},{10,... | collective-permute-start | bytes 884744 | tf_op jit(solution)/shard_map/ppermute | solution.py:68
  107.5 77.1 %collective-permute-start.7 = (bf16[192,768]{1,0:T(8,128)(2,1)}, bf16[192,768]{1,0:T(8,128)(2,1)}, u32[]{:S(2)}, u32[]{:S(2)}) collective-permute-start(bf16[192,768]{1,0:T(8,128)(2,1)} %multiply_convert_fusion.9), channel_id=1, source_target_pairs={{0,1},{1,0},{2,3},{3,2},{4,5},{5,4},{6,7},{7,6},{8,9},{9,8},{10,11... | collective-permute-start | bytes 884744 | tf_op jit(solution)/shard_map/ppermute | solution.py:68
  107.8 76.8 %collective-permute-start.9 = (bf16[192,768]{1,0:T(8,128)(2,1)}, bf16[192,768]{1,0:T(8,128)(2,1)}, u32[]{:S(2)}, u32[]{:S(2)}) collective-permute-start(bf16[192,768]{1,0:T(8,128)(2,1)} %collective-permute-done.8), channel_id=1, source_target_pairs={{0,1},{1,0},{2,3},{3,2},{4,5},{5,4},{6,7},{7,6},{8,9},{9,8},{10,11... | collective-permute-start | bytes 884744 | tf_op jit(solution)/shard_map/ppermute | solution.py:68
  146.5 31.0 %collective-permute-start.3 = (bf16[2,512,192]{2,1,0:T(8,128)(2,1)}, bf16[2,512,192]{2,1,0:T(8,128)(2,1)}, u32[]{:S(2)}, u32[]{:S(2)}) collective-permute-start(bf16[2,512,192]{2,1,0:T(8,128)(2,1)} %pad_maximum_fusion.17), channel_id=1, source_target_pairs={{0,2},{1,3},{2,0},{3,1},{4,6},{5,7},{6,4},{7,5},{8,10},{9,11},{10,... | collective-permute-start | bytes 1179656 | tf_op jit(solution)/shard_map/ppermute | solution.py:68
  188.8 31.2 %collective-permute-start.11 = (bf16[512,768]{1,0:T(8,128)(2,1)}, bf16[512,768]{1,0:T(8,128)(2,1)}, u32[]{:S(2)}, u32[]{:S(2)}) collective-permute-start(bf16[512,768]{1,0:T(8,128)(2,1)} %multiply_convert_fusion.6), channel_id=1, source_target_pairs={{0,2},{1,3},{2,0},{3,1},{4,6},{5,7},{6,4},{7,5},{8,10},{9,11},{10,... | collective-permute-start | bytes 2359304 | tf_op jit(solution)/shard_map/ppermute | solution.py:68
  191.4 26.2 %collective-permute-start.15 = (bf16[2,512,192]{1,2,0:T(8,128)(2,1)}, bf16[2,512,192]{1,2,0:T(8,128)(2,1)}, u32[]{:S(2)}, u32[]{:S(2)}) collective-permute-start(bf16[2,512,192]{1,2,0:T(8,128)(2,1)} %pad_maximum_fusion.21), channel_id=1, source_target_pairs={{0,2},{1,3},{2,0},{3,1},{4,6},{5,7},{6,4},{7,5},{8,10},{9,11},{10,... | collective-permute-start | bytes 1179656 | tf_op jit(solution)/shard_map/ppermute | solution.py:68
  219.5 9.8 %collective-permute-start.16 = (bf16[2,512,192]{1,2,0:T(8,128)(2,1)}, bf16[2,512,192]{1,2,0:T(8,128)(2,1)S(1)}, u32[]{:S(2)}, u32[]{:S(2)}) collective-permute-start(bf16[2,512,192]{1,2,0:T(8,128)(2,1)} %pad_maximum_fusion.22), channel_id=1, source_target_pairs={{0,1},{1,0},{2,3},{3,2},{4,5},{5,4},{6,7},{7,6},{8,9},{9,8},{10,11... | collective-permute-start | bytes 1179656 | tf_op jit(solution)/shard_map/ppermute | solution.py:68
  219.5 15.0 %collective-permute-start.10 = (bf16[512,768]{1,0:T(8,128)(2,1)}, bf16[512,768]{1,0:T(8,128)(2,1)}, u32[]{:S(2)}, u32[]{:S(2)}) collective-permute-start(bf16[512,768]{1,0:T(8,128)(2,1)} %multiply_convert_fusion.6), channel_id=1, source_target_pairs={{0,1},{1,0},{2,3},{3,2},{4,5},{5,4},{6,7},{7,6},{8,9},{9,8},{10,11... | collective-permute-start | bytes 2359304 | tf_op jit(solution)/shard_map/ppermute | solution.py:68
  220.0 14.5 %collective-permute-start.12 = (bf16[512,768]{1,0:T(8,128)(2,1)}, bf16[512,768]{1,0:T(8,128)(2,1)}, u32[]{:S(2)}, u32[]{:S(2)}) collective-permute-start(bf16[512,768]{1,0:T(8,128)(2,1)} %collective-permute-done.11), channel_id=1, source_target_pairs={{0,1},{1,0},{2,3},{3,2},{4,5},{5,4},{6,7},{7,6},{8,9},{9,8},{10,11... | collective-permute-start | bytes 2359304 | tf_op jit(solution)/shard_map/ppermute | solution.py:68
  229.4 35.4 %collective-permute-start.19 = (bf16[1744,768]{1,0:T(8,128)(2,1)}, bf16[1744,768]{1,0:T(8,128)(2,1)S(1)}, u32[]{:S(2)}, u32[]{:S(2)}) collective-permute-start(bf16[1744,768]{1,0:T(8,128)(2,1)} %collective-permute-done.18), channel_id=1, source_target_pairs={{0,1},{1,0},{2,3},{3,2},{4,5},{5,4},{6,7},{7,6},{8,9},{9,8},{10,11... | collective-permute-start | bytes 8036360 | tf_op jit(solution)/shard_map/ppermute | solution.py:68
  264.8 27.3 %collective-permute-start.13 = (bf16[2,512,768]{2,1,0:T(8,128)(2,1)}, bf16[2,512,768]{2,1,0:T(8,128)(2,1)}, u32[]{:S(2)}, u32[]{:S(2)}) collective-permute-start(bf16[2,512,768]{2,1,0:T(8,128)(2,1)} %pad_maximum_fusion.5), channel_id=1, source_target_pairs={{0,1},{1,0},{2,3},{3,2},{4,5},{5,4},{6,7},{7,6},{8,9},{9,8},{10,11... | collective-permute-start | bytes 4718600 | tf_op jit(solution)/shard_map/ppermute | solution.py:68
  297.4 20.3 %collective-permute-start.14 = (bf16[512,768]{1,0:T(8,128)(2,1)}, bf16[512,768]{1,0:T(8,128)(2,1)}, u32[]{:S(2)}, u32[]{:S(2)}) collective-permute-start(bf16[512,768]{1,0:T(8,128)(2,1)} %fusion.53), channel_id=1, source_target_pairs={{0,2},{1,3},{2,0},{3,1},{4,6},{5,7},{6,4},{7,5},{8,10},{9,11},{10,... | collective-permute-start | bytes 2359304 | tf_op jit(solution)/shard_map/ppermute | solution.py:68
  324.8 19.2 %collective-permute-start.21 = (bf16[512,768]{1,0:T(8,128)(2,1)S(1)}, bf16[512,768]{1,0:T(8,128)(2,1)S(1)}, u32[]{:S(2)}, u32[]{:S(2)}) collective-permute-start(bf16[512,768]{1,0:T(8,128)(2,1)S(1)} %get-tuple-element.108), channel_id=1, source_target_pairs={{0,2},{1,3},{2,0},{3,1},{4,6},{5,7},{6,4},{7,5},{8,10},{9,11},{10,... | collective-permute-start | bytes 2359304 | tf_op jit(solution)/shard_map/ppermute | solution.py:68
  326.6 17.4 %collective-permute-start.20 = (bf16[512,768]{1,0:T(8,128)(2,1)S(1)}, bf16[512,768]{1,0:T(8,128)(2,1)S(1)}, u32[]{:S(2)}, u32[]{:S(2)}) collective-permute-start(bf16[512,768]{1,0:T(8,128)(2,1)S(1)} %get-tuple-element.108), channel_id=1, source_target_pairs={{0,1},{1,0},{2,3},{3,2},{4,5},{5,4},{6,7},{7,6},{8,9},{9,8},{10,11... | collective-permute-start | bytes 2359304 | tf_op jit(solution)/shard_map/ppermute | solution.py:68
  369.4 19.7 %collective-permute-start.24 = (bf16[512,768]{1,0:T(8,128)(2,1)S(1)}, bf16[512,768]{1,0:T(8,128)(2,1)S(1)}, u32[]{:S(2)}, u32[]{:S(2)}) collective-permute-start(bf16[512,768]{1,0:T(8,128)(2,1)S(1)} %fusion.47), channel_id=1, source_target_pairs={{0,2},{1,3},{2,0},{3,1},{4,6},{5,7},{6,4},{7,5},{8,10},{9,11},{10,... | collective-permute-start | bytes 2359304 | tf_op jit(solution)/shard_map/ppermute | solution.py:68
  396.8 13.2 %collective-permute-start.27 = (bf16[2,512,192]{2,1,0:T(8,128)(2,1)S(1)}, bf16[2,512,192]{2,1,0:T(8,128)(2,1)S(1)}, u32[]{:S(2)}, u32[]{:S(2)}) collective-permute-start(bf16[2,512,192]{2,1,0:T(8,128)(2,1)S(1)} %pad_maximum_fusion.19), channel_id=1, source_target_pairs={{0,2},{1,3},{2,0},{3,1},{4,6},{5,7},{6,4},{7,5},{8,10},{9,11},{10,... | collective-permute-start | bytes 1179656 | tf_op jit(solution)/shard_map/ppermute | solution.py:68
  399.5 12.1 %collective-permute-start.31 = (bf16[2,192,768]{2,1,0:T(8,128)(2,1)}, bf16[2,192,768]{2,1,0:T(8,128)(2,1)S(1)}, u32[]{:S(2)}, u32[]{:S(2)}) collective-permute-start(bf16[2,192,768]{2,1,0:T(8,128)(2,1)} %pad_maximum_fusion.12), channel_id=1, source_target_pairs={{0,1},{1,0},{2,3},{3,2},{4,5},{5,4},{6,7},{7,6},{8,9},{9,8},{10,11... | collective-permute-start | bytes 1769480 | tf_op jit(solution)/shard_map/ppermute | solution.py:68
  410.9 5.4 collective-permute-start.28
  414.6 90.2 %collective-permute-start.32 = (bf16[192,768]{1,0:T(8,128)(2,1)}, bf16[192,768]{1,0:T(8,128)(2,1)}, u32[]{:S(2)}, u32[]{:S(2)}) collective-permute-start(bf16[192,768]{1,0:T(8,128)(2,1)} %fusion.241), channel_id=1, source_target_pairs={{0,2},{1,3},{2,0},{3,1},{4,6},{5,7},{6,4},{7,5},{8,10},{9,11},{10,... | collective-permute-start | bytes 884744 | tf_op jit(solution)/shard_map/ppermute | solution.py:68
  507.4 136.4 %reduce-scatter.5.cloned.1.call-start = ((), (), s32[]{:S(2)}) async-start(), calls=%async_computation.4 | async-start | bytes 2654208 | tf_op jit(solution)/shard_map/reduce_scatter | solution.py:266
  520.3 187.6 %all-gather.3.cloned.1.call-start = ((), (), s32[]{:S(2)}) async-start(), calls=%async_computation.3 | async-start | bytes 1327104 | tf_op jit(solution)/shard_map/all_gather | solution.py:267
  571.8 167.4 %all-gather.5.cloned.1.call-start = ((), (), s32[]{:S(2)}) async-start(), calls=%async_computation.5 | async-start | bytes 2654208 | tf_op jit(solution)/shard_map/all_gather | solution.py:267
  651.9 8.5 %collective-permute-start.29 = (bf16[2,512,768]{2,1,0:T(8,128)(2,1)}, bf16[2,512,768]{2,1,0:T(8,128)(2,1)}, u32[]{:S(2)}, u32[]{:S(2)}) collective-permute-start(bf16[2,512,768]{2,1,0:T(8,128)(2,1)} %pad_maximum_fusion.8), channel_id=1, source_target_pairs={{0,1},{1,0},{2,3},{3,2},{4,5},{5,4},{6,7},{7,6},{8,9},{9,8},{10,11... | collective-permute-start | bytes 4718600 | tf_op jit(solution)/shard_map/ppermute | solution.py:68
  665.7 38.2 %collective-permute-start.30 = (bf16[512,768]{1,0:T(8,128)(2,1)}, bf16[512,768]{1,0:T(8,128)(2,1)}, u32[]{:S(2)}, u32[]{:S(2)}) collective-permute-start(bf16[512,768]{1,0:T(8,128)(2,1)} %fusion.43), channel_id=1, source_target_pairs={{0,2},{1,3},{2,0},{3,1},{4,6},{5,7},{6,4},{7,5},{8,10},{9,11},{10,... | collective-permute-start | bytes 2359304 | tf_op jit(solution)/shard_map/ppermute | solution.py:68
  (87 other events, 785.2 us)
Sparse Core Ops, SparseCore 0:
  507.5 64.2 reduce-scatter.2
  575.9 67.8 reduce-scatter.4
  646.0 40.3 all-gather.2
  688.4 50.8 all-gather.4

commit v2 on v1

v2 whole, which is shorter than its diff:
```python
import functools

import jax
import jax.numpy as jnp
from jax import lax
from jax.experimental import pallas as pl
from jax.experimental.pallas import tpu as pltpu
from jax.sharding import PartitionSpec as P

HEAD_DIM = 64
LANES = 128
CLIP_RANGE = 3.0
NORM_EPSILON = 1e-05
MASKED_SCORE = -1e30
SEG_LANE = HEAD_DIM
ROW_TERM = HEAD_DIM + 16
Q_BLOCK = 256
CHUNKS = 2
BF16, F32 = jnp.bfloat16, jnp.float32
ROWS_ROWS = (((0,), (0,)), ((), ()))
COLS_COLS = (((1,), (1,)), ((), ()))


def clip_act(values):
    return CLIP_RANGE * jnp.tanh(values / CLIP_RANGE)


def clip_slope(values):
    level = jnp.tanh(values / CLIP_RANGE)
    return 1.0 - level * level


def normal_parts(values):
    bell = jnp.exp(-0.5 * values * values)
    step = 1.0 / (1.0 + 0.23164188843 * jnp.abs(values))
    series = 0.5307027145 * step - 0.7265760135
    series = series * step + 0.7107068705
    series = series * step - 0.142248368
    series = series * step + 0.127414796
    tail = series * step * bell
    return jnp.where(values >= 0.0, 1.0 - tail, tail), bell


def norm_forward(hidden, gain, shift):
    row_mean = jnp.mean(hidden, axis=-1, keepdims=True)
    centred = hidden - row_mean
    inv_std = lax.rsqrt(jnp.mean(centred * centred, axis=-1, keepdims=True) + NORM_EPSILON)
    normed = centred * inv_std
    return (normed * gain + shift, normed, inv_std)


def norm_backward(grad_out, normed, inv_std, gain):
    grad_normed = grad_out * gain
    centre = jnp.mean(grad_normed, axis=-1, keepdims=True)
    inner_sum = jnp.mean(grad_normed * normed, axis=-1, keepdims=True)
    return inv_std * (grad_normed - centre - normed * inner_sum)


def dot(left, right):
    return jnp.dot(left, right, preferred_element_type=F32)


def dot_rows(left, right):
    return lax.dot_general(left, right, ROWS_ROWS, preferred_element_type=F32)


def dot_cols(left, right):
    return lax.dot_general(left, right, COLS_COLS, preferred_element_type=F32)


def swap(array, bit):
    size = lax.axis_size("tensor")
    return lax.ppermute(array, "tensor", [(i, i ^ bit) for i in range(size)])


def gather_blocks(own):
    far = swap(own, 2)
    near = swap(own, 1)
    return [own, near, far, swap(far, 1)]


def reduce_blocks(blocks):
    near = swap(jnp.stack([blocks[1], blocks[3]]).astype(BF16), 1).astype(F32)
    far = swap((blocks[2] + near[1]).astype(BF16), 2).astype(F32)
    return blocks[0] + near[0] + far


def sum_small(array):
    array = array + swap(array, 1)
    return array + swap(array, 2)


def lookup(indices, lookup_table):
    labels = jnp.arange(lookup_table.shape[0], dtype=jnp.int32)
    picked = jnp.where(indices[:, None] == labels[None, :], lookup_table[None, :], 0)
    return jnp.sum(picked, axis=1)


def segment_tables(lengths, parent):
    count = lengths.shape[0]
    labels = jnp.arange(count, dtype=jnp.int32)
    row, col = labels[:, None], labels[None, :]
    starts = jnp.sum(jnp.where(col < row, lengths[None, :], 0), axis=1)
    two = lookup(parent, parent)
    allowed = (col == row) | (col == parent[:, None]) | (col == two[:, None])
    allowed = allowed | (parent[None, :] == row) | (two[None, :] == row)
    after = LANES - SEG_LANE - count
    lanes = jnp.pad(jnp.stack([starts, starts + lengths]), ((0, 6), (SEG_LANE, after)))
    blocked = jnp.pad((~allowed).astype(BF16), ((SEG_LANE, after), (SEG_LANE, after)))
    return lanes, blocked


def split_three(values):
    first = values.astype(BF16).astype(F32)
    second = (values - first).astype(BF16).astype(F32)
    return first, second, values - first - second


def in_lane(shape, axis, terms):
    lane = lax.broadcasted_iota(jnp.int32, shape, axis)
    spread = jnp.zeros(shape, F32)
    for offset, term in enumerate(terms):
        spread = jnp.where(lane == ROW_TERM + offset, term, spread)
    return spread


def forward_kernel(base_ref, x0, x1, x2, x3, w_ref, b_ref, seg_ref, blocked_ref, *rest, student):
    if student:
        qkv_ref, ctx_ref, source, own, near, far, joined, query_part, key_part, keys, vals_t = rest
    else:
        sent, source, joined, query_part, key_part, keys, vals_t = rest
    blocks = (x0, x1, x2, x3)
    own_rows = x0.shape[0]
    rows = own_rows * len(blocks)
    head = pl.program_id(0)

    @pl.when(head == 0)
    def _():
        lane = lax.broadcasted_iota(jnp.int32, (own_rows, LANES), 1)
        for j, block in enumerate(blocks):
            part = slice(j * own_rows, (j + 1) * own_rows)
            if student:
                source[part, :] = clip_act(block[...].astype(F32)).astype(BF16)
            else:
                source[part, :] = block[...]
            place = lax.broadcasted_iota(jnp.int32, (own_rows, LANES), 0) + base_ref[j]
            inside = (place >= seg_ref[0:1, :]) & (place < seg_ref[1:2, :])
            query_part[part, :] = jnp.where(inside, MASKED_SCORE, 0.0).astype(BF16)
            links = dot(jnp.where(inside, 1.0, 0.0).astype(BF16), blocked_ref[...])
            ones = (lane >= ROW_TERM) & (lane < ROW_TERM + 3)
            key_part[part, :] = jnp.where(ones, 1.0, links).astype(BF16)

    proj = (dot(source[...], w_ref[0]) + b_ref[0]).astype(BF16)
    queries = proj[:, :LANES] + query_part[...]
    keys[...] = proj[:, LANES : 2 * LANES] + key_part[...]
    vals_t[...] = proj[:, 2 * LANES :].T
    if student:
        qkv_ref[:, LANES : 2 * LANES] = keys[...]
        lane = lax.broadcasted_iota(jnp.int32, (rows, LANES), 1)
        ones = jnp.where((lane >= ROW_TERM) & (lane < ROW_TERM + 3), 1.0, 0.0).astype(BF16)
        qkv_ref[:, 2 * LANES :] = proj[:, 2 * LANES :] + ones
    scores = []
    for start in range(0, rows, Q_BLOCK):
        scores.append(dot_cols(keys[...], queries[start : start + Q_BLOCK]))
    for index, block in enumerate(scores):
        part = slice(index * Q_BLOCK, (index + 1) * Q_BLOCK)
        peak = jnp.max(block, axis=0, keepdims=True)
        raised = jnp.exp(block - peak)
        total = jnp.sum(raised, axis=0, keepdims=True)
        weights = (raised * (1.0 / total)).astype(BF16)
        context = dot(vals_t[...], weights)[:HEAD_DIM].T
        joined[head, part, :] = context
        if student:
            ctx_ref[0, part, :] = context
            terms = split_three(-(peak + jnp.log(total)))
            spread = in_lane((LANES, Q_BLOCK), 0, terms)
            qkv_ref[part, :LANES] = queries[part] + spread.T.astype(BF16)

    @pl.when(head == pl.num_programs(0) - 1)
    def _():
        for j in range(len(blocks)):
            part = slice(j * own_rows, (j + 1) * own_rows)
            block = jnp.concatenate([joined[h, part, :] for h in range(joined.shape[0])], axis=1)
            if not student:
                sent[j] = block.astype(BF16)
            elif j < 2:
                (own, near)[j][...] = clip_act(block).astype(BF16)
            else:
                far[j - 2] = clip_act(block).astype(BF16)


def attend_forward(base, blocks, weight, bias, seg_lanes, blocked, student):
    own_rows, width = blocks[0].shape
    rows = own_rows * len(blocks)
    heads = weight.shape[0]
    cols = 3 * LANES
    head_cols = heads * HEAD_DIM
    whole = lambda *shape: pl.BlockSpec(shape, lambda h: (0,) * len(shape))
    array = jax.ShapeDtypeStruct
    if student:
        out_specs = [
            pl.BlockSpec((rows, cols), lambda h: (0, h)),
            pl.BlockSpec((1, rows, HEAD_DIM), lambda h: (h, 0, 0)),
            whole(rows, width),
            whole(own_rows, head_cols),
            whole(own_rows, head_cols),
            whole(2, own_rows, head_cols),
        ]
        out_shape = [
            array((rows, heads * cols), BF16),
            array((heads, rows, HEAD_DIM), F32),
            array((rows, width), BF16),
            array((own_rows, head_cols), BF16),
            array((own_rows, head_cols), BF16),
            array((2, own_rows, head_cols), BF16),
        ]
        scratch = []
    else:
        out_specs = [whole(len(blocks), own_rows, head_cols)]
        out_shape = [array((len(blocks), own_rows, head_cols), BF16)]
        scratch = [pltpu.VMEM((rows, width), BF16)]
    scratch += [
        pltpu.VMEM((heads, rows, HEAD_DIM), F32),
        pltpu.VMEM((rows, LANES), BF16),
        pltpu.VMEM((rows, LANES), BF16),
        pltpu.VMEM((rows, LANES), BF16),
        pltpu.VMEM((LANES, rows), BF16),
    ]
    return pl.pallas_call(
        functools.partial(forward_kernel, student=student),
        grid=(heads,),
        in_specs=[pl.BlockSpec(memory_space=pltpu.SMEM)]
        + [whole(own_rows, width)] * 4
        + [
            pl.BlockSpec((1, width, cols), lambda h: (h, 0, 0)),
            pl.BlockSpec((1, 1, cols), lambda h: (h, 0, 0)),
            whole(*seg_lanes.shape),
            whole(*blocked.shape),
        ],
        out_specs=out_specs,
        out_shape=out_shape,
        scratch_shapes=scratch,
        compiler_params=pltpu.CompilerParams(vmem_limit_bytes=58 * 2**20),
        cost_estimate=pl.CostEstimate(
            flops=16 * heads * rows * rows * HEAD_DIM,
            bytes_accessed=2 * rows * (width + 2 * heads * cols),
            transcendentals=heads * rows * rows,
        ),
        name="student_attention" if student else "teacher_attention",
    )(base, *blocks, weight, bias, seg_lanes, blocked)


def backward_kernel(
    qkv_ref, ctx_ref, x_ref, w_ref, g0, g1, g2, g3,
    wg_ref, bg_ref, own_ref, near_ref, far_ref,
    grads, packed, keys_t, total, *, key_block,
):
    blocks = (g0, g1, g2, g3)
    own_rows = g0.shape[0]
    rows = own_rows * len(blocks)
    heads = grads.shape[0]
    head = pl.program_id(0)

    @pl.when(head == 0)
    def _():
        for h in range(heads):
            for j, block in enumerate(blocks):
                part = slice(j * own_rows, (j + 1) * own_rows)
                one = block[:, h * HEAD_DIM : (h + 1) * HEAD_DIM].astype(F32)
                grads[h, part, :] = jnp.concatenate([one, jnp.zeros_like(one)], axis=1).astype(BF16)
        packed[...] = jnp.zeros_like(packed)

    queries = qkv_ref[:, :LANES]
    slopes = grads[head]
    inner = -jnp.sum(
        slopes[:, :HEAD_DIM].astype(F32) * ctx_ref[0], axis=1, keepdims=True
    )
    slopes = slopes + in_lane((rows, LANES), 1, split_three(inner)).astype(BF16)
    keys_t[...] = qkv_ref[:, LANES : 2 * LANES].T
    query_grad = None
    for start in range(0, rows, key_block):
        part = slice(start, start + key_block)
        weights = jnp.exp(dot_cols(qkv_ref[part, LANES : 2 * LANES], queries))
        grad_weights = dot_cols(qkv_ref[part, 2 * LANES :], slopes)
        grad_scores = (weights * grad_weights).astype(BF16)
        step = dot(keys_t[:, part], grad_scores)
        query_grad = step if query_grad is None else query_grad + step
        key_grad = dot(grad_scores, queries)[:, :HEAD_DIM]
        packed[part, LANES : LANES + HEAD_DIM] = key_grad.astype(BF16)
        value_grad = dot(weights.astype(BF16), slopes)[:, :HEAD_DIM]
        packed[part, 2 * LANES : 2 * LANES + HEAD_DIM] = value_grad.astype(BF16)
    packed[:, :HEAD_DIM] = query_grad[:HEAD_DIM].T.astype(BF16)
    bg_ref[0] = jnp.sum(packed[...].astype(F32), axis=0, keepdims=True)
    weight_grad = dot_rows(packed[...], x_ref[...])
    for c, factor in enumerate((0.125, 1.0, 1.0)):
        wg_ref[0, c * HEAD_DIM : (c + 1) * HEAD_DIM, :] = (
            weight_grad[c * LANES : c * LANES + HEAD_DIM] * factor
        ).astype(BF16)
    for j in range(len(blocks)):
        part = slice(j * own_rows, (j + 1) * own_rows)
        step = dot_cols(packed[part, :], w_ref[0])
        total[part, :] = jnp.where(head == 0, step, total[part, :] + step)

    @pl.when(head == pl.num_programs(0) - 1)
    def _():
        part = lambda j: slice(j * own_rows, (j + 1) * own_rows)
        own_ref[...] = total[part(0), :]
        far_ref[...] = total[part(2), :]
        near_ref[0] = total[part(1), :].astype(BF16)
        near_ref[1] = total[part(3), :].astype(BF16)


def attend_backward(qkv, context, source, weight, blocks):
    rows, width = source.shape
    own_rows, head_cols = blocks[0].shape
    cols = 3 * LANES
    heads = weight.shape[0]
    array = jax.ShapeDtypeStruct
    whole = lambda *shape: pl.BlockSpec(shape, lambda h: (0,) * len(shape))
    head_block = lambda *shape: pl.BlockSpec((1,) + shape, lambda h: (h, 0, 0))
    return pl.pallas_call(
        functools.partial(backward_kernel, key_block=256),
        grid=(heads,),
        in_specs=[
            pl.BlockSpec((rows, cols), lambda h: (0, h)),
            head_block(rows, HEAD_DIM),
            whole(rows, width),
            head_block(width, cols),
        ]
        + [whole(own_rows, head_cols)] * 4,
        out_specs=[
            head_block(3 * HEAD_DIM, width),
            head_block(1, cols),
            whole(own_rows, width),
            whole(2, own_rows, width),
            whole(own_rows, width),
        ],
        out_shape=[
            array((heads, 3 * HEAD_DIM, width), BF16),
            array((heads, 1, cols), F32),
            array((own_rows, width), F32),
            array((2, own_rows, width), BF16),
            array((own_rows, width), F32),
        ],
        scratch_shapes=[
            pltpu.VMEM((heads, rows, LANES), BF16),
            pltpu.VMEM((rows, cols), BF16),
            pltpu.VMEM((LANES, rows), BF16),
            pltpu.VMEM((rows, width), F32),
        ],
        compiler_params=pltpu.CompilerParams(vmem_limit_bytes=58 * 2**20),
        cost_estimate=pl.CostEstimate(
            flops=40 * heads * rows * rows * HEAD_DIM,
            bytes_accessed=2 * rows * heads * (cols + 7 * LANES),
            transcendentals=heads * rows * rows,
        ),
        name="attention_backward",
    )(qkv, context, source, weight, *blocks)


(OUT_BIAS, GAIN_1, SHIFT_1, DOWN_BIAS, GAIN_2, SHIFT_2, UP_BIAS) = range(7)
T_VECTORS = 7
LOSS_ROW, UP_ROW = 6, 7


def middle_kernel(
    x_ref, ca0, ca1, ca23, ca3, tc_ref, w_out, tw_out, w_up, w_down, vec,
    pack_own, pack_near, pack_a, pack_b, pack_c, pack_d,
    out_ref, gh_ref, ffn_ref, outg_ref, g0_ref, g1_ref, g2_ref, g3_ref, small_ref,
    tc1, tc2, tcf, tc3, y_all, g_all, slope, hid, gu_all, t_out, first, normed, two, inv,
    part0, part2, send1, send2, send3, near0, near2, far0, gs, gr, packs,
    send_sem, recv_sem, pack_sem,
):
    me = lax.axis_index("tensor")
    near_id = me + 1 - 2 * lax.rem(me, 2)
    far_id = lax.rem(me + 2, 4)
    own_rows, width = x_ref.shape
    hidden = w_down.shape[0]
    head_cols = ca0.shape[1]
    size = own_rows // CHUNKS
    chunks = [slice(c * size, (c + 1) * size) for c in range(CHUNKS)]
    tiles = [slice(n, n + 256) for n in range(0, hidden, 256)]
    group = lambda j: slice(j * head_cols, (j + 1) * head_cols)
    row = lambda index: vec[index : index + 1, :]

    barrier = pltpu.get_barrier_semaphore()
    for other in (near_id, far_id):
        pl.semaphore_signal(
            barrier, inc=1, device_id={"tensor": other}, device_id_type=pl.DeviceIdType.MESH
        )
    pl.semaphore_wait(barrier, 2)

    count = [0]
    started = []

    def put(source, target, device):
        index = count[0]
        count[0] += 1
        copy = pltpu.make_async_remote_copy(
            src_ref=source,
            dst_ref=target,
            send_sem=send_sem.at[index],
            recv_sem=recv_sem.at[index],
            device_id={"tensor": device},
            device_id_type=pl.DeviceIdType.MESH,
        )
        copy.start()
        started.append(copy)
        return copy

    t_far = put(tc_ref.at[2], tc2, far_id)
    t_pass = put(tc_ref.at[3], tcf, far_id)
    t_near = put(tc_ref.at[1], tc1, near_id)

    pack_refs = [pack_own.at[0], pack_own.at[1], pack_near.at[0], pack_near.at[1]]
    pack_refs += [pack_a, pack_b, pack_c, pack_d]

    def load_pack(index):
        slot = index % 2
        return pltpu.make_async_copy(pack_refs[index], packs.at[slot], pack_sem.at[slot])

    load_pack(0).start()
    small_ref[...] = jnp.zeros_like(small_ref)

    def add_small(index, values):
        small_ref[index : index + 1, :] += jnp.sum(values, axis=0, keepdims=True)

    def share(own_block, where):
        return (
            put(own_block.at[0, where], own_block.at[1, where], near_id),
            put(own_block.at[0, where], own_block.at[2, where], far_id),
        )

    y_sent = []
    for rows in chunks:
        attn = dot(ca0[rows, :], w_out[group(0), :]) + dot(ca1[rows, :], w_out[group(1), :])
        attn += dot(ca23[0, rows, :], w_out[group(2), :]) + dot(ca3[rows, :], w_out[group(3), :])
        y_one, y_normed, y_inv = norm_forward(
            x_ref[rows, :].astype(F32) + attn + row(OUT_BIAS), row(GAIN_1), row(SHIFT_1)
        )
        first[rows, :] = y_one
        normed[rows, :] = y_normed
        inv[rows, :] = jnp.broadcast_to(y_inv, (size, LANES))
        y_all[0, rows, :] = clip_act(y_one).astype(BF16)
        y_sent.append(share(y_all, rows))

    def forward_block(j, rows):
        total = None
        for cols in tiles:
            upward = dot(y_all[j, rows, :], w_up[:, cols]) + row(UP_BIAS)[:, cols]
            cdf, bell = normal_parts(upward)
            level = jnp.tanh(upward * cdf * (1.0 / CLIP_RANGE))
            act = (CLIP_RANGE * level).astype(BF16)
            hid[j, rows, cols] = act
            slope[j, rows, cols] = (1.0 - level * level) * (
                cdf + upward * bell * 0.3989422804014327
            )
            step = dot(act, w_down[cols, :])
            total = step if total is None else total + step
        return total

    def backward_block(j, rows):
        total = None
        for cols in tiles:
            grad = dot_cols(g_all[j, rows, :], w_down[cols, :])
            grad = (grad * slope[j, rows, cols]).astype(BF16)
            gu_all[j, rows, cols] = grad
            small_ref[UP_ROW : UP_ROW + 1, cols] += jnp.sum(
                grad.astype(F32), axis=0, keepdims=True
            )
            step = dot_cols(grad, w_up[:, cols])
            total = step if total is None else total + step
        return total

    def near_blocks(work, sent):
        copies = []
        for rows in chunks:
            part0[rows, :] = work(0, rows)
        for rows, (near, _) in zip(chunks, sent):
            near.wait_recv()
            send1[rows, :] = work(1, rows).astype(BF16)
            copies.append(put(send1.at[rows], near0.at[rows], near_id))
        return copies

    def far_blocks(block, work, sent):
        copies = []
        for rows, (_, far) in zip(chunks, sent):
            far.wait_recv()
            passed = put(block.at[2, rows], block.at[3, rows], near_id)
            part2[rows, :] = work(2, rows)
            passed.wait_recv()
            send3[rows, :] = work(3, rows).astype(BF16)
            met = put(send3.at[rows], near2.at[rows], near_id)
            met.wait_recv()
            send2[rows, :] = (part2[rows, :] + near2[rows, :].astype(F32)).astype(BF16)
            copies.append(put(send2.at[rows], far0.at[rows], far_id))
        return copies

    def summed(rows, near, far):
        near.wait_recv()
        far.wait_recv()
        return part0[rows, :] + near0[rows, :].astype(F32) + far0[rows, :].astype(F32)

    y_near = near_blocks(forward_block, y_sent)

    t_pass.wait_recv()
    t_last = put(tcf, tc3, near_id)
    t_near.wait_recv()
    t_far.wait_recv()
    t_row = lambda index: row(T_VECTORS + index)
    t_attn = dot(tc_ref[0], tw_out[group(0), :]) + dot(tc1[...], tw_out[group(1), :])
    t_attn += dot(tc2[...], tw_out[group(2), :])
    t_last.wait_recv()
    t_attn += dot(tc3[...], tw_out[group(3), :])
    t_one, _, _ = norm_forward(x_ref[...].astype(F32) + t_attn + t_row(0), t_row(1), t_row(2))
    two[...] = t_one
    t_out[...] = t_one + t_row(3)
    half = hidden // 2
    t_in = t_one.astype(BF16)
    for index in range(len(pack_refs)):
        slot = index % 2
        if index + 1 < len(pack_refs):
            load_pack(index + 1).start()
        load_pack(index).wait()
        upward = dot_cols(t_in, packs[slot, :half, :])
        upward = upward + packs[slot, hidden : hidden + 1, :half].astype(F32)
        act = (upward * normal_parts(upward)[0]).astype(BF16)
        t_out[...] += dot(act, packs[slot, half:hidden, :])
    t_out[...] = norm_forward(t_out[...], t_row(4), t_row(5))[0]

    y_far = far_blocks(y_all, forward_block, y_sent)

    g_sent = []
    for copy in started:
        copy.wait_send()
    started.clear()
    for rows, near, far in zip(chunks, y_near, y_far):
        ffn = summed(rows, near, far)
        out, n_two, inv_two = norm_forward(
            first[rows, :] + ffn + row(DOWN_BIAS), row(GAIN_2), row(SHIFT_2)
        )
        out_ref[rows, :] = out.astype(BF16)
        gap = out - t_out[rows, :]
        add_small(LOSS_ROW, gap * gap)
        add_small(GAIN_2, gap * n_two)
        add_small(SHIFT_2, gap)
        grad_two = norm_backward(gap, n_two, inv_two, row(GAIN_2))
        two[rows, :] = grad_two
        grad_ffn = grad_two.astype(BF16)
        add_small(DOWN_BIAS, grad_ffn.astype(F32))
        g_all[0, rows, :] = grad_ffn
        g_sent.append(share(g_all, rows))

    g_near = near_blocks(backward_block, g_sent)
    g_far = far_blocks(g_all, backward_block, g_sent)
    flat = lambda block: block[...].reshape(4 * own_rows, block.shape[2])
    ffn_ref[:width, :] = dot_rows(flat(y_all), flat(gu_all)).astype(BF16)
    ffn_ref[width:, :] = dot_rows(flat(hid), flat(g_all)).astype(BF16)

    passes = []
    for c, (rows, near, far) in enumerate(zip(chunks, g_near, g_far)):
        y_one = first[rows, :]
        grad_one = two[rows, :] + summed(rows, near, far) * clip_slope(y_one)
        n_one = normed[rows, :]
        add_small(GAIN_1, grad_one * n_one)
        add_small(SHIFT_1, grad_one)
        grad_h = norm_backward(grad_one, n_one, inv[rows, :1], row(GAIN_1))
        gh_ref[rows, :] = grad_h
        grad_attn = grad_h.astype(BF16)
        add_small(OUT_BIAS, grad_attn.astype(F32))
        for j, ca in enumerate((ca0.at[rows], ca1.at[rows], ca23.at[0, rows], ca3.at[rows])):
            act = ca[...]
            level = act.astype(F32) * (1.0 / CLIP_RANGE)
            grad = dot_cols(grad_attn, w_out[group(j), :]) * (1.0 - level * level)
            gs[j, rows, :] = grad.astype(BF16)
            step = dot_rows(act, grad_attn)
            if c:
                step = step + part2[group(j), :]
            part2[group(j), :] = step
        passes.append(
            (
                put(gs.at[3, rows], gr.at[3, rows], far_id),
                put(gs.at[2, rows], gr.at[1, rows], far_id),
                put(gs.at[1, rows], gr.at[0, rows], near_id),
            )
        )
    g0_ref[...] = gs[0]
    for j in range(4):
        outg_ref[j] = part2[group(j), :].astype(BF16)
    lasts = []
    for rows, (passing, _, _) in zip(chunks, passes):
        passing.wait_recv()
        lasts.append(put(gr.at[3, rows], gr.at[2, rows], near_id))
    for rows, (_, far, near), last in zip(chunks, passes, lasts):
        near.wait_recv()
        g1_ref[rows, :] = gr[0, rows, :]
        far.wait_recv()
        g2_ref[rows, :] = gr[1, rows, :]
        last.wait_recv()
        g3_ref[rows, :] = gr[2, rows, :]
    for copy in started:
        copy.wait_send()


def middle(x_own, cas, tc, w_out, tw_out, w_up, w_down, vectors, packs):
    own_rows, width = x_own.shape
    hidden = w_down.shape[0]
    head_cols = cas[0].shape[1]
    array = jax.ShapeDtypeStruct
    vmem = pl.BlockSpec(memory_space=pltpu.VMEM)
    transfers = 4 + 4 * 3 * CHUNKS + 4 * CHUNKS
    square = lambda kind: pltpu.VMEM((own_rows, width), kind)
    four = lambda cols, kind: pltpu.VMEM((4, own_rows, cols), kind)
    return pl.pallas_call(
        middle_kernel,
        in_specs=[vmem] * 11 + [pl.BlockSpec(memory_space=pl.ANY)] * 6,
        out_specs=[vmem] * 9,
        out_shape=[
            array((own_rows, width), BF16),
            array((own_rows, width), F32),
            array((width + hidden, width), BF16),
            array((4, head_cols, width), BF16),
        ]
        + [array((own_rows, head_cols), BF16)] * 4
        + [array((8, width), F32)],
        scratch_shapes=[pltpu.VMEM((own_rows, head_cols), BF16)] * 4
        + [four(width, BF16), four(width, BF16), four(hidden, F32), four(hidden, BF16)]
        + [four(hidden, BF16)]
        + [square(F32)] * 4
        + [pltpu.VMEM((own_rows, LANES), F32)]
        + [square(F32), pltpu.VMEM((4 * max(own_rows // 4, head_cols), width), F32)]
        + [square(BF16)] * 6
        + [four(head_cols, BF16), four(head_cols, BF16)]
        + [
            pltpu.VMEM((2,) + packs[2].shape, BF16),
            pltpu.SemaphoreType.DMA((transfers,)),
            pltpu.SemaphoreType.DMA((transfers,)),
            pltpu.SemaphoreType.DMA((2,)),
        ],
        compiler_params=pltpu.CompilerParams(
            collective_id=3, has_side_effects=True, vmem_limit_bytes=62 * 2**20
        ),
        cost_estimate=pl.CostEstimate(
            flops=120 * own_rows * width * hidden, bytes_accessed=2**25, transcendentals=2**22
        ),
        name="middle",
    )(x_own, *cas, tc, w_out, tw_out, w_up, w_down, vectors, *packs)


def padded_heads(weight, bias):
    width, _, cols = weight.shape
    heads = cols // HEAD_DIM
    scale = jnp.array([0.125, 1.0, 1.0], F32)
    weight = weight.reshape(width, 3, heads, HEAD_DIM).transpose(2, 0, 1, 3)
    weight = weight * scale[None, None, :, None].astype(weight.dtype)
    weight = jnp.pad(weight, ((0, 0), (0, 0), (0, 0), (0, LANES - HEAD_DIM)))
    full = jnp.stack([bias[0] * 0.125, jnp.zeros_like(bias[0]), bias[1]]).astype(F32)
    full = full.reshape(3, heads, HEAD_DIM).transpose(1, 0, 2)
    full = jnp.pad(full, ((0, 0), (0, 0), (0, LANES - HEAD_DIM)))
    return (
        weight.reshape(heads, width, 3 * LANES).astype(BF16),
        full.reshape(heads, 1, 3 * LANES),
    )


def reduce_dp(array):
    share = lax.psum_scatter(array.astype(BF16), "dp", scatter_dimension=0, tiled=True)
    return lax.all_gather(share, "dp", axis=0, tiled=True).astype(F32)


def body(
    tokens,
    seg_lengths,
    parents,
    qkv_latent,
    qv_bias,
    out_latent,
    out_bias,
    norm1_gain,
    norm1_shift,
    up_latent,
    up_bias,
    down_latent,
    down_bias,
    norm2_gain,
    norm2_shift,
    teacher_qkv,
    teacher_qv_bias,
    teacher_out,
    teacher_out_bias,
    teacher_norm1_gain,
    teacher_norm1_shift,
    teacher_up,
    teacher_up_bias,
    teacher_down,
    teacher_down_bias,
    teacher_norm2_gain,
    teacher_norm2_shift,
):
    own_rows, model_width = tokens.shape
    group = lax.axis_size("tensor")
    me = lax.axis_index("tensor")
    all_rows = own_rows * group
    local_cols = qkv_latent.shape[2]
    local_heads = local_cols // HEAD_DIM
    hid = up_latent.shape[1]
    half = hid // 2
    near_x = swap(tokens, 1)
    far_x = swap(tokens, 2)
    blocks = [tokens, near_x, far_x, swap(far_x, 1)]
    sums = sum_small(
        jnp.stack([jnp.sum(jnp.abs(out_latent), axis=0), jnp.sum(jnp.abs(down_latent), axis=0)])
    )
    w_qkv = (jnp.mean(jnp.abs(qkv_latent), axis=0) * jnp.sign(qkv_latent)).astype(BF16)
    w_out = (sums[0] / model_width * jnp.sign(out_latent)).astype(BF16)
    w_up = (jnp.mean(jnp.abs(up_latent), axis=0) * jnp.sign(up_latent)).astype(BF16)
    w_down = (sums[1] / (hid * group) * jnp.sign(down_latent)).astype(BF16)
    seg_lanes, blocked = segment_tables(seg_lengths[0], parents[0])
    base = jnp.stack([(me ^ j) * own_rows for j in range(group)]).astype(jnp.int32)

    up_t = teacher_up.T
    bias_rows = jnp.pad(teacher_up_bias.reshape(2, 1, half), ((0, 0), (0, 15), (0, model_width - half)))
    pack = jnp.concatenate(
        [up_t.reshape(2, half, -1), teacher_down.reshape(2, half, -1), bias_rows], axis=1
    )
    pack, far_x = lax.optimization_barrier((pack, far_x))
    side = lax.rem(lax.axis_index("dp"), 2)
    far_a = swap(lax.dynamic_index_in_dim(pack, side, 0, keepdims=False), 2)
    far_b = lax.ppermute(far_a, "dp", [(i, i ^ 1) for i in range(lax.axis_size("dp"))])
    packs = [pack, swap(pack, 1), far_a, far_b, swap(far_a, 1), swap(far_b, 1)]
    outs = jnp.concatenate([w_out, teacher_out])
    outs = gather_blocks(outs)
    w_out_all = jnp.concatenate([block[:local_cols] for block in outs])
    t_out_all = jnp.concatenate([block[local_cols:] for block in outs])

    wide_qkv, wide_bias = padded_heads(w_qkv, qv_bias)
    qkv, context, x_in_all, ca_own, ca_near, ca_far = attend_forward(
        base, blocks, wide_qkv, wide_bias, seg_lanes, blocked, True
    )
    (t_context,) = attend_forward(
        base, blocks, *padded_heads(teacher_qkv, teacher_qv_bias), seg_lanes, blocked, False
    )
    ca_23 = swap(ca_far, 2)
    cas = [ca_own, swap(ca_near, 1), ca_23, swap(ca_23[1], 1)]
    vectors = [out_bias, norm1_gain, norm1_shift, down_bias, norm2_gain, norm2_shift, up_bias]
    vectors += [teacher_out_bias, teacher_norm1_gain, teacher_norm1_shift]
    vectors += [teacher_down_bias, teacher_norm2_gain, teacher_norm2_shift]
    vectors = jnp.pad(jnp.stack(vectors).astype(F32), ((0, 3), (0, 0)))
    out_own, grad_h, ffn_grads, out_grads, g0, g1, g2, g3, small = middle(
        tokens, cas, t_context, w_out_all, t_out_all, w_up, w_down, vectors, packs
    )
    ffn_share = lax.psum_scatter(ffn_grads, "dp", scatter_dimension=0, tiled=True)
    ffn_grads = lax.all_gather(ffn_share, "dp", axis=0, tiled=True).astype(F32)

    weight_grad, proj_bias_grad, gx_own, gx_near, gx_far = attend_backward(
        qkv, context, x_in_all, wide_qkv, [g0, g1, g2, g3]
    )
    out_grad = reduce_blocks([out_grads[j].astype(F32) for j in range(group)])
    gx_near = swap(gx_near, 1).astype(F32)
    gx_far = swap((gx_far + gx_near[1]).astype(BF16), 2).astype(F32)
    grad_x_in = gx_own + gx_near[0] + gx_far
    input_grad = grad_h + grad_x_in * clip_slope(tokens.astype(F32))

    shared = sum_small(small[:7])
    tree_loss = jnp.sum(shared[6])[None] / (all_rows * model_width)
    proj_bias_grad = proj_bias_grad.reshape(local_heads, 3, LANES)[:, :, :HEAD_DIM]
    proj_bias_grad = proj_bias_grad.transpose(1, 0, 2).reshape(3, local_cols)
    small = jnp.concatenate(
        [
            shared[:6].reshape(-1),
            small[7],
            proj_bias_grad[0] * 0.125,
            proj_bias_grad[2],
        ]
    )
    small = lax.psum(small, "dp")
    shared = small[: 6 * model_width].reshape(6, model_width)
    late = reduce_dp(
        jnp.concatenate([weight_grad.reshape(-1, model_width).astype(F32), out_grad])
    )
    qkv_rows = 3 * local_cols
    qkv_grad = late[:qkv_rows].reshape(local_heads, 3, HEAD_DIM, model_width)
    qkv_grad = qkv_grad.transpose(3, 1, 0, 2).reshape(model_width, 3, local_cols)
    return (
        out_own,
        tree_loss,
        input_grad,
        qkv_grad,
        small[6 * model_width + hid :].reshape(2, local_cols),
        late[qkv_rows:],
        shared[0],
        shared[1],
        shared[2],
        ffn_grads[:model_width],
        small[6 * model_width : 6 * model_width + hid],
        ffn_grads[model_width:],
        shared[3],
        shared[4],
        shared[5],
    )


def solution(mesh):
    rows, cols = ("dp", "tensor"), "tensor"
    vec = P()
    params = (
        P(None, None, cols),
        P(None, cols),
        P(cols, None),
        vec,
        vec,
        vec,
        P(None, cols),
        P(cols),
        P(cols, None),
        vec,
        vec,
        vec,
    )
    in_specs = (P(rows, None), P("dp", None), P("dp", None)) + params + params
    out_specs = (P(rows, None), P("dp"), P(rows, None)) + params
    return jax.shard_map(body, mesh=mesh, in_specs=in_specs, out_specs=out_specs, check_vma=False)
```

time: 759 us -> 566 us (0.75)
  Pallas kernels: 88.3 us -> 212 us
  matrix products: 112 us -> 0 us
  waiting for transfers between devices: 299 us -> 219 us
  local copies, waits for them, and re-layouts: 93.3 us -> 35.2 us
  other arithmetic: 82.1 us -> 28 us
  starting transfers between devices: 24.4 us -> 14 us
    dot_general x17 -> x0, matrix products: 112 us -> none  [the longest x9 65.1 us: dot(): return jnp.dot(left, right, preferred_element_type=F32)]
    pallas_call x2 -> x3, Pallas kernels: 54.4 us -> 163 us  [the longest x1 105 us: middle(): pl.pallas_call(middle_kernel, in_specs=[vmem] * 11 + [pl.BlockSpec(memory...]
    ppermute x33 -> x21, waiting for transfers between devices: 154 us -> 60.8 us  [swap(): return lax.ppermute(array, 'tensor', [(i, i ^ bit) for i in range(size)])]
    reduce_scatter x0 -> x1, waiting for transfers between devices: none -> 71.4 us  [body(): lax.psum_scatter(ffn_grads, 'dp', scatter_dimension=0, tiled=True)]
    reduce_scatter x2 -> x1, waiting for transfers between devices: 123 us -> 62.9 us  [reduce_dp(): lax.psum_scatter(array.astype(BF16), 'dp', scatter_dimension=0, tiled=True)]
    all_gather x0 -> x1, waiting for transfers between devices: none -> 23 us  [body(): ffn_grads = lax.all_gather(ffn_share, 'dp', axis=0, tiled=True).astype(F32)]
    concatenate x8 -> x1, local copies, waits for them, and re-layouts: 22.5 us -> 0.08 us  [body(): jnp.concatenate([shared[:6].reshape(-1), small[7], proj_bias_grad[0] * 0....]
    all_gather x2 -> x1, waiting for transfers between devices: 21.2 us -> 0.01 us  [reduce_dp(): return lax.all_gather(share, 'dp', axis=0, tiled=True).astype(F32)]
  transfers between devices with their start and end apart: 37 -> 26, of which waited for: 13 -> 9; matrix products, arithmetic and copies ran while one was open for 32% -> 9% of each run, Pallas kernels for 12% -> 19%
where the time goes in v2:
time: 566 us; the launch traced here: 560 us
  waiting for transfers between devices  219 us (39%)
  Pallas kernels  212 us (37%)
  blocking collectives  35.3 us (6%)
  local copies, waits for them, and re-layouts  35.2 us (6%)
  other arithmetic  28 us (5%)
  between operations  16.9 us (3%)
  starting transfers between devices  14 us (2%)
    pallas_call x1, Pallas kernels, middle(): pl.pallas_call(middle_kernel, in_specs=[vmem] * 11 + [pl.BlockSpec(memory...  105 us
    reduce_scatter x1, waiting for transfers between devices, body(): lax.psum_scatter(ffn_grads, 'dp', scatter_dimension=0, tiled=True)  71.4 us
    reduce_scatter x1, waiting for transfers between devices, reduce_dp(): lax.psum_scatter(array.astype(BF16), 'dp', scatter_dimension=0, tiled=True)  62.9 us
    ppermute x21, waiting for transfers between devices, swap(): return lax.ppermute(array, 'tensor', [(i, i ^ bit) for i in range(size)])  60.8 us
    pallas_call x2, Pallas kernels, attend_forward(): pl.pallas_call(functools.partial(forward_kernel, student=student), grid=(...  58 us
    pallas_call x1, Pallas kernels, attend_backward(): pl.pallas_call(functools.partial(backward_kernel, key_block=256), grid=(h...  48.2 us
    psum x1, blocking collectives, body(): small = lax.psum(small, 'dp')  35.3 us
    all_gather x1, waiting for transfers between devices, body(): ffn_grads = lax.all_gather(ffn_share, 'dp', axis=0, tiled=True).astype(F32)  23 us
  transfers between devices with their start and end apart: 26, of which 9 were waited for; matrix products, arithmetic and copies ran while one was open for 9% of the time, Pallas kernels for 19%

profile of v2, /device:TPU:0, one launch (start us, length us, event | category | flops | bytes accessed | tf_op | source)
XLA Modules:
  0.0 560.0 jit_solution(12295432343229201897)
XLA Ops:
  7.3 3.0 collective-permute-start.1
  11.5 2.1 abs_reduce_fusion.1
  19.4 1.8 abs_reduce_fusion.2
  21.5 1.4 multiply_convert_fusion.2
  22.9 1.8 multiply_convert_fusion.1.w_up
  24.6 1.5 copy.70
  30.1 3.5 collective-permute-done.7
  37.2 1.9 collective-permute-start.9
  44.1 2.2 copy.69.w_ref
  46.3 1.4 pad.36.clone
  47.7 4.0 copy.65.w_ref
  52.2 1.7 multiply_convert_fusion.w_down
  53.9 22.6 %collective-permute-done.9 = bf16[384,768]{1,0:T(8,128)(2,1)} collective-permute-done((bf16[384,768]{1,0:T(8,128)(2,1)}, bf16[384,768]{1,0:T(8,128)(2,1)}, u32[]{:S(2)}, u32[]{:S(2)}) %collective-permute-start.9) | collective-permute-done | bytes 589856 | tf_op jit(solution)/shard_map/ppermute | solution.py:73
  79.3 1.5 collective-permute-start.13
  81.7 31.0 %student_attention.1 = (bf16[2048,1152]{1,0:T(8,128)(2,1)}, f32[3,2048,64]{2,1,0:T(8,128)}, bf16[2048,768]{1,0:T(8,128)(2,1)}, bf16[512,192]{1,0:T(8,128)(2,1)},...) custom-call(s32[4]{0:T(128)} %pad_add_fusion.1.base_ref, bf16[512,768]{1,0:T(8,128)(2,1)} %x_ref.1, ...), custom_call_target="tpu_custom_call" | custom-call | flops 12884901888 | bytes 12582912 | tf_op jit(solution)/shard_map/student_attention/pallas_call | solution.py:229
  113.3 1.6 pad_maximum_fusion
  114.9 11.7 %collective-permute-done.4.ca23 = bf16[2,512,192]{2,1,0:T(8,128)(2,1)S(1)} collective-permute-done((bf16[2,512,192]{2,1,0:T(8,128)(2,1)}, bf16[2,512,192]{2,1,0:T(8,128)(2,1)S(1)}, u32[]{:S(2)}, u32[]{:S(2)}) %collective-permute-start.4) | collective-permute-done | bytes 393248 | tf_op jit(solution)/shard_map/ppermute | solution.py:73
  127.3 27.1 %teacher_attention.1.tc_ref = bf16[4,512,192]{2,1,0:T(8,128)(2,1)} custom-call(s32[4]{0:T(128)} %pad_add_fusion.1.base_ref, bf16[512,768]{1,0:T(8,128)(2,1)} %x_ref.1, bf16[512,768]{1,0:T(8,128)(2,1)} %collective-permute-done.x1, bf16[512,768]{1,0:T(8,128)(2,1)} %collective-permute-done.1.x2, bf16[512,768]{1,0:T(8,128)(2,1)} %copy-done.50, ...), custom_call_target="tpu_custom_call" | custom-call | flops 12884901888 | bytes 12582912 | tf_op jit(solution)/shard_map/teacher_attention/pallas_call | solution.py:229
  155.1 105.4 %middle.1 = (bf16[512,768]{1,0:T(8,128)(2,1)}, f32[512,768]{1,0:T(8,128)}, bf16[1536,768]{1,0:T(8,128)(2,1)}, bf16[4,192,768]{2,1,0:T(8,128)(2,1)}, bf16[512,192...) custom-call(bf16[512,768]{1,0:T(8,128)(2,1)} %x_ref.1, ...), custom_call_target="tpu_custom_call" | custom-call | flops 36238786560 | bytes 33554432 | tf_op jit(solution)/shard_map/middle/pallas_call | solution.py:614
  261.8 2.0 collective-permute-done.20
  263.9 1.6 collective-permute-start.21
  265.5 48.2 %attention_backward.1 = (bf16[3,192,768]{2,1,0:T(8,128)(2,1)}, f32[3,1,384]{2,1,0:T(1,128)}, f32[512,768]{1,0:T(8,128)}, bf16[2,512,768]{2,1,0:T(8,128)(2,1)}, f32[512,768]{1,0:T(8,128)}) custom-call(bf16[2048,1152]{1,0:T(8,128)(2,1)} %get-tuple-element.43.qkv_ref, f32[3,2048,64]{2,1,0:T(8,128)} %get-tuple-element.44.ctx_ref, ...), custom_call_target="tpu_custom_call" | custom-call | flops 32212254720 | bytes 15728640 | tf_op jit(solution)/shard_map/attention_backward/pallas_call | solution.py:321
  316.9 62.9 %reduce-scatter.3.cloned.1.call-done = bf16[96,768]{1,0:T(8,128)(2,1)} async-done(((bf16[768,768]{1,0:T(8,128)(2,1)}), bf16[96,768]{1,0:T(8,128)(2,1)}) %reduce-scatter.3.cloned.1.call-update) | async-done | bytes 147472 | tf_op jit(solution)/shard_map/reduce_scatter | solution.py:667
  379.8 71.4 %reduce-scatter.5.cloned.1.call-done = bf16[192,768]{1,0:T(8,128)(2,1)} async-done(((bf16[1536,768]{1,0:T(8,128)(2,1)}), bf16[192,768]{1,0:T(8,128)(2,1)}) %reduce-scatter.5.cloned.1.call-update) | async-done | bytes 294928 | tf_op jit(solution)/shard_map/reduce_scatter | solution.py:752
  451.9 2.9 collective-permute-done.18
  454.9 1.6 convert_element_type.92
  457.6 1.5 collective-permute-start.19
  459.9 18.0 %collective-permute-done.17 = f32[7,768]{1,0:T(8,128)S(1)} collective-permute-done((f32[7,768]{1,0:T(8,128)S(1)}, f32[7,768]{1,0:T(8,128)S(1)}, u32[]{:S(2)}, u32[]{:S(2)}) %collective-permute-start.17) | collective-permute-done | bytes 21536 | tf_op jit(solution)/shard_map/ppermute | solution.py:73
  478.0 35.3 %psum.7 = f32[5760]{0:T(1024)S(1)} all-reduce(f32[5760]{0:T(1024)S(1)} %concatenate.26), channel_id=1, replica_groups=mesh['dp'=8,'tensor'=4] {'dp'}, use_global_device_ids=true, to_apply=%region_8.9 | all-reduce | flops 5760 | bytes 46080 | tf_op jit(solution)/shard_map/psum | solution.py:776
  515.9 4.0 fusion.7
  523.8 23.0 %all-gather.5.cloned.1.call-done = bf16[1536,768]{1,0:T(8,128)(2,1)} async-done(((bf16[192,768]{1,0:T(8,128)(2,1)}), bf16[1536,768]{1,0:T(8,128)(2,1)}) %all-gather.5.cloned.1.call-update) | async-done | bytes 2359312 | tf_op jit(solution)/shard_map/all_gather | solution.py:753
  546.8 4.2 fusion.22
  (235 shorter events, 39.5 us)
Async XLA Ops:
  7.2 372.5 %reduce-scatter.3.cloned.1.call-start = ((), (), s32[]{:S(2)}) async-start(), calls=%async_computation.2 | async-start | bytes 1327104 | tf_op jit(solution)/shard_map/reduce_scatter | solution.py:667
  7.3 27.9 %collective-permute-start.1 = (bf16[512,768]{1,0:T(8,128)(2,1)}, bf16[512,768]{1,0:T(8,128)(2,1)}, u32[]{:S(2)}, u32[]{:S(2)}) collective-permute-start(bf16[512,768]{1,0:T(8,128)(2,1)} %x_ref.1), channel_id=1, source_target_pairs={{0,2},{1,3},{2,0},{3,1},{4,6},{5,7},{6,4},{7,5},{8,10},{9,11},{10,... | collective-permute-start | bytes 2359304 | tf_op jit(solution)/shard_map/ppermute | solution.py:73
  10.3 70.5 %collective-permute-start = (bf16[512,768]{1,0:T(8,128)(2,1)}, bf16[512,768]{1,0:T(8,128)(2,1)}, u32[]{:S(2)}, u32[]{:S(2)}) collective-permute-start(bf16[512,768]{1,0:T(8,128)(2,1)} %x_ref.1), channel_id=1, source_target_pairs={{0,1},{1,0},{2,3},{3,2},{4,5},{5,4},{6,7},{7,6},{8,9},{9,8},{10,11... | collective-permute-start | bytes 2359304 | tf_op jit(solution)/shard_map/ppermute | solution.py:73
  14.1 15.8 %collective-permute-start.6 = (f32[2,768]{1,0:T(2,128)}, f32[2,768]{1,0:T(2,128)S(1)}, u32[]{:S(2)}, u32[]{:S(2)}) collective-permute-start(f32[2,768]{1,0:T(2,128)} %pad_maximum_fusion.5), channel_id=1, source_target_pairs={{0,1},{1,0},{2,3},{3,2},{4,5},{5,4},{6,7},{7,6},{8,9},{9,8},{10,11... | collective-permute-start | bytes 18440 | tf_op jit(solution)/shard_map/ppermute | solution.py:73
  30.0 3.7 collective-permute-start.7
  36.3 43.0 %collective-permute-start.12 = (bf16[784,768]{1,0:T(8,128)(2,1)}, bf16[784,768]{1,0:T(8,128)(2,1)}, u32[]{:S(2)}, u32[]{:S(2)}) collective-permute-start(bf16[784,768]{1,0:T(8,128)(2,1)} %dynamic-slice_bitcast_fusion), channel_id=1, source_target_pairs={{0,2},{1,3},{2,0},{3,1},{4,6},{5,7},{6,4},{7,5},{8,10},{9,11},{10,... | collective-permute-start | bytes 3612680 | tf_op jit(solution)/shard_map/ppermute | solution.py:73
  37.2 39.3 %collective-permute-start.9 = (bf16[384,768]{1,0:T(8,128)(2,1)}, bf16[384,768]{1,0:T(8,128)(2,1)}, u32[]{:S(2)}, u32[]{:S(2)}) collective-permute-start(bf16[384,768]{1,0:T(8,128)(2,1)} %pad_maximum_fusion.3), channel_id=1, source_target_pairs={{0,2},{1,3},{2,0},{3,1},{4,6},{5,7},{6,4},{7,5},{8,10},{9,11},{10,... | collective-permute-start | bytes 1769480 | tf_op jit(solution)/shard_map/ppermute | solution.py:73
  40.2 37.4 %collective-permute-start.8 = (bf16[384,768]{1,0:T(8,128)(2,1)}, bf16[384,768]{1,0:T(8,128)(2,1)}, u32[]{:S(2)}, u32[]{:S(2)}) collective-permute-start(bf16[384,768]{1,0:T(8,128)(2,1)} %pad_maximum_fusion.3), channel_id=1, source_target_pairs={{0,1},{1,0},{2,3},{3,2},{4,5},{5,4},{6,7},{7,6},{8,9},{9,8},{10,11... | collective-permute-start | bytes 1769480 | tf_op jit(solution)/shard_map/ppermute | solution.py:73
  51.7 29.1 %collective-permute-start.2 = (bf16[512,768]{1,0:T(8,128)(2,1)}, bf16[512,768]{1,0:T(8,128)(2,1)S(1)}, u32[]{:S(2)}, u32[]{:S(2)}) collective-permute-start(bf16[512,768]{1,0:T(8,128)(2,1)} %collective-permute-done.1.x2), channel_id=1, source_target_pairs={{0,1},{1,0},{2,3},{3,2},{4,5},{5,4},{6,7},{7,6},{8,9},{9,8},{10,11... | collective-permute-start | bytes 2359304 | tf_op jit(solution)/shard_map/ppermute | solution.py:73
  76.5 36.8 %collective-permute-start.10 = (bf16[384,768]{1,0:T(8,128)(2,1)}, bf16[384,768]{1,0:T(8,128)(2,1)S(1)}, u32[]{:S(2)}, u32[]{:S(2)}) collective-permute-start(bf16[384,768]{1,0:T(8,128)(2,1)} %collective-permute-done.9), channel_id=1, source_target_pairs={{0,1},{1,0},{2,3},{3,2},{4,5},{5,4},{6,7},{7,6},{8,9},{9,8},{10,11... | collective-permute-start | bytes 1769480 | tf_op jit(solution)/shard_map/ppermute | solution.py:73
  78.7 34.6 %copy-start.9 = (bf16[192,768]{1,0:T(8,128)(2,1)S(1)}, bf16[192,768]{1,0:T(8,128)(2,1)}, u32[]{:S(2)}) copy-start(bf16[192,768]{1,0:T(8,128)(2,1)} %copy-done.8) | copy-start | bytes 884740
  78.7 34.6 %copy-start.12 = (bf16[192,768]{1,0:T(8,128)(2,1)S(1)}, bf16[192,768]{1,0:T(8,128)(2,1)}, u32[]{:S(2)}) copy-start(bf16[192,768]{1,0:T(8,128)(2,1)} %param.46) | copy-start | bytes 884740
  78.7 75.7 %collective-permute-start.11 = (bf16[2,784,768]{2,1,0:T(8,128)(2,1)S(1)}, bf16[2,784,768]{2,1,0:T(8,128)(2,1)}, u32[]{:S(2)}, u32[]{:S(2)}) collective-permute-start(bf16[2,784,768]{2,1,0:T(8,128)(2,1)S(1)} %copy-done.4), channel_id=1, source_target_pairs={{0,1},{1,0},{2,3},{3,2},{4,5},{5,4},{6,7},{7,6},{8,9},{9,8},{10,11... | collective-permute-start | bytes 7225352 | tf_op jit(solution)/shard_map/ppermute | solution.py:73
  79.3 47.9 %collective-permute-start.13 = (bf16[784,768]{1,0:T(8,128)(2,1)}, bf16[784,768]{1,0:T(8,128)(2,1)}, u32[]{:S(2)}, u32[]{:S(2)}) collective-permute-start(bf16[784,768]{1,0:T(8,128)(2,1)} %collective-permute-done.12.pack_a), channel_id=1, source_target_pairs={{0,4},{4,0},{8,12},{12,8},{16,20},{20,16},{24,28},{28,24},{1,5},{5... | collective-permute-start | bytes 3612680 | tf_op jit(solution)/shard_map/ppermute | solution.py:729
  112.7 13.9 %collective-permute-start.4 = (bf16[2,512,192]{2,1,0:T(8,128)(2,1)}, bf16[2,512,192]{2,1,0:T(8,128)(2,1)S(1)}, u32[]{:S(2)}, u32[]{:S(2)}) collective-permute-start(bf16[2,512,192]{2,1,0:T(8,128)(2,1)} %get-tuple-element.38), channel_id=1, source_target_pairs={{0,2},{1,3},{2,0},{3,1},{4,6},{5,7},{6,4},{7,5},{8,10},{9,11},{10,... | collective-permute-start | bytes 1179656 | tf_op jit(solution)/shard_map/ppermute | solution.py:73
  114.9 39.5 %collective-permute-start.3 = (bf16[512,192]{1,0:T(8,128)(2,1)S(1)}, bf16[512,192]{1,0:T(8,128)(2,1)S(1)}, u32[]{:S(2)}, u32[]{:S(2)}) collective-permute-start(bf16[512,192]{1,0:T(8,128)(2,1)S(1)} %copy-done.52), channel_id=1, source_target_pairs={{0,1},{1,0},{2,3},{3,2},{4,5},{5,4},{6,7},{7,6},{8,9},{9,8},{10,11... | collective-permute-start | bytes 589832 | tf_op jit(solution)/shard_map/ppermute | solution.py:73
  126.6 27.7 %copy-start.19 = (bf16[2,512,192]{2,1,0:T(8,128)(2,1)}, bf16[2,512,192]{2,1,0:T(8,128)(2,1)S(1)}, u32[]{:S(2)}) copy-start(bf16[2,512,192]{2,1,0:T(8,128)(2,1)S(1)} %collective-permute-done.4.ca23) | copy-start | bytes 1179652
  126.6 27.8 %collective-permute-start.5 = (bf16[512,192]{1,0:T(8,128)(2,1)S(1)}, bf16[512,192]{1,0:T(8,128)(2,1)S(1)}, u32[]{:S(2)}, u32[]{:S(2)}) collective-permute-start(bf16[512,192]{1,0:T(8,128)(2,1)S(1)} %slice_bitcast_fusion.2), channel_id=1, source_target_pairs={{0,1},{1,0},{2,3},{3,2},{4,5},{5,4},{6,7},{7,6},{8,9},{9,8},{10,11... | collective-permute-start | bytes 589832 | tf_op jit(solution)/shard_map/ppermute | solution.py:73
  126.7 27.7 %collective-permute-start.14 = (bf16[784,768]{1,0:T(8,128)(2,1)}, bf16[784,768]{1,0:T(8,128)(2,1)}, u32[]{:S(2)}, u32[]{:S(2)}) collective-permute-start(bf16[784,768]{1,0:T(8,128)(2,1)} %collective-permute-done.12.pack_a), channel_id=1, source_target_pairs={{0,1},{1,0},{2,3},{3,2},{4,5},{5,4},{6,7},{7,6},{8,9},{9,8},{10,11... | collective-permute-start | bytes 3612680 | tf_op jit(solution)/shard_map/ppermute | solution.py:73
  127.2 27.2 %collective-permute-start.15 = (bf16[784,768]{1,0:T(8,128)(2,1)}, bf16[784,768]{1,0:T(8,128)(2,1)}, u32[]{:S(2)}, u32[]{:S(2)}) collective-permute-start(bf16[784,768]{1,0:T(8,128)(2,1)} %collective-permute-done.13.pack_b), channel_id=1, source_target_pairs={{0,1},{1,0},{2,3},{3,2},{4,5},{5,4},{6,7},{7,6},{8,9},{9,8},{10,11... | collective-permute-start | bytes 3612680 | tf_op jit(solution)/shard_map/ppermute | solution.py:73
  261.7 2.1 collective-permute-start.20
  263.9 49.8 %collective-permute-start.21 = (bf16[192,768]{1,0:T(8,128)(2,1)S(1)}, bf16[192,768]{1,0:T(8,128)(2,1)S(1)}, u32[]{:S(2)}, u32[]{:S(2)}) collective-permute-start(bf16[192,768]{1,0:T(8,128)(2,1)S(1)} %fusion.12), channel_id=1, source_target_pairs={{0,2},{1,3},{2,0},{3,1},{4,6},{5,7},{6,4},{7,5},{8,10},{9,11},{10,... | collective-permute-start | bytes 884744 | tf_op jit(solution)/shard_map/ppermute | solution.py:73
  316.0 135.2 %copy-start.49 = (bf16[2,512,768]{2,1,0:T(8,128)(2,1)S(1)}, bf16[2,512,768]{2,1,0:T(8,128)(2,1)}, u32[]{:S(2)}) copy-start(bf16[2,512,768]{2,1,0:T(8,128)(2,1)} %get-tuple-element.51) | copy-start | bytes 4718596
  316.0 135.3 %copy-start.27 = (f32[3,1,384]{2,1,0:T(1,128)S(1)}, f32[3,1,384]{2,1,0:T(1,128)}, u32[]{:S(2)}) copy-start(f32[3,1,384]{2,1,0:T(1,128)} %get-tuple-element.55) | copy-start | bytes 13828
  316.0 135.4 %copy-start.20 = (f32[8,768]{1,0:T(8,128)S(1)}, f32[8,768]{1,0:T(8,128)}, u32[]{:S(2)}) copy-start(f32[8,768]{1,0:T(8,128)} %get-tuple-element.41) | copy-start | bytes 73732
  316.1 135.2 %reduce-scatter.5.cloned.1.call-start = ((), (), s32[]{:S(2)}) async-start(), calls=%async_computation.4 | async-start | bytes 2654208 | tf_op jit(solution)/shard_map/reduce_scatter | solution.py:752
  316.8 203.0 %all-gather.3.cloned.1.call-start = ((), (), s32[]{:S(2)}) async-start(), calls=%async_computation.3 | async-start | bytes 1327104 | tf_op jit(solution)/shard_map/all_gather | solution.py:668
  379.8 167.1 %all-gather.5.cloned.1.call-start = ((), (), s32[]{:S(2)}) async-start(), calls=%async_computation.5 | async-start | bytes 2654208 | tf_op jit(solution)/shard_map/all_gather | solution.py:753
  451.3 3.6 collective-permute-start.18
  451.4 7.7 %collective-permute-start.16 = (f32[7,768]{1,0:T(8,128)S(1)}, f32[7,768]{1,0:T(8,128)S(1)}, u32[]{:S(2)}, u32[]{:S(2)}) collective-permute-start(f32[7,768]{1,0:T(8,128)S(1)} %bitcast.73), channel_id=1, source_target_pairs={{0,1},{1,0},{2,3},{3,2},{4,5},{5,4},{6,7},{7,6},{8,9},{9,8},{10,11... | collective-permute-start | bytes 64520 | tf_op jit(solution)/shard_map/ppermute | solution.py:73
  457.6 58.2 %collective-permute-start.19 = (bf16[512,768]{1,0:T(8,128)(2,1)}, bf16[512,768]{1,0:T(8,128)(2,1)}, u32[]{:S(2)}, u32[]{:S(2)}) collective-permute-start(bf16[512,768]{1,0:T(8,128)(2,1)} %fusion.3), channel_id=1, source_target_pairs={{0,2},{1,3},{2,0},{3,1},{4,6},{5,7},{6,4},{7,5},{8,10},{9,11},{10,... | collective-permute-start | bytes 2359304 | tf_op jit(solution)/shard_map/ppermute | solution.py:73
  459.1 18.8 %collective-permute-start.17 = (f32[7,768]{1,0:T(8,128)S(1)}, f32[7,768]{1,0:T(8,128)S(1)}, u32[]{:S(2)}, u32[]{:S(2)}) collective-permute-start(f32[7,768]{1,0:T(8,128)S(1)} %slice_add_fusion.2), channel_id=1, source_target_pairs={{0,2},{1,3},{2,0},{3,1},{4,6},{5,7},{6,4},{7,5},{8,10},{9,11},{10,... | collective-permute-start | bytes 64520 | tf_op jit(solution)/shard_map/ppermute | solution.py:73
  (49 other events, 224.8 us)
Sparse Core Ops, SparseCore 0:
  316.2 63.5 reduce-scatter.2
  383.2 67.9 reduce-scatter.4
  453.4 40.3 all-gather.2
  495.9 50.8 all-gather.4

commit v3 on v2

--- a/solution.py
+++ b/solution.py
@@ -77,12 +77,6 @@
     far = swap(own, 2)
     near = swap(own, 1)
     return [own, near, far, swap(far, 1)]
-
-
-def reduce_blocks(blocks):
-    near = swap(jnp.stack([blocks[1], blocks[3]]).astype(BF16), 1).astype(F32)
-    far = swap((blocks[2] + near[1]).astype(BF16), 2).astype(F32)
-    return blocks[0] + near[0] + far
 
 
 def sum_small(array):
@@ -250,71 +244,297 @@
     )(base, *blocks, weight, bias, seg_lanes, blocked)
 
 
+def in_pair(place, bit):
+    digit = lax.rem(lax.div(place, bit), 2)
+    return place + bit - 2 * bit * digit, digit
+
+
+def halving_steps(partial, total, landing, rows, landing_row, order, place, copy_of, done=0, base=None):
+    low, size = rows
+    here = low if base is None else base
+    steps, levels, used = [], [], landing_row
+    for level, bit in enumerate(order):
+        partner, digit = in_pair(place, bit)
+        halved = size % 32 == 0
+        count = size // 2 if halved else size
+        low = pl.multiple_of(low + digit * count, 16) if halved else low
+        if level >= done:
+            give = pl.multiple_of(here + (1 - digit) * count, 16) if halved else here
+            here = pl.multiple_of(here + digit * count, 16) if halved else here
+            copy = copy_of(partial.at[pl.ds(give, count)], landing.at[pl.ds(used, count)], partner)
+            last = level == len(order) - 1
+
+            def add(used=used, here=here, count=count, out=total if last else partial, at=low if last else here):
+                arrived = landing[used : used + count, :].astype(F32)
+                mine = partial[pl.ds(here, count), :].astype(F32)
+                out[pl.ds(at, count), :] = (mine + arrived).astype(out.dtype)
+
+            steps.append((copy, add))
+            used += count
+        if halved:
+            levels.append((count, low, partner))
+        size = count
+    for count, keep, partner in reversed(levels):
+        where = total.at[pl.ds(keep, count)]
+        steps.append((copy_of(where, where, partner), lambda: None))
+    return steps, used
+
+
+def run_step(plans, index):
+    for steps in plans:
+        if 0 < index <= len(steps):
+            copy, after = steps[index - 1]
+            copy().wait()
+            after()
+        if index < len(steps):
+            steps[index][0]().start()
+
+
+def split_rows(first, count):
+    large = count * 2 // 3 // 64 * 64
+    return ((first, large), (first + large, count - large))
+
+
+def dp_bits():
+    bits = [1 << i for i in range((lax.axis_size("dp") - 1).bit_length())]
+    return bits, (bits[1:] + bits[:1])
+
+
 def backward_kernel(
-    qkv_ref, ctx_ref, x_ref, w_ref, g0, g1, g2, g3,
-    wg_ref, bg_ref, own_ref, near_ref, far_ref,
-    grads, packed, keys_t, total, *, key_block,
+    qkv_ref, ctx_ref, x_ref, w_ref, g0, g1, g2, g3, ffn_ref, outg_ref, small_ref,
+    ffn_out, late_out, small_out, gx_out, gxfar_out,
+    grads, packed, keys_t, total, ffn_part, ffn, late_in, late, small, small_in, landing, small_land,
+    out_near, out_near_land, out_far, out_far_land, gx_near, gx_near_land, gx_far, gx_far_land,
+    send_sem, recv_sem, *, key_block,
 ):
     blocks = (g0, g1, g2, g3)
     own_rows = g0.shape[0]
     rows = own_rows * len(blocks)
     heads = grads.shape[0]
+    head_cols = heads * HEAD_DIM
     head = pl.program_id(0)
+    group = lax.axis_size("tensor")
+    me, place = lax.axis_index("tensor"), lax.axis_index("dp")
+    near_id = me + 1 - 2 * lax.rem(me, 2)
+    far_id = lax.rem(me + 2, group)
+    part = lambda j: slice(j * own_rows, (j + 1) * own_rows)
+    bits, turned = dp_bits()
+
+    count = [0]
+    sends = []
+
+    def copy_to(source, target, device):
+        index = count[0]
+        count[0] += 1
+
+        def make():
+            return pltpu.make_async_remote_copy(
+                src_ref=source,
+                dst_ref=target,
+                send_sem=send_sem.at[index],
+                recv_sem=recv_sem.at[index],
+                device_id=device,
+                device_id_type=pl.DeviceIdType.MESH,
+            )
+
+        sends.append(make)
+        return make
+
+    over_dp = lambda source, target, other: copy_to(source, target, {"dp": other})
+    over_tensor = lambda source, target, other: copy_to(source, target, {"tensor": other})
+
+    used = [0]
+
+    def reduced(partial, target, first, size, done=0):
+        plans, taken = [], 0
+        for rows_of, order in zip(split_rows(first, size), (bits, turned)):
+            steps, used[0] = halving_steps(
+                partial, target, landing, rows_of, used[0], order, place, over_dp, done,
+                taken if done else None,
+            )
+            plans.append(steps)
+            taken += rows_of[1] // 2
+        return plans
+
+    width = x_ref.shape[1]
+    ffn_plans = reduced(ffn_part, ffn, 0, ffn.shape[0], 1)
+    early_plans = reduced(late_in, late, 0, 2 * head_cols)
+    middle_plans = reduced(late_in, late, 2 * head_cols, head_cols)
+    last_plans = reduced(late_in, late, 3 * head_cols, head_cols)
+    small_steps = []
+    for level, bit in enumerate(bits):
+        partner, _ = in_pair(place, bit)
+        small_steps.append(over_dp(small_in.at[level], small_land.at[level], partner))
+    tensor_small = [
+        over_tensor(small.at[0], small.at[1], near_id),
+        over_tensor(small.at[2], small.at[3], far_id),
+    ]
+    out_steps = [
+        over_tensor(out_near, out_near_land, near_id),
+        over_tensor(out_far, out_far_land, far_id),
+    ]
+    gx_steps = [
+        over_tensor(gx_near, gx_near_land, near_id),
+        over_tensor(gx_far, gx_far_land, far_id),
+    ]
 
     @pl.when(head == 0)
     def _():
+        barrier = pltpu.get_barrier_semaphore()
+        others = [{"tensor": near_id}, {"tensor": far_id}]
+        others += [{"dp": in_pair(place, bit)[0]} for bit in bits]
+        for other in others:
+            pl.semaphore_signal(
+                barrier, inc=1, device_id=other, device_id_type=pl.DeviceIdType.MESH
+            )
+        pl.semaphore_wait(barrier, len(others))
+        ffn_part[...] = ffn_ref[...]
+        run_step(ffn_plans, 0)
+        out_near[0] = outg_ref[1]
+        out_near[1] = outg_ref[3]
+        out_steps[0]().start()
+        small[0] = small_ref[...]
+        tensor_small[0]().start()
         for h in range(heads):
             for j, block in enumerate(blocks):
-                part = slice(j * own_rows, (j + 1) * own_rows)
                 one = block[:, h * HEAD_DIM : (h + 1) * HEAD_DIM].astype(F32)
-                grads[h, part, :] = jnp.concatenate([one, jnp.zeros_like(one)], axis=1).astype(BF16)
+                grads[h, part(j), :] = jnp.concatenate(
+                    [one, jnp.zeros_like(one)], axis=1
+                ).astype(BF16)
         packed[...] = jnp.zeros_like(packed)
 
     queries = qkv_ref[:, :LANES]
     slopes = grads[head]
-    inner = -jnp.sum(
-        slopes[:, :HEAD_DIM].astype(F32) * ctx_ref[0], axis=1, keepdims=True
-    )
+    inner = -jnp.sum(slopes[:, :HEAD_DIM].astype(F32) * ctx_ref[0], axis=1, keepdims=True)
     slopes = slopes + in_lane((rows, LANES), 1, split_three(inner)).astype(BF16)
     keys_t[...] = qkv_ref[:, LANES : 2 * LANES].T
-    query_grad = None
-    for start in range(0, rows, key_block):
-        part = slice(start, start + key_block)
-        weights = jnp.exp(dot_cols(qkv_ref[part, LANES : 2 * LANES], queries))
-        grad_weights = dot_cols(qkv_ref[part, 2 * LANES :], slopes)
-        grad_scores = (weights * grad_weights).astype(BF16)
-        step = dot(keys_t[:, part], grad_scores)
-        query_grad = step if query_grad is None else query_grad + step
-        key_grad = dot(grad_scores, queries)[:, :HEAD_DIM]
-        packed[part, LANES : LANES + HEAD_DIM] = key_grad.astype(BF16)
-        value_grad = dot(weights.astype(BF16), slopes)[:, :HEAD_DIM]
-        packed[part, 2 * LANES : 2 * LANES + HEAD_DIM] = value_grad.astype(BF16)
+
+    def over_keys(first, last, query_grad):
+        for start in range(first, last, key_block):
+            span = slice(start, start + key_block)
+            weights = jnp.exp(dot_cols(qkv_ref[span, LANES : 2 * LANES], queries))
+            grad_weights = dot_cols(qkv_ref[span, 2 * LANES :], slopes)
+            grad_scores = (weights * grad_weights).astype(BF16)
+            step = dot(keys_t[:, span], grad_scores)
+            query_grad = step if query_grad is None else query_grad + step
+            key_grad = dot(grad_scores, queries)[:, :HEAD_DIM]
+            packed[span, LANES : LANES + HEAD_DIM] = key_grad.astype(BF16)
+            value_grad = dot(weights.astype(BF16), slopes)[:, :HEAD_DIM]
+            packed[span, 2 * LANES : 2 * LANES + HEAD_DIM] = value_grad.astype(BF16)
+        return query_grad
+
+    query_grad = over_keys(0, rows // 2, None)
+
+    @pl.when(head == 0)
+    def _():
+        out_steps[0]().wait_recv()
+        out_far[...] = (outg_ref[2].astype(F32) + out_near_land[1].astype(F32)).astype(BF16)
+        out_steps[1]().start()
+        tensor_small[0]().wait_recv()
+        small[2] = small[0] + small[1]
+        tensor_small[1]().start()
+
+    @pl.when(head == 1)
+    def _():
+        run_step(ffn_plans, 2)
+        run_step(early_plans, 1)
+
+    @pl.when(head == 2)
+    def _():
+        run_step(ffn_plans, 4)
+        run_step(early_plans, 3)
+        run_step(middle_plans, 1)
+
+    query_grad = over_keys(rows // 2, rows, query_grad)
     packed[:, :HEAD_DIM] = query_grad[:HEAD_DIM].T.astype(BF16)
-    bg_ref[0] = jnp.sum(packed[...].astype(F32), axis=0, keepdims=True)
+    sums = jnp.sum(packed[...].astype(F32), axis=0, keepdims=True)
+    small[4 + head, 0:1, : 3 * LANES] = sums
     weight_grad = dot_rows(packed[...], x_ref[...])
+    slot = jnp.where(head == 0, 0, head_cols + head * head_cols)
     for c, factor in enumerate((0.125, 1.0, 1.0)):
-        wg_ref[0, c * HEAD_DIM : (c + 1) * HEAD_DIM, :] = (
+        target = pl.multiple_of(slot + c * HEAD_DIM, HEAD_DIM)
+        late_in[pl.ds(target, HEAD_DIM), :] = (
             weight_grad[c * LANES : c * LANES + HEAD_DIM] * factor
         ).astype(BF16)
-    for j in range(len(blocks)):
-        part = slice(j * own_rows, (j + 1) * own_rows)
-        step = dot_cols(packed[part, :], w_ref[0])
-        total[part, :] = jnp.where(head == 0, step, total[part, :] + step)
-
-    @pl.when(head == pl.num_programs(0) - 1)
+
+    @pl.when(head == 0)
     def _():
-        part = lambda j: slice(j * own_rows, (j + 1) * own_rows)
-        own_ref[...] = total[part(0), :]
-        far_ref[...] = total[part(2), :]
-        near_ref[0] = total[part(1), :].astype(BF16)
-        near_ref[1] = total[part(3), :].astype(BF16)
-
-
-def attend_backward(qkv, context, source, weight, blocks):
+        out_steps[1]().wait_recv()
+        late_in[head_cols : 2 * head_cols, :] = (
+            outg_ref[0].astype(F32)
+            + out_near_land[0].astype(F32)
+            + out_far_land[...].astype(F32)
+        ).astype(BF16)
+        tensor_small[1]().wait_recv()
+        run_step(ffn_plans, 1)
+        run_step(early_plans, 0)
+
+    @pl.when(head == 1)
+    def _():
+        run_step(middle_plans, 0)
+        run_step(ffn_plans, 3)
+        run_step(early_plans, 2)
+
+    @pl.when(head == 2)
+    def _():
+        run_step(last_plans, 0)
+        small_in[0, :8, :] = small[2] + small[3]
+        small_in[0, UP_ROW : UP_ROW + 1, :] = small_ref[UP_ROW : UP_ROW + 1, :]
+        small_in[0, 8:, :] = jnp.zeros((8, width), F32)
+        for h in range(heads):
+            small_in[0, 8 + h : 9 + h, : 3 * LANES] = small[4 + h, 0:1, : 3 * LANES]
+        small_steps[0]().start()
+
+    for j in (1, 3, 2, 0):
+        step = dot_cols(packed[part(j), :], w_ref[0])
+        total[part(j), :] = jnp.where(head == 0, step, total[part(j), :] + step)
+
+    @pl.when(head == heads - 1)
+    def _():
+        gx_near[0] = total[part(1), :].astype(BF16)
+        gx_near[1] = total[part(3), :].astype(BF16)
+        gx_steps[0]().start()
+        run_step(ffn_plans, 5)
+        run_step(early_plans, 4)
+        run_step(middle_plans, 2)
+        run_step(last_plans, 1)
+        gx_steps[0]().wait_recv()
+        gx_far[...] = (total[part(2), :] + gx_near_land[1].astype(F32)).astype(BF16)
+        gx_steps[1]().start()
+        gx_out[...] = total[part(0), :] + gx_near_land[0].astype(F32)
+        for index in range(1, 2 * len(bits) + 1):
+            if index > 1:
+                run_step(last_plans, index)
+            if index <= len(bits):
+                small_steps[index - 1]().wait_recv()
+                arrived = small_in[index - 1] + small_land[index - 1]
+                if index < len(bits):
+                    small_in[index] = arrived
+                    small_steps[index]().start()
+                else:
+                    small_out[...] = arrived
+            run_step(middle_plans, 2 + index)
+            run_step(early_plans, 4 + index)
+            run_step(ffn_plans, 5 + index)
+        ffn_out[...] = ffn[...]
+        late_out[...] = late[...]
+        gx_steps[1]().wait_recv()
+        gxfar_out[...] = gx_far_land[...]
+        shared = small[2, LOSS_ROW : LOSS_ROW + 1, :] + small[3, LOSS_ROW : LOSS_ROW + 1, :]
+        small_out[LOSS_ROW : LOSS_ROW + 1, :] = shared
+        for copy in small_steps + tensor_small + out_steps + gx_steps:
+            copy().wait_send()
+
+
+def attend_backward(qkv, context, source, weight, blocks, ffn_grads, out_grads, small):
     rows, width = source.shape
     own_rows, head_cols = blocks[0].shape
     cols = 3 * LANES
     heads = weight.shape[0]
+    levels = (lax.axis_size("dp") - 1).bit_length()
+    ffn_rows, late_rows = 2 * ffn_grads.shape[0], (heads + 1) * head_cols
+    landing = ffn_rows + late_rows + 8 * 48 * levels
+    transfers = 2 * 4 * 2 * levels + levels + 6
     array = jax.ShapeDtypeStruct
     whole = lambda *shape: pl.BlockSpec(shape, lambda h: (0,) * len(shape))
     head_block = lambda *shape: pl.BlockSpec((1,) + shape, lambda h: (h, 0, 0))
@@ -327,35 +547,56 @@
             whole(rows, width),
             head_block(width, cols),
         ]
-        + [whole(own_rows, head_cols)] * 4,
+        + [whole(own_rows, head_cols)] * 4
+        + [whole(*ffn_grads.shape), whole(*out_grads.shape), whole(*small.shape)],
         out_specs=[
-            head_block(3 * HEAD_DIM, width),
-            head_block(1, cols),
+            whole(ffn_rows, width),
+            whole(late_rows, width),
+            whole(16, width),
             whole(own_rows, width),
-            whole(2, own_rows, width),
             whole(own_rows, width),
         ],
         out_shape=[
-            array((heads, 3 * HEAD_DIM, width), BF16),
-            array((heads, 1, cols), F32),
+            array((ffn_rows, width), BF16),
+            array((late_rows, width), BF16),
+            array((16, width), F32),
             array((own_rows, width), F32),
-            array((2, own_rows, width), BF16),
-            array((own_rows, width), F32),
+            array((own_rows, width), BF16),
         ],
         scratch_shapes=[
             pltpu.VMEM((heads, rows, LANES), BF16),
             pltpu.VMEM((rows, cols), BF16),
             pltpu.VMEM((LANES, rows), BF16),
             pltpu.VMEM((rows, width), F32),
+            pltpu.VMEM((ffn_rows // 2, width), BF16),
+            pltpu.VMEM((ffn_rows, width), BF16),
+            pltpu.VMEM((late_rows, width), BF16),
+            pltpu.VMEM((late_rows, width), BF16),
+            pltpu.VMEM((4 + heads, 8, width), F32),
+            pltpu.VMEM((levels, 16, width), F32),
+            pltpu.VMEM((landing, width), BF16),
+            pltpu.VMEM((levels, 16, width), F32),
+            pltpu.VMEM((2, head_cols, width), BF16),
+            pltpu.VMEM((2, head_cols, width), BF16),
+            pltpu.VMEM((head_cols, width), BF16),
+            pltpu.VMEM((head_cols, width), BF16),
+            pltpu.VMEM((2, own_rows, width), BF16),
+            pltpu.VMEM((2, own_rows, width), BF16),
+            pltpu.VMEM((own_rows, width), BF16),
+            pltpu.VMEM((own_rows, width), BF16),
+            pltpu.SemaphoreType.DMA((transfers,)),
+            pltpu.SemaphoreType.DMA((transfers,)),
         ],
-        compiler_params=pltpu.CompilerParams(vmem_limit_bytes=58 * 2**20),
+        compiler_params=pltpu.CompilerParams(
+            collective_id=4, has_side_effects=True, vmem_limit_bytes=62 * 2**20
+        ),
         cost_estimate=pl.CostEstimate(
-            flops=40 * heads * rows * rows * HEAD_DIM,
+            flops=60 * heads * rows * rows * HEAD_DIM,
             bytes_accessed=2 * rows * heads * (cols + 7 * LANES),
             transcendentals=heads * rows * rows,
         ),
         name="attention_backward",
-    )(qkv, context, source, weight, *blocks)
+    )(qkv, context, source, weight, *blocks, ffn_grads, out_grads, small)
 
 
 (OUT_BIAS, GAIN_1, SHIFT_1, DOWN_BIAS, GAIN_2, SHIFT_2, UP_BIAS) = range(7)
@@ -366,9 +607,9 @@
 def middle_kernel(
     x_ref, ca0, ca1, ca23, ca3, tc_ref, w_out, tw_out, w_up, w_down, vec,
     pack_own, pack_near, pack_a, pack_b, pack_c, pack_d,
-    out_ref, gh_ref, ffn_ref, outg_ref, g0_ref, g1_ref, g2_ref, g3_ref, small_ref,
+    out_ref, gh_ref, kept_ref, outg_ref, g0_ref, g1_ref, g2_ref, g3_ref, small_ref,
     tc1, tc2, tcf, tc3, y_all, g_all, slope, hid, gu_all, t_out, first, normed, two, inv,
-    part0, part2, send1, send2, send3, near0, near2, far0, gs, gr, packs,
+    part0, part2, send1, send2, send3, near0, near2, far0, gs, gr, packs, ffn_ref, ffn_land,
     send_sem, recv_sem, pack_sem,
 ):
     me = lax.axis_index("tensor")
@@ -383,17 +624,19 @@
     group = lambda j: slice(j * head_cols, (j + 1) * head_cols)
     row = lambda index: vec[index : index + 1, :]
 
+    place = lax.axis_index("dp")
+    first_bits = [order[0] for order in dp_bits()]
+    others = [{"tensor": near_id}, {"tensor": far_id}]
+    others += [{"dp": in_pair(place, bit)[0]} for bit in first_bits]
     barrier = pltpu.get_barrier_semaphore()
-    for other in (near_id, far_id):
-        pl.semaphore_signal(
-            barrier, inc=1, device_id={"tensor": other}, device_id_type=pl.DeviceIdType.MESH
-        )
-    pl.semaphore_wait(barrier, 2)
+    for other in others:
+        pl.semaphore_signal(barrier, inc=1, device_id=other, device_id_type=pl.DeviceIdType.MESH)
+    pl.semaphore_wait(barrier, len(others))
 
     count = [0]
     started = []
 
-    def put(source, target, device):
+    def put(source, target, device, axis="tensor"):
         index = count[0]
         count[0] += 1
         copy = pltpu.make_async_remote_copy(
@@ -401,7 +644,7 @@
             dst_ref=target,
             send_sem=send_sem.at[index],
             recv_sem=recv_sem.at[index],
-            device_id={"tensor": device},
+            device_id={axis: device},
             device_id_type=pl.DeviceIdType.MESH,
         )
         copy.start()
@@ -556,6 +799,15 @@
     flat = lambda block: block[...].reshape(4 * own_rows, block.shape[2])
     ffn_ref[:width, :] = dot_rows(flat(y_all), flat(gu_all)).astype(BF16)
     ffn_ref[width:, :] = dot_rows(flat(hid), flat(g_all)).astype(BF16)
+    halves, taken = [], 0
+    for (low, size), bit in zip(split_rows(0, width + hidden), first_bits):
+        partner, digit = in_pair(place, bit)
+        size = size // 2
+        give = ffn_ref.at[pl.ds(pl.multiple_of(low + (1 - digit) * size, 16), size)]
+        keep = pl.multiple_of(low + digit * size, 16)
+        land = slice(taken, taken + size)
+        halves.append((put(give, ffn_land.at[land], partner, "dp"), keep, land))
+        taken += size
 
     passes = []
     for c, (rows, near, far) in enumerate(zip(chunks, g_near, g_far)):
@@ -598,6 +850,10 @@
         g2_ref[rows, :] = gr[1, rows, :]
         last.wait_recv()
         g3_ref[rows, :] = gr[2, rows, :]
+    for copy, keep, land in halves:
+        copy.wait_recv()
+        mine = ffn_ref[pl.ds(keep, land.stop - land.start), :].astype(F32)
+        kept_ref[land, :] = (mine + ffn_land[land, :].astype(F32)).astype(BF16)
     for copy in started:
         copy.wait_send()
 
@@ -608,7 +864,7 @@
     head_cols = cas[0].shape[1]
     array = jax.ShapeDtypeStruct
     vmem = pl.BlockSpec(memory_space=pltpu.VMEM)
-    transfers = 4 + 4 * 3 * CHUNKS + 4 * CHUNKS
+    transfers = 4 + 4 * 3 * CHUNKS + 4 * CHUNKS + 2
     square = lambda kind: pltpu.VMEM((own_rows, width), kind)
     four = lambda cols, kind: pltpu.VMEM((4, own_rows, cols), kind)
     return pl.pallas_call(
@@ -618,7 +874,7 @@
         out_shape=[
             array((own_rows, width), BF16),
             array((own_rows, width), F32),
-            array((width + hidden, width), BF16),
+            array(((width + hidden) // 2, width), BF16),
             array((4, head_cols, width), BF16),
         ]
         + [array((own_rows, head_cols), BF16)] * 4
@@ -633,6 +889,8 @@
         + [four(head_cols, BF16), four(head_cols, BF16)]
         + [
             pltpu.VMEM((2,) + packs[2].shape, BF16),
+            pltpu.VMEM((width + hidden, width), BF16),
+            pltpu.VMEM(((width + hidden) // 2, width), BF16),
             pltpu.SemaphoreType.DMA((transfers,)),
             pltpu.SemaphoreType.DMA((transfers,)),
             pltpu.SemaphoreType.DMA((2,)),
@@ -661,11 +919,6 @@
         weight.reshape(heads, width, 3 * LANES).astype(BF16),
         full.reshape(heads, 1, 3 * LANES),
     )
-
-
-def reduce_dp(array):
-    share = lax.psum_scatter(array.astype(BF16), "dp", scatter_dimension=0, tiled=True)
-    return lax.all_gather(share, "dp", axis=0, tiled=True).astype(F32)
 
 
 def body(
@@ -749,54 +1002,36 @@
     out_own, grad_h, ffn_grads, out_grads, g0, g1, g2, g3, small = middle(
         tokens, cas, t_context, w_out_all, t_out_all, w_up, w_down, vectors, packs
     )
-    ffn_share = lax.psum_scatter(ffn_grads, "dp", scatter_dimension=0, tiled=True)
-    ffn_grads = lax.all_gather(ffn_share, "dp", axis=0, tiled=True).astype(F32)
-
-    weight_grad, proj_bias_grad, gx_own, gx_near, gx_far = attend_backward(
-        qkv, context, x_in_all, wide_qkv, [g0, g1, g2, g3]
+    ffn_grads, late, small, gx_own, gx_far = attend_backward(
+        qkv, context, x_in_all, wide_qkv, [g0, g1, g2, g3], ffn_grads, out_grads, small
     )
-    out_grad = reduce_blocks([out_grads[j].astype(F32) for j in range(group)])
-    gx_near = swap(gx_near, 1).astype(F32)
-    gx_far = swap((gx_far + gx_near[1]).astype(BF16), 2).astype(F32)
-    grad_x_in = gx_own + gx_near[0] + gx_far
+    grad_x_in = gx_own + gx_far.astype(F32)
     input_grad = grad_h + grad_x_in * clip_slope(tokens.astype(F32))
-
-    shared = sum_small(small[:7])
-    tree_loss = jnp.sum(shared[6])[None] / (all_rows * model_width)
-    proj_bias_grad = proj_bias_grad.reshape(local_heads, 3, LANES)[:, :, :HEAD_DIM]
-    proj_bias_grad = proj_bias_grad.transpose(1, 0, 2).reshape(3, local_cols)
-    small = jnp.concatenate(
-        [
-            shared[:6].reshape(-1),
-            small[7],
-            proj_bias_grad[0] * 0.125,
-            proj_bias_grad[2],
-        ]
-    )
-    small = lax.psum(small, "dp")
-    shared = small[: 6 * model_width].reshape(6, model_width)
-    late = reduce_dp(
-        jnp.concatenate([weight_grad.reshape(-1, model_width).astype(F32), out_grad])
-    )
-    qkv_rows = 3 * local_cols
-    qkv_grad = late[:qkv_rows].reshape(local_heads, 3, HEAD_DIM, model_width)
+    ffn_grads = ffn_grads.astype(F32)
+    tree_loss = jnp.sum(small[LOSS_ROW])[None] / (all_rows * model_width)
+    proj_bias_grad = small[8 : 8 + local_heads, : 3 * LANES].reshape(local_heads, 3, LANES)
+    proj_bias_grad = proj_bias_grad[:, :, :HEAD_DIM].transpose(1, 0, 2).reshape(3, local_cols)
+    proj_bias_grad = jnp.stack([proj_bias_grad[0] * 0.125, proj_bias_grad[2]])
+    late = late.astype(F32)
+    qkv_grad = jnp.concatenate([late[:local_cols], late[2 * local_cols :]])
+    qkv_grad = qkv_grad.reshape(local_heads, 3, HEAD_DIM, model_width)
     qkv_grad = qkv_grad.transpose(3, 1, 0, 2).reshape(model_width, 3, local_cols)
     return (
         out_own,
         tree_loss,
         input_grad,
         qkv_grad,
-        small[6 * model_width + hid :].reshape(2, local_cols),
-        late[qkv_rows:],
-        shared[0],
-        shared[1],
-        shared[2],
+        proj_bias_grad,
+        late[local_cols : 2 * local_cols],
+        small[0],
+        small[1],
+        small[2],
         ffn_grads[:model_width],
-        small[6 * model_width : 6 * model_width + hid],
+        small[7],
         ffn_grads[model_width:],
-        shared[3],
-        shared[4],
-        shared[5],
+        small[3],
+        small[4],
+        small[5],
     )
 
 

time: 566 us -> 372 us (0.66)
  waiting for transfers between devices: 219 us -> 37.9 us
  Pallas kernels: 212 us -> 266 us
  blocking collectives: 35.3 us -> 0 us
  between operations: 16.9 us -> 3.36 us
  local copies, waits for them, and re-layouts: 35.2 us -> 26.8 us
  other arithmetic: 28 us -> 22.1 us
    reduce_scatter x2 -> x0, waiting for transfers between devices: 134 us -> none  [the longest x1 71.4 us: body(): lax.psum_scatter(ffn_grads, 'dp', scatter_dimension=0, tiled=True)]
    pallas_call x1, Pallas kernels: 48.2 us -> 101 us  [attend_backward(): pl.pallas_call(functools.partial(backward_kernel, key_block=256), grid=(h...]
    psum x1 -> x0, blocking collectives: 35.3 us -> none  [body(): small = lax.psum(small, 'dp')]
    all_gather x2 -> x0, waiting for transfers between devices: 23 us -> none  [the longest x1 23 us: body(): ffn_grads = lax.all_gather(ffn_share, 'dp', axis=0, tiled=True).astype(F32)]
    ppermute x21 -> x15, waiting for transfers between devices: 60.8 us -> 37.9 us  [swap(): return lax.ppermute(array, 'tensor', [(i, i ^ bit) for i in range(size)])]
    ppermute x21 -> x15, starting transfers between devices: 12.4 us -> 8.65 us  [swap(): return lax.ppermute(array, 'tensor', [(i, i ^ bit) for i in range(size)])]
  transfers between devices with their start and end apart: 26 -> 16, of which waited for: 9 -> 3; matrix products, arithmetic and copies ran while one was open for 9% -> 9% of each run, Pallas kernels for 19% -> 16%
where the time goes in v3:
time: 372 us; the launch traced here: 366 us
  Pallas kernels  266 us (72%)
  waiting for transfers between devices  37.9 us (10%)
  local copies, waits for them, and re-layouts  26.8 us (7%)
  other arithmetic  22.1 us (6%)
  starting transfers between devices  10.1 us (3%)
    pallas_call x1, Pallas kernels, middle(): pl.pallas_call(middle_kernel, in_specs=[vmem] * 11 + [pl.BlockSpec(memory...  107 us
    pallas_call x1, Pallas kernels, attend_backward(): pl.pallas_call(functools.partial(backward_kernel, key_block=256), grid=(h...  101 us
    pallas_call x2, Pallas kernels, attend_forward(): pl.pallas_call(functools.partial(forward_kernel, student=student), grid=(...  58.1 us
    ppermute x15, waiting for transfers between devices, swap(): return lax.ppermute(array, 'tensor', [(i, i ^ bit) for i in range(size)])  37.9 us
    ppermute x15, starting transfers between devices, swap(): return lax.ppermute(array, 'tensor', [(i, i ^ bit) for i in range(size)])  8.65 us
  transfers between devices with their start and end apart: 16, of which 3 were waited for; matrix products, arithmetic and copies ran while one was open for 9% of the time, Pallas kernels for 16%

profile of v3, /device:TPU:0, one launch (start us, length us, event | category | flops | bytes accessed | tf_op | source)
XLA Modules:
  0.0 365.8 jit_solution(3822670087138707096)
XLA Ops:
  0.7 3.0 collective-permute-start.1
  3.7 1.1 abs_reduce_fusion.3
  4.9 2.1 abs_reduce_fusion.1
  8.4 1.8 abs_reduce_fusion.2
  11.0 1.7 multiply_convert_fusion.1.w_up
  12.7 2.4 copy.70
  15.2 1.1 multiply_bitcast_fusion
  18.4 3.5 collective-permute-done.7
  22.0 1.2 multiply_convert_fusion.3
  23.4 1.1 dynamic-slice_bitcast_fusion
  24.5 1.4 collective-permute-start.12
  30.9 1.2 copy.75
  32.3 2.2 copy.69.w_ref
  34.6 1.4 pad.36.clone
  35.9 4.0 %copy.65.w_ref = bf16[3,768,384]{2,1,0:T(8,128)(2,1)} copy(bf16[3,768,384]{1,2,0:T(8,128)(2,1)} %bitcast.36) | data formatting | bytes 3538944 | tf_op jit(solution)/shard_map/reshape | solution.py:919
  40.4 1.6 multiply_convert_fusion.w_down
  42.1 23.2 %collective-permute-done.9 = bf16[384,768]{1,0:T(8,128)(2,1)} collective-permute-done((bf16[384,768]{1,0:T(8,128)(2,1)}, bf16[384,768]{1,0:T(8,128)(2,1)}, u32[]{:S(2)}, u32[]{:S(2)}) %collective-permute-start.9) | collective-permute-done | bytes 589856 | tf_op jit(solution)/shard_map/ppermute | solution.py:73
  65.3 1.1 fusion.14
  67.0 1.5 collective-permute-start.13
  68.5 31.0 %student_attention.1 = (bf16[2048,1152]{1,0:T(8,128)(2,1)}, f32[3,2048,64]{2,1,0:T(8,128)}, bf16[2048,768]{1,0:T(8,128)(2,1)}, bf16[512,192]{1,0:T(8,128)(2,1)},...) custom-call(s32[4]{0:T(128)} %pad_add_fusion.1.base_ref, bf16[512,768]{1,0:T(8,128)(2,1)} %x_ref.1, ...), custom_call_target="tpu_custom_call" | custom-call | flops 12884901888 | bytes 12582912 | tf_op jit(solution)/shard_map/student_attention/pallas_call | solution.py:223
  99.5 1.1 collective-permute-start.4
  100.7 1.6 pad_maximum_fusion.1
  102.3 11.1 %collective-permute-done.4.ca23 = bf16[2,512,192]{2,1,0:T(8,128)(2,1)S(1)} collective-permute-done((bf16[2,512,192]{2,1,0:T(8,128)(2,1)}, bf16[2,512,192]{2,1,0:T(8,128)(2,1)S(1)}, u32[]{:S(2)}, u32[]{:S(2)}) %collective-permute-start.4) | collective-permute-done | bytes 393248 | tf_op jit(solution)/shard_map/ppermute | solution.py:73
  114.1 27.1 %teacher_attention.1.tc_ref = bf16[4,512,192]{2,1,0:T(8,128)(2,1)} custom-call(s32[4]{0:T(128)} %pad_add_fusion.1.base_ref, bf16[512,768]{1,0:T(8,128)(2,1)} %x_ref.1, bf16[512,768]{1,0:T(8,128)(2,1)} %collective-permute-done.x1, bf16[512,768]{1,0:T(8,128)(2,1)} %collective-permute-done.1.x2, bf16[512,768]{1,0:T(8,128)(2,1)} %collective-permute-done.2.x3, ...), custom_call_target="tpu_custom_call" | custom-call | flops 12884901888 | bytes 12582912 | tf_op jit(solution)/shard_map/teacher_attention/pallas_call | solution.py:223
  142.1 106.7 %middle.1 = (bf16[512,768]{1,0:T(8,128)(2,1)}, f32[512,768]{1,0:T(8,128)}, bf16[768,768]{1,0:T(8,128)(2,1)}, bf16[4,192,768]{2,1,0:T(8,128)(2,1)}, bf16[512,192]...) custom-call(bf16[512,768]{1,0:T(8,128)(2,1)} %x_ref.1, ...), custom_call_target="tpu_custom_call" | custom-call | flops 36238786560 | bytes 33554432 | tf_op jit(solution)/shard_map/middle/pallas_call | solution.py:870
  248.8 100.7 %attention_backward.1 = (bf16[1536,768]{1,0:T(8,128)(2,1)}, bf16[768,768]{1,0:T(8,128)(2,1)}, f32[16,768]{1,0:T(8,128)}, f32[512,768]{1,0:T(8,128)}, bf16[512,768]{1,0:T(8,128)(2,1)}) custom-call(bf16[2048,1152]{1,0:T(8,128)(2,1)} %get-tuple-element.41.qkv_ref, f32[3,2048,64]{2,1,0:T(8,128)} %get-tuple-element.42.ctx_ref, ...), custom_call_target="tpu_custom_call" | custom-call | flops 48318382080 | bytes 15728640 | tf_op jit(solution)/shard_map/attention_backward/pallas_call | solution.py:541
  350.3 1.7 slice_reduce_fusion
  352.0 1.1 slice.135
  354.4 1.3 copy.73
  355.7 1.0 copy-done.2
  356.7 2.6 fusion.11
  360.6 3.0 multiply_add_fusion
  (166 shorter events, 15.5 us)
Async XLA Ops:
  0.6 6.9 %copy-start.39 = (s32[1,13]{1,0:T(1,128)S(1)}, s32[1,13]{1,0:T(1,128)}, u32[]{:S(2)}) copy-start(s32[1,13]{1,0:T(1,128)} %param.30) | copy-start | bytes 160
  0.7 7.0 %copy-start.34 = (s32[1,13]{1,0:T(1,128)S(1)}, s32[1,13]{1,0:T(1,128)}, u32[]{:S(2)}) copy-start(s32[1,13]{1,0:T(1,128)} %param.31) | copy-start | bytes 160
  0.7 7.2 %copy-start.18 = (bf16[2,192]{1,0:T(2,128)(2,1)S(1)}, bf16[2,192]{1,0:T(2,128)(2,1)}, u32[]{:S(2)}) copy-start(bf16[2,192]{1,0:T(2,128)(2,1)} %param.33) | copy-start | bytes 2308
  0.7 7.3 %copy-start.19 = (bf16[2,192]{1,0:T(2,128)(2,1)S(1)}, bf16[2,192]{1,0:T(2,128)(2,1)}, u32[]{:S(2)}) copy-start(bf16[2,192]{1,0:T(2,128)(2,1)} %param.45) | copy-start | bytes 2308
  0.7 7.6 %copy-start.20 = (bf16[768]{0:T(1024)(128)(2,1)S(1)}, bf16[768]{0:T(1024)(128)(2,1)}, u32[]{:S(2)}) copy-start(bf16[768]{0:T(1024)(128)(2,1)} %param.51) | copy-start | bytes 4612
  0.7 22.7 %collective-permute-start.1 = (bf16[512,768]{1,0:T(8,128)(2,1)}, bf16[512,768]{1,0:T(8,128)(2,1)}, u32[]{:S(2)}, u32[]{:S(2)}) collective-permute-start(bf16[512,768]{1,0:T(8,128)(2,1)} %x_ref.1), channel_id=1, source_target_pairs={{0,2},{1,3},{2,0},{3,1},{4,6},{5,7},{6,4},{7,5},{8,10},{9,11},{10,... | collective-permute-start | bytes 2359304 | tf_op jit(solution)/shard_map/ppermute | solution.py:73
  3.7 64.8 %collective-permute-start = (bf16[512,768]{1,0:T(8,128)(2,1)}, bf16[512,768]{1,0:T(8,128)(2,1)}, u32[]{:S(2)}, u32[]{:S(2)}) collective-permute-start(bf16[512,768]{1,0:T(8,128)(2,1)} %x_ref.1), channel_id=1, source_target_pairs={{0,1},{1,0},{2,3},{3,2},{4,5},{5,4},{6,7},{7,6},{8,9},{9,8},{10,11... | collective-permute-start | bytes 2359304 | tf_op jit(solution)/shard_map/ppermute | solution.py:73
  4.9 5.3 %copy-start = (f32[768,768]{1,0:T(8,128)S(1)}, f32[768,768]{1,0:T(8,128)}, u32[]{:S(2)}) copy-start(f32[768,768]{1,0:T(8,128)} %param.38) | copy-start | bytes 7077892
  7.0 11.3 %collective-permute-start.6 = (f32[2,768]{1,0:T(2,128)S(1)}, f32[2,768]{1,0:T(2,128)S(1)}, u32[]{:S(2)}, u32[]{:S(2)}) collective-permute-start(f32[2,768]{1,0:T(2,128)S(1)} %pad_maximum_fusion.4), channel_id=1, source_target_pairs={{0,1},{1,0},{2,3},{3,2},{4,5},{5,4},{6,7},{7,6},{8,9},{9,8},{10,11... | collective-permute-start | bytes 18440 | tf_op jit(solution)/shard_map/ppermute | solution.py:73
  17.3 9.5 %copy-start.4 = (bf16[2,784,768]{2,1,0:T(8,128)(2,1)}, bf16[2,784,768]{2,1,0:T(8,128)(2,1)S(1)}, u32[]{:S(2)}) copy-start(bf16[2,784,768]{2,1,0:T(8,128)(2,1)S(1)} %fusion.1.pack_own) | copy-start | bytes 7225348
  18.3 3.7 %collective-permute-start.7 = (f32[2,768]{1,0:T(2,128)S(1)}, f32[2,768]{1,0:T(2,128)S(1)}, u32[]{:S(2)}, u32[]{:S(2)}) collective-permute-start(f32[2,768]{1,0:T(2,128)S(1)} %fusion.10), channel_id=1, source_target_pairs={{0,2},{1,3},{2,0},{3,1},{4,6},{5,7},{6,4},{7,5},{8,10},{9,11},{10,... | collective-permute-start | bytes 18440 | tf_op jit(solution)/shard_map/ppermute | solution.py:73
  18.4 7.6 %copy-start.12 = (bf16[192,768]{1,0:T(8,128)(2,1)S(1)}, bf16[192,768]{1,0:T(8,128)(2,1)}, u32[]{:S(2)}) copy-start(bf16[192,768]{1,0:T(8,128)(2,1)} %param.46) | copy-start | bytes 884740
  23.4 4.3 %copy-start.31 = (bf16[768]{0:T(1024)(128)(2,1)S(1)}, bf16[768]{0:T(1024)(128)(2,1)}, u32[]{:S(2)}) copy-start(bf16[768]{0:T(1024)(128)(2,1)} %param.53) | copy-start | bytes 4612
  23.4 4.3 %copy-start.32 = (bf16[768]{0:T(1024)(128)(2,1)S(1)}, bf16[768]{0:T(1024)(128)(2,1)}, u32[]{:S(2)}) copy-start(bf16[768]{0:T(1024)(128)(2,1)} %param.54) | copy-start | bytes 4612
  23.4 4.3 %copy-start.33 = (bf16[768]{0:T(1024)(128)(2,1)S(1)}, bf16[768]{0:T(1024)(128)(2,1)}, u32[]{:S(2)}) copy-start(bf16[768]{0:T(1024)(128)(2,1)} %param.55) | copy-start | bytes 4612
  24.5 42.5 %collective-permute-start.12 = (bf16[784,768]{1,0:T(8,128)(2,1)}, bf16[784,768]{1,0:T(8,128)(2,1)}, u32[]{:S(2)}, u32[]{:S(2)}) collective-permute-start(bf16[784,768]{1,0:T(8,128)(2,1)} %dynamic-slice_bitcast_fusion), channel_id=1, source_target_pairs={{0,2},{1,3},{2,0},{3,1},{4,6},{5,7},{6,4},{7,5},{8,10},{9,11},{10,... | collective-permute-start | bytes 3612680 | tf_op jit(solution)/shard_map/ppermute | solution.py:73
  26.8 38.4 %collective-permute-start.9 = (bf16[384,768]{1,0:T(8,128)(2,1)}, bf16[384,768]{1,0:T(8,128)(2,1)}, u32[]{:S(2)}, u32[]{:S(2)}) collective-permute-start(bf16[384,768]{1,0:T(8,128)(2,1)} %pad_maximum_fusion.3), channel_id=1, source_target_pairs={{0,2},{1,3},{2,0},{3,1},{4,6},{5,7},{6,4},{7,5},{8,10},{9,11},{10,... | collective-permute-start | bytes 1769480 | tf_op jit(solution)/shard_map/ppermute | solution.py:73
  28.4 37.9 %collective-permute-start.8 = (bf16[384,768]{1,0:T(8,128)(2,1)}, bf16[384,768]{1,0:T(8,128)(2,1)S(1)}, u32[]{:S(2)}, u32[]{:S(2)}) collective-permute-start(bf16[384,768]{1,0:T(8,128)(2,1)} %pad_maximum_fusion.3), channel_id=1, source_target_pairs={{0,1},{1,0},{2,3},{3,2},{4,5},{5,4},{6,7},{7,6},{8,9},{9,8},{10,11... | collective-permute-start | bytes 1769480 | tf_op jit(solution)/shard_map/ppermute | solution.py:73
  35.9 4.5 %copy-start.1 = (f32[768,768]{1,0:T(8,128)S(1)}, f32[768,768]{1,0:T(8,128)}, u32[]{:S(2)}) copy-start(f32[768,768]{1,0:T(8,128)} %param.40) | copy-start | bytes 7077892
  39.9 28.6 %collective-permute-start.2 = (bf16[512,768]{1,0:T(8,128)(2,1)}, bf16[512,768]{1,0:T(8,128)(2,1)}, u32[]{:S(2)}, u32[]{:S(2)}) collective-permute-start(bf16[512,768]{1,0:T(8,128)(2,1)} %collective-permute-done.1.x2), channel_id=1, source_target_pairs={{0,1},{1,0},{2,3},{3,2},{4,5},{5,4},{6,7},{7,6},{8,9},{9,8},{10,11... | collective-permute-start | bytes 2359304 | tf_op jit(solution)/shard_map/ppermute | solution.py:73
  40.4 26.0 %copy-start.5 = (bf16[2,784,768]{2,1,0:T(8,128)(2,1)S(1)}, bf16[2,784,768]{2,1,0:T(8,128)(2,1)}, u32[]{:S(2)}) copy-start(bf16[2,784,768]{2,1,0:T(8,128)(2,1)} %copy-done.4) | copy-start | bytes 7225348
  65.3 35.4 %collective-permute-start.10 = (bf16[384,768]{1,0:T(8,128)(2,1)}, bf16[384,768]{1,0:T(8,128)(2,1)S(1)}, u32[]{:S(2)}, u32[]{:S(2)}) collective-permute-start(bf16[384,768]{1,0:T(8,128)(2,1)} %collective-permute-done.9), channel_id=1, source_target_pairs={{0,1},{1,0},{2,3},{3,2},{4,5},{5,4},{6,7},{7,6},{8,9},{9,8},{10,11... | collective-permute-start | bytes 1769480 | tf_op jit(solution)/shard_map/ppermute | solution.py:73
  66.4 34.3 %copy-start.9 = (bf16[192,768]{1,0:T(8,128)(2,1)S(1)}, bf16[192,768]{1,0:T(8,128)(2,1)}, u32[]{:S(2)}) copy-start(bf16[192,768]{1,0:T(8,128)(2,1)} %copy-done.8) | copy-start | bytes 884740
  66.5 34.3 %copy-start.13 = (bf16[192,768]{1,0:T(8,128)(2,1)S(1)}, bf16[192,768]{1,0:T(8,128)(2,1)}, u32[]{:S(2)}) copy-start(bf16[192,768]{1,0:T(8,128)(2,1)} %param.46) | copy-start | bytes 884740
  66.5 74.9 %collective-permute-start.11 = (bf16[2,784,768]{2,1,0:T(8,128)(2,1)S(1)}, bf16[2,784,768]{2,1,0:T(8,128)(2,1)}, u32[]{:S(2)}, u32[]{:S(2)}) collective-permute-start(bf16[2,784,768]{2,1,0:T(8,128)(2,1)S(1)} %copy-done.5), channel_id=1, source_target_pairs={{0,1},{1,0},{2,3},{3,2},{4,5},{5,4},{6,7},{7,6},{8,9},{9,8},{10,11... | collective-permute-start | bytes 7225352 | tf_op jit(solution)/shard_map/ppermute | solution.py:73
  67.0 47.0 %collective-permute-start.13 = (bf16[784,768]{1,0:T(8,128)(2,1)}, bf16[784,768]{1,0:T(8,128)(2,1)}, u32[]{:S(2)}, u32[]{:S(2)}) collective-permute-start(bf16[784,768]{1,0:T(8,128)(2,1)} %collective-permute-done.12.pack_a), channel_id=1, source_target_pairs={{0,4},{4,0},{8,12},{12,8},{16,20},{20,16},{24,28},{28,24},{1,5},{5... | collective-permute-start | bytes 3612680 | tf_op jit(solution)/shard_map/ppermute | solution.py:982
  99.5 13.9 %collective-permute-start.4 = (bf16[2,512,192]{2,1,0:T(8,128)(2,1)}, bf16[2,512,192]{2,1,0:T(8,128)(2,1)S(1)}, u32[]{:S(2)}, u32[]{:S(2)}) collective-permute-start(bf16[2,512,192]{2,1,0:T(8,128)(2,1)} %get-tuple-element.38), channel_id=1, source_target_pairs={{0,2},{1,3},{2,0},{3,1},{4,6},{5,7},{6,4},{7,5},{8,10},{9,11},{10,... | collective-permute-start | bytes 1179656 | tf_op jit(solution)/shard_map/ppermute | solution.py:73
  102.3 39.0 %collective-permute-start.3 = (bf16[512,192]{1,0:T(8,128)(2,1)S(1)}, bf16[512,192]{1,0:T(8,128)(2,1)S(1)}, u32[]{:S(2)}, u32[]{:S(2)}) collective-permute-start(bf16[512,192]{1,0:T(8,128)(2,1)S(1)} %copy-done.37), channel_id=1, source_target_pairs={{0,1},{1,0},{2,3},{3,2},{4,5},{5,4},{6,7},{7,6},{8,9},{9,8},{10,11... | collective-permute-start | bytes 589832 | tf_op jit(solution)/shard_map/ppermute | solution.py:73
  113.4 27.8 %copy-start.17 = (bf16[2,512,192]{2,1,0:T(8,128)(2,1)}, bf16[2,512,192]{2,1,0:T(8,128)(2,1)S(1)}, u32[]{:S(2)}) copy-start(bf16[2,512,192]{2,1,0:T(8,128)(2,1)S(1)} %collective-permute-done.4.ca23) | copy-start | bytes 1179652
  113.5 27.8 %collective-permute-start.5 = (bf16[512,192]{1,0:T(8,128)(2,1)S(1)}, bf16[512,192]{1,0:T(8,128)(2,1)S(1)}, u32[]{:S(2)}, u32[]{:S(2)}) collective-permute-start(bf16[512,192]{1,0:T(8,128)(2,1)S(1)} %slice_bitcast_fusion), channel_id=1, source_target_pairs={{0,1},{1,0},{2,3},{3,2},{4,5},{5,4},{6,7},{7,6},{8,9},{9,8},{10,11... | collective-permute-start | bytes 589832 | tf_op jit(solution)/shard_map/ppermute | solution.py:73
  113.6 27.8 %collective-permute-start.14 = (bf16[784,768]{1,0:T(8,128)(2,1)}, bf16[784,768]{1,0:T(8,128)(2,1)}, u32[]{:S(2)}, u32[]{:S(2)}) collective-permute-start(bf16[784,768]{1,0:T(8,128)(2,1)} %collective-permute-done.12.pack_a), channel_id=1, source_target_pairs={{0,1},{1,0},{2,3},{3,2},{4,5},{5,4},{6,7},{7,6},{8,9},{9,8},{10,11... | collective-permute-start | bytes 3612680 | tf_op jit(solution)/shard_map/ppermute | solution.py:73
  114.1 27.3 %collective-permute-start.15 = (bf16[784,768]{1,0:T(8,128)(2,1)}, bf16[784,768]{1,0:T(8,128)(2,1)}, u32[]{:S(2)}, u32[]{:S(2)}) collective-permute-start(bf16[784,768]{1,0:T(8,128)(2,1)} %collective-permute-done.13.pack_b), channel_id=1, source_target_pairs={{0,1},{1,0},{2,3},{3,2},{4,5},{5,4},{6,7},{7,6},{8,9},{9,8},{10,11... | collective-permute-start | bytes 3612680 | tf_op jit(solution)/shard_map/ppermute | solution.py:73
  (24 other events, 76.3 us)

commit v4 on v3

--- a/solution.py
+++ b/solution.py
@@ -15,6 +15,7 @@
 SEG_LANE = HEAD_DIM
 ROW_TERM = HEAD_DIM + 16
 Q_BLOCK = 256
+PACK_PAD = 32
 CHUNKS = 2
 BF16, F32 = jnp.bfloat16, jnp.float32
 ROWS_ROWS = (((0,), (0,)), ((), ()))
@@ -71,17 +72,6 @@
 def swap(array, bit):
     size = lax.axis_size("tensor")
     return lax.ppermute(array, "tensor", [(i, i ^ bit) for i in range(size)])
-
-
-def gather_blocks(own):
-    far = swap(own, 2)
-    near = swap(own, 1)
-    return [own, near, far, swap(far, 1)]
-
-
-def sum_small(array):
-    array = array + swap(array, 1)
-    return array + swap(array, 2)
 
 
 def lookup(indices, lookup_table):
@@ -110,6 +100,57 @@
     return first, second, values - first - second
 
 
+def sign_of(values):
+    return jnp.where(values > 0.0, 1.0, jnp.where(values < 0.0, -1.0, 0.0))
+
+
+def prepare_kernel(
+    out_ref, t_out_ref, up_ref, down_ref, t_up_ref, t_down_ref, t_bias_ref, *rest
+):
+    *vectors, outs_ref, w_up_ref, s_down_ref, pack_ref, sums_ref, vec_ref = rest
+    vec_ref[...] = jnp.zeros_like(vec_ref)
+    for index, vector in enumerate(vectors):
+        vec_ref[index : index + 1, :] = vector[...].astype(F32).reshape(1, -1)
+    hidden, width = down_ref.shape
+    half = hidden // 2
+    rows = out_ref.shape[0]
+    total = lambda ref: jnp.sum(jnp.abs(ref[...]), axis=0, keepdims=True)
+    sums_ref[...] = jnp.zeros_like(sums_ref)
+    sums_ref[0:1, :] = total(out_ref)
+    sums_ref[1:2, :] = total(down_ref)
+    outs_ref[:rows, :] = sign_of(out_ref[...]).astype(BF16)
+    outs_ref[rows:, :] = t_out_ref[...]
+    w_up_ref[...] = (total(up_ref) * (1.0 / width) * sign_of(up_ref[...])).astype(BF16)
+    s_down_ref[...] = sign_of(down_ref[...]).astype(BF16)
+    up_t = t_up_ref[...].T
+    pack_ref[:, hidden:, :] = jnp.zeros((2, PACK_PAD, width), BF16)
+    for side in range(2):
+        cols = slice(side * half, (side + 1) * half)
+        pack_ref[side, :half, :] = up_t[cols]
+        pack_ref[side, half:hidden, :] = t_down_ref[cols, :]
+        bias = t_bias_ref[cols].astype(F32).reshape(1, -1)
+        pack_ref[side, hidden : hidden + 1, :half] = bias.astype(BF16)
+
+
+def prepare(latents, vectors):
+    array = jax.ShapeDtypeStruct
+    out_latent, _, up_latent, down_latent, *_ = latents
+    hidden, width = down_latent.shape
+    return pl.pallas_call(
+        prepare_kernel,
+        out_shape=[
+            array((2 * out_latent.shape[0], width), BF16),
+            array(up_latent.shape, BF16),
+            array(down_latent.shape, BF16),
+            array((2, hidden + PACK_PAD, width), BF16),
+            array((8, width), F32),
+            array((16, width), F32),
+        ],
+        compiler_params=pltpu.CompilerParams(vmem_limit_bytes=58 * 2**20),
+        name="prepare",
+    )(*latents, *vectors)
+
+
 def in_lane(shape, axis, terms):
     lane = lax.broadcasted_iota(jnp.int32, shape, axis)
     spread = jnp.zeros(shape, F32)
@@ -118,130 +159,270 @@
     return spread
 
 
+def make_copies(send_sem, recv_sem):
+    count = [0]
+
+    def copy_to(source, target, axis, device):
+        index = count[0]
+        count[0] += 1
+
+        def make():
+            return pltpu.make_async_remote_copy(
+                src_ref=source,
+                dst_ref=target,
+                send_sem=send_sem.at[index],
+                recv_sem=recv_sem.at[index],
+                device_id={axis: device},
+                device_id_type=pl.DeviceIdType.MESH,
+            )
+
+        return make
+
+    return copy_to
+
+
+def greet(others):
+    barrier = pltpu.get_barrier_semaphore()
+    for other in others:
+        pl.semaphore_signal(barrier, inc=1, device_id=other, device_id_type=pl.DeviceIdType.MESH)
+    pl.semaphore_wait(barrier, len(others))
+
+
+def neighbours():
+    me = lax.axis_index("tensor")
+    return me + 1 - 2 * lax.rem(me, 2), lax.rem(me + 2, lax.axis_size("tensor"))
+
+
 def forward_kernel(base_ref, x0, x1, x2, x3, w_ref, b_ref, seg_ref, blocked_ref, *rest, student):
     if student:
-        qkv_ref, ctx_ref, source, own, near, far, joined, query_part, key_part, keys, vals_t = rest
+        pack_ref, outs, sums_ref, *rest = rest
+        q_ref, k_ref, v_ref, ctx_ref, source, own, near, far, *rest = rest
+        sums_out, pack_near, piece_a, outs1, outs2, sums, *rest = rest
     else:
-        sent, source, joined, query_part, key_part, keys, vals_t = rest
+        ca_near, ca_far, outs2, piece_a, *rest = rest
+        sent, ca1, ca2, ca_pass, ca3, outs3, next_a, piece_b, piece_c, source, *rest = rest
+    joined, queries, keys, vals_t, send_sem, recv_sem = rest
     blocks = (x0, x1, x2, x3)
     own_rows = x0.shape[0]
     rows = own_rows * len(blocks)
+    heads = joined.shape[0]
     head = pl.program_id(0)
+    near_id, far_id = neighbours()
+    place = lax.axis_index("dp")
+    copy_to = make_copies(send_sem, recv_sem)
+    side_id, side = in_pair(place, 1)
+    next_id, level = in_pair(place, 2)
+    others = [{"tensor": near_id}, {"tensor": far_id}, {"dp": side_id}]
+    if not student:
+        others.append({"dp": next_id})
+    if student:
+        size = piece_a.shape[0]
+        quarter = pack_ref.at[side, pl.ds(pl.multiple_of(level * size, 16), size)]
+        half = outs.shape[0] // 2
+        rows_of = pl.ds(pl.multiple_of(side * half, 16), half)
+        outs_far = copy_to(outs.at[rows_of], outs2.at[rows_of], "tensor", far_id)
+        pack_far = copy_to(quarter, piece_a, "tensor", far_id)
+        sum_near = copy_to(sums.at[0], sums.at[1], "tensor", near_id)
+        sum_far = copy_to(sums.at[2], sums.at[3], "tensor", far_id)
+        stages = [
+            (
+                [],
+                [
+                    sum_near,
+                    outs_far,
+                    copy_to(outs, outs1, "tensor", near_id),
+                    copy_to(pack_ref, pack_near, "tensor", near_id),
+                ],
+            ),
+            ([outs_far], [pack_far, copy_to(outs2.at[rows_of], outs2.at[rows_of], "dp", side_id)]),
+            ([], []),
+        ]
+    else:
+        passing = copy_to(ca_far.at[1], ca_pass, "tensor", far_id)
+        stages = [
+            (
+                [],
+                [
+                    passing,
+                    copy_to(ca_far.at[0], ca2, "tensor", far_id),
+                    copy_to(ca_near, ca1, "tensor", near_id),
+                    copy_to(outs2, outs3, "tensor", near_id),
+                    copy_to(piece_a, next_a, "dp", next_id),
+                    copy_to(piece_a, piece_c, "tensor", near_id),
+                    copy_to(piece_a, piece_b, "dp", side_id),
+                ],
+            ),
+            ([], []),
+            ([passing], [copy_to(ca_pass, ca3, "tensor", near_id)]),
+        ]
+
+    def run_stage(index):
+        before, copies = stages[index]
+        for copy in before:
+            copy().wait_recv()
+        for copy in copies:
+            copy().start()
 
     @pl.when(head == 0)
     def _():
+        if student:
+            sums[0] = sums_ref[...]
+        greet(others)
+        run_stage(0)
         lane = lax.broadcasted_iota(jnp.int32, (own_rows, LANES), 1)
+        ones = (lane >= ROW_TERM) & (lane < ROW_TERM + 3)
         for j, block in enumerate(blocks):
             part = slice(j * own_rows, (j + 1) * own_rows)
             if student:
                 source[part, :] = clip_act(block[...].astype(F32)).astype(BF16)
             else:
                 source[part, :] = block[...]
-            place = lax.broadcasted_iota(jnp.int32, (own_rows, LANES), 0) + base_ref[j]
-            inside = (place >= seg_ref[0:1, :]) & (place < seg_ref[1:2, :])
-            query_part[part, :] = jnp.where(inside, MASKED_SCORE, 0.0).astype(BF16)
+            spot = lax.broadcasted_iota(jnp.int32, (own_rows, LANES), 0) + base_ref[j]
+            inside = (spot >= seg_ref[0:1, :]) & (spot < seg_ref[1:2, :])
             links = dot(jnp.where(inside, 1.0, 0.0).astype(BF16), blocked_ref[...])
-            ones = (lane >= ROW_TERM) & (lane < ROW_TERM + 3)
-            key_part[part, :] = jnp.where(ones, 1.0, links).astype(BF16)
-
-    proj = (dot(source[...], w_ref[0]) + b_ref[0]).astype(BF16)
-    queries = proj[:, :LANES] + query_part[...]
-    keys[...] = proj[:, LANES : 2 * LANES] + key_part[...]
-    vals_t[...] = proj[:, 2 * LANES :].T
+            extras = (
+                jnp.where(inside, MASKED_SCORE, 0.0).astype(BF16),
+                jnp.where(ones, 1.0, links).astype(BF16),
+                jnp.where(ones, 1.0, 0.0).astype(BF16),
+            )
+            for c, (scale, extra) in enumerate(zip((0.125, 1.0, 1.0), extras)):
+                proj = dot(source[part, :], w_ref[c]) + b_ref[c : c + 1, :]
+                proj = proj.astype(BF16)
+                for h in range(heads):
+                    one = proj[:, h * HEAD_DIM : (h + 1) * HEAD_DIM] * scale
+                    wide = jnp.concatenate([one, jnp.zeros_like(one)], axis=1) + extra
+                    if c == 0:
+                        queries[h, part, :] = wide
+                    elif c == 1:
+                        keys[h, part, :] = wide
+                    else:
+                        vals_t[h, :, part] = wide.T
+                        if student:
+                            v_ref[h, part, :] = wide
+
     if student:
-        qkv_ref[:, LANES : 2 * LANES] = keys[...]
-        lane = lax.broadcasted_iota(jnp.int32, (rows, LANES), 1)
-        ones = jnp.where((lane >= ROW_TERM) & (lane < ROW_TERM + 3), 1.0, 0.0).astype(BF16)
-        qkv_ref[:, 2 * LANES :] = proj[:, 2 * LANES :] + ones
-    scores = []
-    for start in range(0, rows, Q_BLOCK):
-        scores.append(dot_cols(keys[...], queries[start : start + Q_BLOCK]))
-    for index, block in enumerate(scores):
+        k_ref[0] = keys[head]
+
+    scores = {}
+    for index in range(rows // Q_BLOCK):
+        if index % (rows // Q_BLOCK // 2) == 0:
+            if index:
+
+                @pl.when(head == 0)
+                def _():
+                    run_stage(1)
+
+                @pl.when(head == 1)
+                def _():
+                    run_stage(2)
+                    if student:
+                        sum_near().wait_recv()
+                        sums[2] = sums[0] + sums[1]
+                        sum_far().start()
+
+            for later in range(index, index + rows // Q_BLOCK // 2):
+                start = later * Q_BLOCK
+                scores[later] = dot_cols(keys[head], queries[head, start : start + Q_BLOCK, :])
+        block = scores[index]
         part = slice(index * Q_BLOCK, (index + 1) * Q_BLOCK)
         peak = jnp.max(block, axis=0, keepdims=True)
         raised = jnp.exp(block - peak)
         total = jnp.sum(raised, axis=0, keepdims=True)
         weights = (raised * (1.0 / total)).astype(BF16)
-        context = dot(vals_t[...], weights)[:HEAD_DIM].T
+        context = dot(vals_t[head], weights)[:HEAD_DIM].T
         joined[head, part, :] = context
         if student:
             ctx_ref[0, part, :] = context
             terms = split_three(-(peak + jnp.log(total)))
             spread = in_lane((LANES, Q_BLOCK), 0, terms)
-            qkv_ref[part, :LANES] = queries[part] + spread.T.astype(BF16)
-
-    @pl.when(head == pl.num_programs(0) - 1)
+            q_ref[0, part, :] = queries[head, part, :] + spread.T.astype(BF16)
+
+    @pl.when(head == heads - 1)
     def _():
         for j in range(len(blocks)):
             part = slice(j * own_rows, (j + 1) * own_rows)
-            block = jnp.concatenate([joined[h, part, :] for h in range(joined.shape[0])], axis=1)
+            block = jnp.concatenate([joined[h, part, :] for h in range(heads)], axis=1)
             if not student:
                 sent[j] = block.astype(BF16)
             elif j < 2:
                 (own, near)[j][...] = clip_act(block).astype(BF16)
             else:
                 far[j - 2] = clip_act(block).astype(BF16)
-
-
-def attend_forward(base, blocks, weight, bias, seg_lanes, blocked, student):
+        waited = [copy for before, _ in stages for copy in before]
+        if student:
+            sum_far().wait_recv()
+            sums_out[...] = sums[2] + sums[3]
+            sum_far().wait_send()
+            waited.append(sum_near)
+        for _, copies in stages:
+            for copy in copies:
+                copy().wait_send()
+                if copy not in waited:
+                    copy().wait_recv()
+
+
+def attend_forward(base, blocks, weight, bias, seg_lanes, blocked, moved, student):
     own_rows, width = blocks[0].shape
     rows = own_rows * len(blocks)
-    heads = weight.shape[0]
-    cols = 3 * LANES
-    head_cols = heads * HEAD_DIM
+    head_cols = weight.shape[2]
+    heads = head_cols // HEAD_DIM
     whole = lambda *shape: pl.BlockSpec(shape, lambda h: (0,) * len(shape))
+    anywhere = pl.BlockSpec(memory_space=pl.ANY)
     array = jax.ShapeDtypeStruct
+    per_head = lambda cols: pl.BlockSpec((1, rows, cols), lambda h: (h, 0, 0))
     if student:
-        out_specs = [
-            pl.BlockSpec((rows, cols), lambda h: (0, h)),
-            pl.BlockSpec((1, rows, HEAD_DIM), lambda h: (h, 0, 0)),
-            whole(rows, width),
-            whole(own_rows, head_cols),
-            whole(own_rows, head_cols),
-            whole(2, own_rows, head_cols),
+        pack, out_weights, sums = moved
+        piece = (pack.shape[1] // 2, width)
+        outs = [
+            (per_head(LANES), array((heads, rows, LANES), BF16)),
+            (per_head(LANES), array((heads, rows, LANES), BF16)),
+            (whole(heads, rows, LANES), array((heads, rows, LANES), BF16)),
+            (per_head(HEAD_DIM), array((heads, rows, HEAD_DIM), F32)),
+            (whole(rows, width), array((rows, width), BF16)),
+            (whole(own_rows, head_cols), array((own_rows, head_cols), BF16)),
+            (whole(own_rows, head_cols), array((own_rows, head_cols), BF16)),
+            (whole(2, own_rows, head_cols), array((2, own_rows, head_cols), BF16)),
+            (whole(*sums.shape), array(sums.shape, F32)),
+            (anywhere, array(pack.shape, BF16)),
         ]
-        out_shape = [
-            array((rows, heads * cols), BF16),
-            array((heads, rows, HEAD_DIM), F32),
-            array((rows, width), BF16),
-            array((own_rows, head_cols), BF16),
-            array((own_rows, head_cols), BF16),
-            array((2, own_rows, head_cols), BF16),
-        ]
-        scratch = []
+        outs += [(anywhere, array(piece, BF16))]
+        outs += [(anywhere, array(out_weights.shape, BF16))] * 2
+        scratch, transfers = [pltpu.VMEM((4,) + sums.shape, F32)], 7
     else:
-        out_specs = [whole(len(blocks), own_rows, head_cols)]
-        out_shape = [array((len(blocks), own_rows, head_cols), BF16)]
-        scratch = [pltpu.VMEM((rows, width), BF16)]
+        ca_near, ca_far, out_weights, piece = moved
+        outs = [(whole(len(blocks), own_rows, head_cols), array((len(blocks), own_rows, head_cols), BF16))]
+        outs += [(anywhere, array(ca_near.shape, BF16))] * 4
+        outs += [(anywhere, array(out_weights.shape, BF16))]
+        outs += [(anywhere, array(piece.shape, BF16))] * 3
+        scratch, transfers = [pltpu.VMEM((rows, width), BF16)], 8
     scratch += [
         pltpu.VMEM((heads, rows, HEAD_DIM), F32),
-        pltpu.VMEM((rows, LANES), BF16),
-        pltpu.VMEM((rows, LANES), BF16),
-        pltpu.VMEM((rows, LANES), BF16),
-        pltpu.VMEM((LANES, rows), BF16),
+        pltpu.VMEM((heads, rows, LANES), BF16),
+        pltpu.VMEM((heads, rows, LANES), BF16),
+        pltpu.VMEM((heads, LANES, rows), BF16),
+        pltpu.SemaphoreType.DMA((transfers,)),
+        pltpu.SemaphoreType.DMA((transfers,)),
     ]
     return pl.pallas_call(
         functools.partial(forward_kernel, student=student),
         grid=(heads,),
         in_specs=[pl.BlockSpec(memory_space=pltpu.SMEM)]
         + [whole(own_rows, width)] * 4
-        + [
-            pl.BlockSpec((1, width, cols), lambda h: (h, 0, 0)),
-            pl.BlockSpec((1, 1, cols), lambda h: (h, 0, 0)),
-            whole(*seg_lanes.shape),
-            whole(*blocked.shape),
-        ],
-        out_specs=out_specs,
-        out_shape=out_shape,
+        + [whole(*a.shape) for a in (weight, bias, seg_lanes, blocked)]
+        + [whole(*a.shape) if a.dtype == F32 else anywhere for a in moved],
+        out_specs=[spec for spec, _ in outs],
+        out_shape=[shape for _, shape in outs],
         scratch_shapes=scratch,
-        compiler_params=pltpu.CompilerParams(vmem_limit_bytes=58 * 2**20),
+        compiler_params=pltpu.CompilerParams(
+            collective_id=1 if student else 2, has_side_effects=True, vmem_limit_bytes=58 * 2**20
+        ),
         cost_estimate=pl.CostEstimate(
             flops=16 * heads * rows * rows * HEAD_DIM,
-            bytes_accessed=2 * rows * (width + 2 * heads * cols),
+            bytes_accessed=2 * rows * (width + 6 * heads * LANES),
             transcendentals=heads * rows * rows,
         ),
         name="student_attention" if student else "teacher_attention",
-    )(base, *blocks, weight, bias, seg_lanes, blocked)
+    )(base, *blocks, weight, bias, seg_lanes, blocked, *moved)
 
 
 def in_pair(place, bit):
@@ -291,19 +472,19 @@
 
 
 def split_rows(first, count):
-    large = count * 2 // 3 // 64 * 64
-    return ((first, large), (first + large, count - large))
+    small = count // 2 if count % 512 == 0 else -(-count // 3 // 64) * 64
+    return ((first, count - small), (first + count - small, small))
 
 
 def dp_bits():
     bits = [1 << i for i in range((lax.axis_size("dp") - 1).bit_length())]
-    return bits, (bits[1:] + bits[:1])
+    return bits, (bits[1:2] + bits[:1] + bits[2:])
 
 
 def backward_kernel(
-    qkv_ref, ctx_ref, x_ref, w_ref, g0, g1, g2, g3, ffn_ref, outg_ref, small_ref,
+    q_ref, k_ref, v_ref, ctx_ref, x_ref, w_ref, g0, g1, g2, g3, ffn_ref, outg_ref, small_ref,
     ffn_out, late_out, small_out, gx_out, gxfar_out,
-    grads, packed, keys_t, total, ffn_part, ffn, late_in, late, small, small_in, landing, small_land,
+    grads, wide, packed, keys_t, total, ffn_part, ffn, late_in, late, small, small_in, landing, small_land,
     out_near, out_near_land, out_far, out_far_land, gx_near, gx_near_land, gx_far, gx_far_land,
     send_sem, recv_sem, *, key_block,
 ):
@@ -313,35 +494,14 @@
     heads = grads.shape[0]
     head_cols = heads * HEAD_DIM
     head = pl.program_id(0)
-    group = lax.axis_size("tensor")
-    me, place = lax.axis_index("tensor"), lax.axis_index("dp")
-    near_id = me + 1 - 2 * lax.rem(me, 2)
-    far_id = lax.rem(me + 2, group)
+    place = lax.axis_index("dp")
+    near_id, far_id = neighbours()
     part = lambda j: slice(j * own_rows, (j + 1) * own_rows)
     bits, turned = dp_bits()
 
-    count = [0]
-    sends = []
-
-    def copy_to(source, target, device):
-        index = count[0]
-        count[0] += 1
-
-        def make():
-            return pltpu.make_async_remote_copy(
-                src_ref=source,
-                dst_ref=target,
-                send_sem=send_sem.at[index],
-                recv_sem=recv_sem.at[index],
-                device_id=device,
-                device_id_type=pl.DeviceIdType.MESH,
-            )
-
-        sends.append(make)
-        return make
-
-    over_dp = lambda source, target, other: copy_to(source, target, {"dp": other})
-    over_tensor = lambda source, target, other: copy_to(source, target, {"tensor": other})
+    copy_to = make_copies(send_sem, recv_sem)
+    over_dp = lambda source, target, other: copy_to(source, target, "dp", other)
+    over_tensor = lambda source, target, other: copy_to(source, target, "tensor", other)
 
     used = [0]
 
@@ -380,14 +540,8 @@
 
     @pl.when(head == 0)
     def _():
-        barrier = pltpu.get_barrier_semaphore()
         others = [{"tensor": near_id}, {"tensor": far_id}]
-        others += [{"dp": in_pair(place, bit)[0]} for bit in bits]
-        for other in others:
-            pl.semaphore_signal(
-                barrier, inc=1, device_id=other, device_id_type=pl.DeviceIdType.MESH
-            )
-        pl.semaphore_wait(barrier, len(others))
+        greet(others + [{"dp": in_pair(place, bit)[0]} for bit in bits])
         ffn_part[...] = ffn_ref[...]
         run_step(ffn_plans, 0)
         out_near[0] = outg_ref[1]
@@ -402,18 +556,23 @@
                     [one, jnp.zeros_like(one)], axis=1
                 ).astype(BF16)
         packed[...] = jnp.zeros_like(packed)
-
-    queries = qkv_ref[:, :LANES]
+        wide[...] = jnp.zeros_like(wide)
+        for h in range(heads):
+            for c, scale in enumerate((0.125, 1.0, 1.0)):
+                one = w_ref[c, :, h * HEAD_DIM : (h + 1) * HEAD_DIM] * scale
+                wide[h, :, c * LANES : c * LANES + HEAD_DIM] = one
+
+    queries = q_ref[0]
     slopes = grads[head]
     inner = -jnp.sum(slopes[:, :HEAD_DIM].astype(F32) * ctx_ref[0], axis=1, keepdims=True)
     slopes = slopes + in_lane((rows, LANES), 1, split_three(inner)).astype(BF16)
-    keys_t[...] = qkv_ref[:, LANES : 2 * LANES].T
+    keys_t[...] = k_ref[0].T
 
     def over_keys(first, last, query_grad):
         for start in range(first, last, key_block):
             span = slice(start, start + key_block)
-            weights = jnp.exp(dot_cols(qkv_ref[span, LANES : 2 * LANES], queries))
-            grad_weights = dot_cols(qkv_ref[span, 2 * LANES :], slopes)
+            weights = jnp.exp(dot_cols(k_ref[0, span, :], queries))
+            grad_weights = dot_cols(v_ref[0, span, :], slopes)
             grad_scores = (weights * grad_weights).astype(BF16)
             step = dot(keys_t[:, span], grad_scores)
             query_grad = step if query_grad is None else query_grad + step
@@ -423,10 +582,21 @@
             packed[span, 2 * LANES : 2 * LANES + HEAD_DIM] = value_grad.astype(BF16)
         return query_grad
 
-    query_grad = over_keys(0, rows // 2, None)
-
-    @pl.when(head == 0)
+    def at(which):
+        return pl.when(head == which)
+
+    quarter = rows // 4
+    query_grad = over_keys(0, quarter, None)
+
+    @at(1)
     def _():
+        run_step(ffn_plans, 2)
+
+    query_grad = over_keys(quarter, 2 * quarter, query_grad)
+
+    @at(0)
+    def _():
+        run_step(ffn_plans, 1)
         out_steps[0]().wait_recv()
         out_far[...] = (outg_ref[2].astype(F32) + out_near_land[1].astype(F32)).astype(BF16)
         out_steps[1]().start()
@@ -434,18 +604,17 @@
         small[2] = small[0] + small[1]
         tensor_small[1]().start()
 
-    @pl.when(head == 1)
+    @at(1)
     def _():
-        run_step(ffn_plans, 2)
         run_step(early_plans, 1)
 
-    @pl.when(head == 2)
+    @at(2)
     def _():
         run_step(ffn_plans, 4)
         run_step(early_plans, 3)
         run_step(middle_plans, 1)
 
-    query_grad = over_keys(rows // 2, rows, query_grad)
+    query_grad = over_keys(2 * quarter, rows, query_grad)
     packed[:, :HEAD_DIM] = query_grad[:HEAD_DIM].T.astype(BF16)
     sums = jnp.sum(packed[...].astype(F32), axis=0, keepdims=True)
     small[4 + head, 0:1, : 3 * LANES] = sums
@@ -466,7 +635,6 @@
             + out_far_land[...].astype(F32)
         ).astype(BF16)
         tensor_small[1]().wait_recv()
-        run_step(ffn_plans, 1)
         run_step(early_plans, 0)
 
     @pl.when(head == 1)
@@ -486,7 +654,7 @@
         small_steps[0]().start()
 
     for j in (1, 3, 2, 0):
-        step = dot_cols(packed[part(j), :], w_ref[0])
+        step = dot_cols(packed[part(j), :], wide[head])
         total[part(j), :] = jnp.where(head == 0, step, total[part(j), :] + step)
 
     @pl.when(head == heads - 1)
@@ -494,14 +662,13 @@
         gx_near[0] = total[part(1), :].astype(BF16)
         gx_near[1] = total[part(3), :].astype(BF16)
         gx_steps[0]().start()
-        run_step(ffn_plans, 5)
-        run_step(early_plans, 4)
-        run_step(middle_plans, 2)
         run_step(last_plans, 1)
         gx_steps[0]().wait_recv()
         gx_far[...] = (total[part(2), :] + gx_near_land[1].astype(F32)).astype(BF16)
         gx_steps[1]().start()
         gx_out[...] = total[part(0), :] + gx_near_land[0].astype(F32)
+        run_step(early_plans, 4)
+        run_step(middle_plans, 2)
         for index in range(1, 2 * len(bits) + 1):
             if index > 1:
                 run_step(last_plans, index)
@@ -515,7 +682,8 @@
                     small_out[...] = arrived
             run_step(middle_plans, 2 + index)
             run_step(early_plans, 4 + index)
-            run_step(ffn_plans, 5 + index)
+        for index in range(5, 2 * len(bits) + 1):
+            run_step(ffn_plans, index)
         ffn_out[...] = ffn[...]
         late_out[...] = late[...]
         gx_steps[1]().wait_recv()
@@ -530,7 +698,7 @@
     rows, width = source.shape
     own_rows, head_cols = blocks[0].shape
     cols = 3 * LANES
-    heads = weight.shape[0]
+    heads = head_cols // HEAD_DIM
     levels = (lax.axis_size("dp") - 1).bit_length()
     ffn_rows, late_rows = 2 * ffn_grads.shape[0], (heads + 1) * head_cols
     landing = ffn_rows + late_rows + 8 * 48 * levels
@@ -542,10 +710,12 @@
         functools.partial(backward_kernel, key_block=256),
         grid=(heads,),
         in_specs=[
-            pl.BlockSpec((rows, cols), lambda h: (0, h)),
+            head_block(rows, LANES),
+            head_block(rows, LANES),
+            head_block(rows, LANES),
             head_block(rows, HEAD_DIM),
             whole(rows, width),
-            head_block(width, cols),
+            whole(*weight.shape),
         ]
         + [whole(own_rows, head_cols)] * 4
         + [whole(*ffn_grads.shape), whole(*out_grads.shape), whole(*small.shape)],
@@ -565,6 +735,7 @@
         ],
         scratch_shapes=[
             pltpu.VMEM((heads, rows, LANES), BF16),
+            pltpu.VMEM((heads, width, cols), BF16),
             pltpu.VMEM((rows, cols), BF16),
             pltpu.VMEM((LANES, rows), BF16),
             pltpu.VMEM((rows, width), F32),
@@ -596,7 +767,7 @@
             transcendentals=heads * rows * rows,
         ),
         name="attention_backward",
-    )(qkv, context, source, weight, *blocks, ffn_grads, out_grads, small)
+    )(*qkv, context, source, weight, *blocks, ffn_grads, out_grads, small)
 
 
 (OUT_BIAS, GAIN_1, SHIFT_1, DOWN_BIAS, GAIN_2, SHIFT_2, UP_BIAS) = range(7)
@@ -605,33 +776,31 @@
 
 
 def middle_kernel(
-    x_ref, ca0, ca1, ca23, ca3, tc_ref, w_out, tw_out, w_up, w_down, vec,
-    pack_own, pack_near, pack_a, pack_b, pack_c, pack_d,
-    out_ref, gh_ref, kept_ref, outg_ref, g0_ref, g1_ref, g2_ref, g3_ref, small_ref,
+    x_ref, ca0, ca1, ca2, ca3, tc_ref, outs0, outs1, outs2, outs3, w_up, s_down, vec,
+    pack_own, pack_near, piece_a, piece_b, piece_c, next_a, sums_ref,
+    out_ref, gh_ref, kept_ref, outg_ref, g0_ref, g1_ref, g2_ref, g3_ref, small_ref, piece_d, next_b, next_c, next_d,
     tc1, tc2, tcf, tc3, y_all, g_all, slope, hid, gu_all, t_out, first, normed, two, inv,
-    part0, part2, send1, send2, send3, near0, near2, far0, gs, gr, packs, ffn_ref, ffn_land,
+    part0, part2, send1, send2, send3, near0, near2, far0, gs, gr, packs, ffn_ref, ffn_land, w_outs, w_down,
     send_sem, recv_sem, pack_sem,
 ):
-    me = lax.axis_index("tensor")
-    near_id = me + 1 - 2 * lax.rem(me, 2)
-    far_id = lax.rem(me + 2, 4)
+    near_id, far_id = neighbours()
     own_rows, width = x_ref.shape
-    hidden = w_down.shape[0]
+    hidden = s_down.shape[0]
     head_cols = ca0.shape[1]
     size = own_rows // CHUNKS
     chunks = [slice(c * size, (c + 1) * size) for c in range(CHUNKS)]
     tiles = [slice(n, n + 256) for n in range(0, hidden, 256)]
     group = lambda j: slice(j * head_cols, (j + 1) * head_cols)
+    outs = (outs0, outs1, outs2, outs3)
+    w_out = lambda j: w_outs[j]
+    tw_out = lambda j: outs[j][head_cols:, :]
     row = lambda index: vec[index : index + 1, :]
 
     place = lax.axis_index("dp")
     first_bits = [order[0] for order in dp_bits()]
     others = [{"tensor": near_id}, {"tensor": far_id}]
     others += [{"dp": in_pair(place, bit)[0]} for bit in first_bits]
-    barrier = pltpu.get_barrier_semaphore()
-    for other in others:
-        pl.semaphore_signal(barrier, inc=1, device_id=other, device_id_type=pl.DeviceIdType.MESH)
-    pl.semaphore_wait(barrier, len(others))
+    greet(others)
 
     count = [0]
     started = []
@@ -654,15 +823,39 @@
     t_far = put(tc_ref.at[2], tc2, far_id)
     t_pass = put(tc_ref.at[3], tcf, far_id)
     t_near = put(tc_ref.at[1], tc1, near_id)
+    next_id, level = in_pair(place, 2)
+    cut = piece_a.shape[0]
+    here = pl.ds(pl.multiple_of(level * cut, 16), cut)
+    there = pl.ds(pl.multiple_of((1 - level) * cut, 16), cut)
+    next_copies = [
+        put(next_a, next_c, near_id),
+        put(piece_b, next_b, next_id, "dp"),
+        put(piece_b, piece_d, near_id),
+    ]
 
     pack_refs = [pack_own.at[0], pack_own.at[1], pack_near.at[0], pack_near.at[1]]
-    pack_refs += [pack_a, pack_b, pack_c, pack_d]
+    pack_refs += [(piece_a, next_a), (piece_c, next_c), (piece_b, next_b), (piece_d, next_d)]
 
     def load_pack(index):
         slot = index % 2
-        return pltpu.make_async_copy(pack_refs[index], packs.at[slot], pack_sem.at[slot])
-
-    load_pack(0).start()
+        source, target = pack_refs[index], packs.at[slot]
+        if not isinstance(source, tuple):
+            return [pltpu.make_async_copy(source, target, pack_sem.at[slot])]
+        return [
+            pltpu.make_async_copy(source[0], target.at[here], pack_sem.at[slot]),
+            pltpu.make_async_copy(source[1], target.at[there], pack_sem.at[2 + slot]),
+        ]
+
+    def start_pack(index):
+        for copy in load_pack(index):
+            copy.start()
+
+    start_pack(0)
+    a_out = (sums_ref[0:1, :] * (1.0 / width)).astype(BF16)
+    a_down = (sums_ref[1:2, :] * (1.0 / (lax.axis_size("tensor") * hidden))).astype(BF16)
+    for j in range(4):
+        w_outs[j] = outs[j][:head_cols, :] * a_out
+    w_down[...] = s_down[...] * a_down
     small_ref[...] = jnp.zeros_like(small_ref)
 
     def add_small(index, values):
@@ -676,8 +869,8 @@
 
     y_sent = []
     for rows in chunks:
-        attn = dot(ca0[rows, :], w_out[group(0), :]) + dot(ca1[rows, :], w_out[group(1), :])
-        attn += dot(ca23[0, rows, :], w_out[group(2), :]) + dot(ca3[rows, :], w_out[group(3), :])
+        attn = dot(ca0[rows, :], w_out(0)) + dot(ca1[rows, :], w_out(1))
+        attn += dot(ca2[rows, :], w_out(2)) + dot(ca3[rows, :], w_out(3))
         y_one, y_normed, y_inv = norm_forward(
             x_ref[rows, :].astype(F32) + attn + row(OUT_BIAS), row(GAIN_1), row(SHIFT_1)
         )
@@ -751,10 +944,9 @@
     t_near.wait_recv()
     t_far.wait_recv()
     t_row = lambda index: row(T_VECTORS + index)
-    t_attn = dot(tc_ref[0], tw_out[group(0), :]) + dot(tc1[...], tw_out[group(1), :])
-    t_attn += dot(tc2[...], tw_out[group(2), :])
+    t_attn = dot(tc_ref[0], tw_out(0)) + dot(tc1[...], tw_out(1)) + dot(tc2[...], tw_out(2))
     t_last.wait_recv()
-    t_attn += dot(tc3[...], tw_out[group(3), :])
+    t_attn += dot(tc3[...], tw_out(3))
     t_one, _, _ = norm_forward(x_ref[...].astype(F32) + t_attn + t_row(0), t_row(1), t_row(2))
     two[...] = t_one
     t_out[...] = t_one + t_row(3)
@@ -762,9 +954,17 @@
     t_in = t_one.astype(BF16)
     for index in range(len(pack_refs)):
         slot = index % 2
+        if index == 4:
+            next_copies[0].wait_recv()
+            next_copies[1].wait_recv()
+            next_copies.append(put(next_b, next_d, near_id))
+        if index == 6:
+            next_copies[2].wait_recv()
+            next_copies[3].wait_recv()
         if index + 1 < len(pack_refs):
-            load_pack(index + 1).start()
-        load_pack(index).wait()
+            start_pack(index + 1)
+        for copy in load_pack(index):
+            copy.wait()
         upward = dot_cols(t_in, packs[slot, :half, :])
         upward = upward + packs[slot, hidden : hidden + 1, :half].astype(F32)
         act = (upward * normal_parts(upward)[0]).astype(BF16)
@@ -820,10 +1020,10 @@
         gh_ref[rows, :] = grad_h
         grad_attn = grad_h.astype(BF16)
         add_small(OUT_BIAS, grad_attn.astype(F32))
-        for j, ca in enumerate((ca0.at[rows], ca1.at[rows], ca23.at[0, rows], ca3.at[rows])):
+        for j, ca in enumerate((ca0.at[rows], ca1.at[rows], ca2.at[rows], ca3.at[rows])):
             act = ca[...]
             level = act.astype(F32) * (1.0 / CLIP_RANGE)
-            grad = dot_cols(grad_attn, w_out[group(j), :]) * (1.0 - level * level)
+            grad = dot_cols(grad_attn, w_out(j)) * (1.0 - level * level)
             gs[j, rows, :] = grad.astype(BF16)
             step = dot_rows(act, grad_attn)
             if c:
@@ -858,19 +1058,20 @@
         copy.wait_send()
 
 
-def middle(x_own, cas, tc, w_out, tw_out, w_up, w_down, vectors, packs):
+def middle(x_own, cas, tc, outs, w_up, s_down, vectors, packs, sums):
     own_rows, width = x_own.shape
-    hidden = w_down.shape[0]
+    hidden = s_down.shape[0]
     head_cols = cas[0].shape[1]
     array = jax.ShapeDtypeStruct
     vmem = pl.BlockSpec(memory_space=pltpu.VMEM)
-    transfers = 4 + 4 * 3 * CHUNKS + 4 * CHUNKS + 2
+    transfers = 8 + 4 * 3 * CHUNKS + 4 * CHUNKS + 2
+    four_outs = pltpu.VMEM((4, head_cols, width), BF16)
     square = lambda kind: pltpu.VMEM((own_rows, width), kind)
     four = lambda cols, kind: pltpu.VMEM((4, own_rows, cols), kind)
     return pl.pallas_call(
         middle_kernel,
-        in_specs=[vmem] * 11 + [pl.BlockSpec(memory_space=pl.ANY)] * 6,
-        out_specs=[vmem] * 9,
+        in_specs=[vmem] * 13 + [pl.BlockSpec(memory_space=pl.ANY)] * 6 + [vmem],
+        out_specs=[vmem] * 9 + [pl.BlockSpec(memory_space=pl.ANY)] * 4,
         out_shape=[
             array((own_rows, width), BF16),
             array((own_rows, width), F32),
@@ -878,7 +1079,8 @@
             array((4, head_cols, width), BF16),
         ]
         + [array((own_rows, head_cols), BF16)] * 4
-        + [array((8, width), F32)],
+        + [array((8, width), F32)]
+        + [array(packs[2].shape, BF16)] * 4,
         scratch_shapes=[pltpu.VMEM((own_rows, head_cols), BF16)] * 4
         + [four(width, BF16), four(width, BF16), four(hidden, F32), four(hidden, BF16)]
         + [four(hidden, BF16)]
@@ -888,12 +1090,14 @@
         + [square(BF16)] * 6
         + [four(head_cols, BF16), four(head_cols, BF16)]
         + [
-            pltpu.VMEM((2,) + packs[2].shape, BF16),
+            pltpu.VMEM(packs[0].shape, BF16),
             pltpu.VMEM((width + hidden, width), BF16),
             pltpu.VMEM(((width + hidden) // 2, width), BF16),
+            four_outs,
+            pltpu.VMEM(s_down.shape, BF16),
             pltpu.SemaphoreType.DMA((transfers,)),
             pltpu.SemaphoreType.DMA((transfers,)),
-            pltpu.SemaphoreType.DMA((2,)),
+            pltpu.SemaphoreType.DMA((4,)),
         ],
         compiler_params=pltpu.CompilerParams(
             collective_id=3, has_side_effects=True, vmem_limit_bytes=62 * 2**20
@@ -902,23 +1106,12 @@
             flops=120 * own_rows * width * hidden, bytes_accessed=2**25, transcendentals=2**22
         ),
         name="middle",
-    )(x_own, *cas, tc, w_out, tw_out, w_up, w_down, vectors, *packs)
-
-
-def padded_heads(weight, bias):
-    width, _, cols = weight.shape
-    heads = cols // HEAD_DIM
-    scale = jnp.array([0.125, 1.0, 1.0], F32)
-    weight = weight.reshape(width, 3, heads, HEAD_DIM).transpose(2, 0, 1, 3)
-    weight = weight * scale[None, None, :, None].astype(weight.dtype)
-    weight = jnp.pad(weight, ((0, 0), (0, 0), (0, 0), (0, LANES - HEAD_DIM)))
-    full = jnp.stack([bias[0] * 0.125, jnp.zeros_like(bias[0]), bias[1]]).astype(F32)
-    full = full.reshape(3, heads, HEAD_DIM).transpose(1, 0, 2)
-    full = jnp.pad(full, ((0, 0), (0, 0), (0, LANES - HEAD_DIM)))
-    return (
-        weight.reshape(heads, width, 3 * LANES).astype(BF16),
-        full.reshape(heads, 1, 3 * LANES),
-    )
+    )(x_own, *cas, tc, *outs, w_up, s_down, vectors, *packs, sums)
+
+
+def projection(weight, bias):
+    rows = jnp.stack([bias[0], jnp.zeros_like(bias[0]), bias[1]]).astype(F32)
+    return weight.transpose(1, 0, 2), jnp.pad(rows, ((0, 5), (0, 0)))
 
 
 def body(
@@ -956,54 +1149,35 @@
     all_rows = own_rows * group
     local_cols = qkv_latent.shape[2]
     local_heads = local_cols // HEAD_DIM
-    hid = up_latent.shape[1]
-    half = hid // 2
     near_x = swap(tokens, 1)
     far_x = swap(tokens, 2)
     blocks = [tokens, near_x, far_x, swap(far_x, 1)]
-    sums = sum_small(
-        jnp.stack([jnp.sum(jnp.abs(out_latent), axis=0), jnp.sum(jnp.abs(down_latent), axis=0)])
-    )
-    w_qkv = (jnp.mean(jnp.abs(qkv_latent), axis=0) * jnp.sign(qkv_latent)).astype(BF16)
-    w_out = (sums[0] / model_width * jnp.sign(out_latent)).astype(BF16)
-    w_up = (jnp.mean(jnp.abs(up_latent), axis=0) * jnp.sign(up_latent)).astype(BF16)
-    w_down = (sums[1] / (hid * group) * jnp.sign(down_latent)).astype(BF16)
-    seg_lanes, blocked = segment_tables(seg_lengths[0], parents[0])
-    base = jnp.stack([(me ^ j) * own_rows for j in range(group)]).astype(jnp.int32)
-
-    up_t = teacher_up.T
-    bias_rows = jnp.pad(teacher_up_bias.reshape(2, 1, half), ((0, 0), (0, 15), (0, model_width - half)))
-    pack = jnp.concatenate(
-        [up_t.reshape(2, half, -1), teacher_down.reshape(2, half, -1), bias_rows], axis=1
-    )
-    pack, far_x = lax.optimization_barrier((pack, far_x))
-    side = lax.rem(lax.axis_index("dp"), 2)
-    far_a = swap(lax.dynamic_index_in_dim(pack, side, 0, keepdims=False), 2)
-    far_b = lax.ppermute(far_a, "dp", [(i, i ^ 1) for i in range(lax.axis_size("dp"))])
-    packs = [pack, swap(pack, 1), far_a, far_b, swap(far_a, 1), swap(far_b, 1)]
-    outs = jnp.concatenate([w_out, teacher_out])
-    outs = gather_blocks(outs)
-    w_out_all = jnp.concatenate([block[:local_cols] for block in outs])
-    t_out_all = jnp.concatenate([block[local_cols:] for block in outs])
-
-    wide_qkv, wide_bias = padded_heads(w_qkv, qv_bias)
-    qkv, context, x_in_all, ca_own, ca_near, ca_far = attend_forward(
-        base, blocks, wide_qkv, wide_bias, seg_lanes, blocked, True
-    )
-    (t_context,) = attend_forward(
-        base, blocks, *padded_heads(teacher_qkv, teacher_qv_bias), seg_lanes, blocked, False
-    )
-    ca_23 = swap(ca_far, 2)
-    cas = [ca_own, swap(ca_near, 1), ca_23, swap(ca_23[1], 1)]
+    latents = [out_latent, teacher_out, up_latent, down_latent]
+    latents += [teacher_up, teacher_down, teacher_up_bias]
     vectors = [out_bias, norm1_gain, norm1_shift, down_bias, norm2_gain, norm2_shift, up_bias]
     vectors += [teacher_out_bias, teacher_norm1_gain, teacher_norm1_shift]
     vectors += [teacher_down_bias, teacher_norm2_gain, teacher_norm2_shift]
-    vectors = jnp.pad(jnp.stack(vectors).astype(F32), ((0, 3), (0, 0)))
-    out_own, grad_h, ffn_grads, out_grads, g0, g1, g2, g3, small = middle(
-        tokens, cas, t_context, w_out_all, t_out_all, w_up, w_down, vectors, packs
+    outs, w_up, s_down, pack, sums, vectors = prepare(latents, vectors)
+    w_qkv = (jnp.mean(jnp.abs(qkv_latent), axis=0) * jnp.sign(qkv_latent)).astype(BF16)
+    seg_lanes, blocked = segment_tables(seg_lengths[0], parents[0])
+    base = jnp.stack([(me ^ j) * own_rows for j in range(group)]).astype(jnp.int32)
+
+    w_three, b_three = projection(w_qkv, qv_bias)
+    tables = (seg_lanes, blocked)
+    *qkv, context, x_in_all, ca_own, ca_near, ca_far, sums, pack_near, piece_a, outs1, outs2 = attend_forward(
+        base, blocks, w_three, b_three, *tables, [pack, outs, sums], True
+    )
+    t_context, ca1, ca2, _, ca3, outs3, next_a, piece_b, piece_c = attend_forward(
+        base, blocks, *projection(teacher_qkv, teacher_qv_bias), *tables,
+        [ca_near, ca_far, outs2, piece_a], False,
+    )
+    cas, outs = [ca_own, ca1, ca2, ca3], [outs, outs1, outs2, outs3]
+    packs = [pack, pack_near, piece_a, piece_b, piece_c, next_a]
+    out_own, grad_h, ffn_grads, out_grads, g0, g1, g2, g3, small, *_ = middle(
+        tokens, cas, t_context, outs, w_up, s_down, vectors, packs, sums
     )
     ffn_grads, late, small, gx_own, gx_far = attend_backward(
-        qkv, context, x_in_all, wide_qkv, [g0, g1, g2, g3], ffn_grads, out_grads, small
+        qkv, context, x_in_all, w_three, [g0, g1, g2, g3], ffn_grads, out_grads, small
     )
     grad_x_in = gx_own + gx_far.astype(F32)
     input_grad = grad_h + grad_x_in * clip_slope(tokens.astype(F32))

time: 372 us -> 309 us (0.83)
  waiting for transfers between devices: 37.9 us -> 0.9 us
  other arithmetic: 22.1 us -> 11.1 us
  local copies, waits for them, and re-layouts: 26.8 us -> 16.2 us
  starting transfers between devices: 10.1 us -> 3.04 us
  Pallas kernels: 266 us -> 270 us
    ppermute x15 -> x3, waiting for transfers between devices: 37.9 us -> 0.9 us  [swap(): return lax.ppermute(array, 'tensor', [(i, i ^ bit) for i in range(size)])]
    reshape x5 -> x0, local copies, waits for them, and re-layouts: 7.42 us -> none  [the longest x2 6.19 us: padded_heads(): weight.reshape(heads, width, 3 * LANES).astype(BF16)]
    pallas_call x1 -> x2, Pallas kernels: 107 us -> 113 us  [the longest x1 105 us: middle(): pl.pallas_call(middle_kernel, in_specs=[vmem] * 13 + [pl.BlockSpec(memory...]
    ppermute x15 -> x3, starting transfers between devices: 8.65 us -> 3.04 us  [swap(): return lax.ppermute(array, 'tensor', [(i, i ^ bit) for i in range(size)])]
    pallas_call x1, Pallas kernels: 101 us -> 95.2 us  [attend_backward(): pl.pallas_call(functools.partial(backward_kernel, key_block=256), grid=(h...]
    convert_element_type x4 -> x0, other arithmetic: 5.07 us -> none  [the longest x1 1.7 us: body(): (jnp.mean(jnp.abs(up_latent), axis=0) * jnp.sign(up_latent)).astype(BF16)]
    pallas_call x2, Pallas kernels: 58.1 us -> 62.6 us  [attend_forward(): pl.pallas_call(functools.partial(forward_kernel, student=student), grid=(...]
  transfers between devices with their start and end apart: 16 -> 3, of which waited for: 3 -> 1; matrix products, arithmetic and copies ran while one was open for 9% -> 4% of each run, Pallas kernels for 16% -> 2%
where the time goes in v4:
time: 309 us; the launch traced here: 305 us
  Pallas kernels  270 us (87%)
  local copies, waits for them, and re-layouts  16.2 us (5%)
  other arithmetic  11.1 us (4%)
    pallas_call x1, Pallas kernels, middle(): pl.pallas_call(middle_kernel, in_specs=[vmem] * 13 + [pl.BlockSpec(memory...  105 us
    pallas_call x1, Pallas kernels, attend_backward(): pl.pallas_call(functools.partial(backward_kernel, key_block=256), grid=(h...  95.2 us
    pallas_call x2, Pallas kernels, attend_forward(): pl.pallas_call(functools.partial(forward_kernel, student=student), grid=(...  62.6 us
    pallas_call x1, Pallas kernels, prepare(): pl.pallas_call(prepare_kernel, out_shape=[array((2 * out_latent.shape[0],...  7.23 us
    unnamed x21, local copies, waits for them, and re-layouts  7.02 us
  transfers between devices with their start and end apart: 3, of which 1 were waited for; matrix products, arithmetic and copies ran while one was open for 4% of the time, Pallas kernels for 2%

profile of v4, /device:TPU:0, one launch (start us, length us, event | category | flops | bytes accessed | tf_op | source)
XLA Modules:
  0.0 304.5 jit_solution(10190908004962085809)
XLA Ops:
  0.6 3.0 collective-permute-start.1
  3.7 0.8 select_reduce_fusion.1
  4.5 0.7 bitcast_add_fusion
  5.1 0.8 fusion.10
  5.9 0.8 fusion.9
  6.6 2.3 copy.43
  9.0 1.9 copy.42
  11.0 0.7 pad.23.seg_ref
  11.7 7.2 %prepare.1 = (bf16[384,768]{1,0:T(8,128)(2,1)}, bf16[768,768]{1,0:T(8,128)(2,1)}, bf16[768,768]{1,0:T(8,128)(2,1)}, bf16[2,800,768]{2,1,0:T(8,128)(2,1)}, f32[8,768]{1,0:T(8,128)}, /*index=5*/f32[16,768]{1,0:T(8,128)}) custom-call(f32[192,768]{1,0:T(8,128)} %out_ref.1, bf16[192,768]{1,0:T(8,128)(2,1)} %t_out_ref.1, f32[768,768]{1,0:T(8,128)} %up_ref.1, ...), custom_call_target="tpu_custom_call" | custom-call | tf_op jit(solution)/shard_map/prepare/pallas_call | solution.py:139
  19.0 0.6 pad_convert_fusion.1
  19.6 0.2 select_reduce_fusion
  19.8 0.7 pad_convert_fusion.blocked_ref
  20.5 0.9 collective-permute-done.1.x2
  21.4 0.7 pad_add_fusion.1.base_ref
  22.1 0.2 abs_reduce_fusion
  22.3 1.7 fusion.w_ref
  24.0 0.9 copy-done.8
  24.9 33.9 %student_attention.1 = (bf16[3,2048,128]{2,1,0:T(8,128)(2,1)}, bf16[3,2048,128]{2,1,0:T(8,128)(2,1)}, bf16[3,2048,128]{2,1,0:T(8,128)(2,1)}, f32[3,2048,64]{2,1,...) custom-call(s32[4]{0:T(128)} %pad_add_fusion.1.base_ref, ...), custom_call_target="tpu_custom_call" | custom-call | flops 12884901888 | bytes 12582912 | tf_op jit(solution)/shard_map/student_attention/pallas_call | solution.py:406
  58.8 28.7 %teacher_attention.1 = (bf16[4,512,192]{2,1,0:T(8,128)(2,1)}, bf16[512,192]{1,0:T(8,128)(2,1)}, bf16[512,192]{1,0:T(8,128)(2,1)}, bf16[512,192]{1,0:T(8,128)(2,1...) custom-call(s32[4]{0:T(128)} %pad_add_fusion.1.base_ref, ...), custom_call_target="tpu_custom_call" | custom-call | flops 12884901888 | bytes 12582912 | tf_op jit(solution)/shard_map/teacher_attention/pallas_call | solution.py:406
  87.6 105.4 %middle.1 = (bf16[512,768]{1,0:T(8,128)(2,1)}, f32[512,768]{1,0:T(8,128)}, bf16[768,768]{1,0:T(8,128)(2,1)}, bf16[4,192,768]{2,1,0:T(8,128)(2,1)}, bf16[512,192]...) custom-call(bf16[512,768]{1,0:T(8,128)(2,1)} %x_ref.1, ...), custom_call_target="tpu_custom_call" | custom-call | flops 36238786560 | bytes 33554432 | tf_op jit(solution)/shard_map/middle/pallas_call | solution.py:1071
  192.9 95.2 %attention_backward.1 = (bf16[1536,768]{1,0:T(8,128)(2,1)}, bf16[768,768]{1,0:T(8,128)(2,1)}, f32[16,768]{1,0:T(8,128)}, f32[512,768]{1,0:T(8,128)}, bf16[512,768]{1,0:T(8,128)(2,1)}) custom-call(bf16[3,2048,128]{2,1,0:T(8,128)(2,1)} %get-tuple-element.79.q_ref, bf16[3,2048,128]{2,1,0:T(8,128)(2,1)} %get-tuple-element.80.k_ref, ...), custom_call_target="tpu_custom_call" | custom-call | flops 48318382080 | bytes 15728640 | tf_op jit(solution)/shard_map/attention_backward/pallas_call | solution.py:709
  288.2 0.8 slice.74
  289.0 1.7 slice_reduce_fusion
  290.7 1.1 slice.90
  291.9 0.9 fusion.8
  293.0 0.1 pad_maximum_fusion
  293.1 1.3 copy.44
  294.4 1.0 copy-done
  295.4 2.6 fusion.7
  298.7 0.6 pad_maximum_fusion.3
  299.3 3.0 %multiply_add_fusion = f32[512,768]{1,0:T(8,128)} fusion(f32[512,768]{1,0:T(8,128)S(1)} %copy-done.3, bf16[512,768]{1,0:T(8,128)(2,1)} %x_ref.1, f32[512,768]{1,0:T(8,128)S(1)} %copy-done.4, bf16[512,768]{1,0:T(8,128)(2,1)} %get-tuple-element.94), kind=kLoop, calls=%fused_computation.3 | loop fusion | flops 3145728 | bytes 6291456 | tf_op jit(solution)/shard_map/add | solution.py:1183
  302.3 0.9 copy.46
  (30 shorter events, 0.5 us)
Async XLA Ops:
  0.6 20.8 %collective-permute-start.1 = (bf16[512,768]{1,0:T(8,128)(2,1)}, bf16[512,768]{1,0:T(8,128)(2,1)S(1)}, u32[]{:S(2)}, u32[]{:S(2)}) collective-permute-start(bf16[512,768]{1,0:T(8,128)(2,1)} %x_ref.1), channel_id=1, source_target_pairs={{0,2},{1,3},{2,0},{3,1},{4,6},{5,7},{6,4},{7,5},{8,10},{9,11},{10,... | collective-permute-start | bytes 2359304 | tf_op jit(solution)/shard_map/ppermute | solution.py:74
  3.7 20.3 %collective-permute-start = (bf16[512,768]{1,0:T(8,128)(2,1)}, bf16[512,768]{1,0:T(8,128)(2,1)}, u32[]{:S(2)}, u32[]{:S(2)}) collective-permute-start(bf16[512,768]{1,0:T(8,128)(2,1)} %x_ref.1), channel_id=1, source_target_pairs={{0,1},{1,0},{2,3},{3,2},{4,5},{5,4},{6,7},{7,6},{8,9},{9,8},{10,11... | collective-permute-start | bytes 2359304 | tf_op jit(solution)/shard_map/ppermute | solution.py:74
  11.6 7.9 %copy-start.6 = (s32[1,13]{1,0:T(1,128)S(1)}, s32[1,13]{1,0:T(1,128)}, u32[]{:S(2)}) copy-start(s32[1,13]{1,0:T(1,128)} %param.29) | copy-start | bytes 160
  11.7 10.5 %copy-start.1 = (f32[768,3,192]{0,2,1:T(8,128)S(1)}, f32[768,3,192]{0,2,1:T(8,128)}, u32[]{:S(2)}) copy-start(f32[768,3,192]{0,2,1:T(8,128)} %param.30) | copy-start | bytes 5308420
  21.4 2.6 copy-start.7
  21.4 2.6 collective-permute-start.2
  24.0 0.9 copy-start.8
  288.2 3.7 %copy-start.2 = (bf16[768,768]{1,0:T(8,128)(2,1)S(1)}, bf16[768,768]{1,0:T(8,128)(2,1)}, u32[]{:S(2)}) copy-start(bf16[768,768]{1,0:T(8,128)(2,1)} %get-tuple-element.95) | copy-start | bytes 3538948
  293.1 2.3 copy-start
  295.4 3.9 %copy-start.3 = (f32[512,768]{1,0:T(8,128)S(1)}, f32[512,768]{1,0:T(8,128)}, u32[]{:S(2)}) copy-start(f32[512,768]{1,0:T(8,128)} %get-tuple-element.92) | copy-start | bytes 4718596
  295.4 3.9 %copy-start.4 = (f32[512,768]{1,0:T(8,128)S(1)}, f32[512,768]{1,0:T(8,128)}, u32[]{:S(2)}) copy-start(f32[512,768]{1,0:T(8,128)} %get-tuple-element.93) | copy-start | bytes 4718596
  299.3 3.1 %copy-start.5 = (bf16[512,768]{1,0:T(8,128)(2,1)S(1)}, bf16[512,768]{1,0:T(8,128)(2,1)}, u32[]{:S(2)}) copy-start(bf16[512,768]{1,0:T(8,128)(2,1)} %get-tuple-element.134) | copy-start | bytes 2359300

commit v5 on v4

--- a/solution.py
+++ b/solution.py
@@ -200,7 +200,8 @@
         sums_out, pack_near, piece_a, outs1, outs2, sums, *rest = rest
     else:
         ca_near, ca_far, outs2, piece_a, *rest = rest
-        sent, ca1, ca2, ca_pass, ca3, outs3, next_a, piece_b, piece_c, source, *rest = rest
+        sent, ta0, ca1, ca2, ca_pass, ca3, ta1, ta2, ta_pass, ta3, *rest = rest
+        outs3, next_a, piece_b, piece_c, source, send_a, *rest = rest
     joined, queries, keys, vals_t, send_sem, recv_sem = rest
     blocks = (x0, x1, x2, x3)
     own_rows = x0.shape[0]
@@ -255,6 +256,13 @@
             ([], []),
             ([passing], [copy_to(ca_pass, ca3, "tensor", near_id)]),
         ]
+        a_passing = copy_to(send_a.at[3], ta_pass, "tensor", far_id)
+        a_copies = [
+            a_passing,
+            copy_to(send_a.at[2], ta2, "tensor", far_id),
+            copy_to(send_a.at[1], ta1, "tensor", near_id),
+        ]
+        a_last = copy_to(ta_pass, ta3, "tensor", near_id)
 
     def run_stage(index):
         before, copies = stages[index]
@@ -302,6 +310,16 @@
 
     if student:
         k_ref[0] = keys[head]
+    else:
+
+        @pl.when(head == heads - 1)
+        def _():
+            for j in range(len(blocks)):
+                part = slice(j * own_rows, (j + 1) * own_rows)
+                pair = jnp.concatenate([joined[0, part, :], joined[1, part, :]], axis=1)
+                send_a[j] = pair.astype(BF16)
+            for copy in a_copies:
+                copy().start()
 
     scores = {}
     for index in range(rows // Q_BLOCK):
@@ -341,14 +359,24 @@
     def _():
         for j in range(len(blocks)):
             part = slice(j * own_rows, (j + 1) * own_rows)
+            if not student:
+                sent[j] = stacked(joined[heads - 1, part, :]).astype(BF16)
+                continue
             block = jnp.concatenate([joined[h, part, :] for h in range(heads)], axis=1)
-            if not student:
-                sent[j] = block.astype(BF16)
-            elif j < 2:
+            if j < 2:
                 (own, near)[j][...] = clip_act(block).astype(BF16)
             else:
                 far[j - 2] = clip_act(block).astype(BF16)
         waited = [copy for before, _ in stages for copy in before]
+        if not student:
+            ta0[...] = send_a[0]
+            a_passing().wait_recv()
+            a_last().start()
+            for copy in a_copies:
+                copy().wait_send()
+            for copy in a_copies[1:] + [a_last]:
+                copy().wait_recv()
+            a_last().wait_send()
         if student:
             sum_far().wait_recv()
             sums_out[...] = sums[2] + sums[3]
@@ -390,11 +418,14 @@
         scratch, transfers = [pltpu.VMEM((4,) + sums.shape, F32)], 7
     else:
         ca_near, ca_far, out_weights, piece = moved
-        outs = [(whole(len(blocks), own_rows, head_cols), array((len(blocks), own_rows, head_cols), BF16))]
-        outs += [(anywhere, array(ca_near.shape, BF16))] * 4
+        last = (len(blocks), own_rows // 2, LANES)
+        pair = array((own_rows, LANES), BF16)
+        outs = [(whole(*last), array(last, BF16)), (whole(*pair.shape), pair)]
+        outs += [(anywhere, array(ca_near.shape, BF16))] * 4 + [(anywhere, pair)] * 4
         outs += [(anywhere, array(out_weights.shape, BF16))]
         outs += [(anywhere, array(piece.shape, BF16))] * 3
-        scratch, transfers = [pltpu.VMEM((rows, width), BF16)], 8
+        scratch, transfers = [pltpu.VMEM((rows, width), BF16)], 12
+        scratch.append(pltpu.VMEM((len(blocks),) + pair.shape, BF16))
     scratch += [
         pltpu.VMEM((heads, rows, HEAD_DIM), F32),
         pltpu.VMEM((heads, rows, LANES), BF16),
@@ -486,11 +517,11 @@
     ffn_out, late_out, small_out, gx_out, gxfar_out,
     grads, wide, packed, keys_t, total, ffn_part, ffn, late_in, late, small, small_in, landing, small_land,
     out_near, out_near_land, out_far, out_far_land, gx_near, gx_near_land, gx_far, gx_far_land,
-    send_sem, recv_sem, *, key_block,
+    send_sem, recv_sem, write_sem, *, key_block,
 ):
     blocks = (g0, g1, g2, g3)
-    own_rows = g0.shape[0]
-    rows = own_rows * len(blocks)
+    rows = x_ref.shape[0]
+    own_rows = rows // len(blocks)
     heads = grads.shape[0]
     head_cols = heads * HEAD_DIM
     head = pl.program_id(0)
@@ -513,7 +544,7 @@
                 taken if done else None,
             )
             plans.append(steps)
-            taken += rows_of[1] // 2
+            taken += rows_of[1] >> done
         return plans
 
     width = x_ref.shape[1]
@@ -549,12 +580,14 @@
         out_steps[0]().start()
         small[0] = small_ref[...]
         tensor_small[0]().start()
-        for h in range(heads):
-            for j, block in enumerate(blocks):
-                one = block[:, h * HEAD_DIM : (h + 1) * HEAD_DIM].astype(F32)
-                grads[h, part(j), :] = jnp.concatenate(
-                    [one, jnp.zeros_like(one)], axis=1
-                ).astype(BF16)
+        size = own_rows // CHUNKS
+        for j, block in enumerate(blocks):
+            for c in range(CHUNKS):
+                where = slice(j * own_rows + c * size, j * own_rows + (c + 1) * size)
+                pair = block[c, :size, :]
+                ones = [pair[:, :HEAD_DIM], pair[:, HEAD_DIM:], side_by_side(block[c, size:, :])]
+                for h, one in enumerate(ones):
+                    grads[h, where, :] = jnp.concatenate([one, jnp.zeros_like(one)], axis=1)
         packed[...] = jnp.zeros_like(packed)
         wide[...] = jnp.zeros_like(wide)
         for h in range(heads):
@@ -666,7 +699,9 @@
         gx_steps[0]().wait_recv()
         gx_far[...] = (total[part(2), :] + gx_near_land[1].astype(F32)).astype(BF16)
         gx_steps[1]().start()
-        gx_out[...] = total[part(0), :] + gx_near_land[0].astype(F32)
+        total[part(0), :] = total[part(0), :] + gx_near_land[0].astype(F32)
+        gx_write = pltpu.make_async_copy(total.at[part(0)], gx_out, write_sem.at[0])
+        gx_write.start()
         run_step(early_plans, 4)
         run_step(middle_plans, 2)
         for index in range(1, 2 * len(bits) + 1):
@@ -684,19 +719,24 @@
             run_step(early_plans, 4 + index)
         for index in range(5, 2 * len(bits) + 1):
             run_step(ffn_plans, index)
-        ffn_out[...] = ffn[...]
-        late_out[...] = late[...]
+        ffn_write = pltpu.make_async_copy(ffn, ffn_out, write_sem.at[1])
+        ffn_write.start()
+        late_write = pltpu.make_async_copy(late, late_out, write_sem.at[2])
+        late_write.start()
         gx_steps[1]().wait_recv()
-        gxfar_out[...] = gx_far_land[...]
+        far_write = pltpu.make_async_copy(gx_far_land, gxfar_out, write_sem.at[3])
+        far_write.start()
         shared = small[2, LOSS_ROW : LOSS_ROW + 1, :] + small[3, LOSS_ROW : LOSS_ROW + 1, :]
         small_out[LOSS_ROW : LOSS_ROW + 1, :] = shared
         for copy in small_steps + tensor_small + out_steps + gx_steps:
             copy().wait_send()
+        for copy in (gx_write, ffn_write, late_write, far_write):
+            copy.wait()
 
 
 def attend_backward(qkv, context, source, weight, blocks, ffn_grads, out_grads, small):
     rows, width = source.shape
-    own_rows, head_cols = blocks[0].shape
+    own_rows, head_cols = rows // len(blocks), weight.shape[2]
     cols = 3 * LANES
     heads = head_cols // HEAD_DIM
     levels = (lax.axis_size("dp") - 1).bit_length()
@@ -706,6 +746,7 @@
     array = jax.ShapeDtypeStruct
     whole = lambda *shape: pl.BlockSpec(shape, lambda h: (0,) * len(shape))
     head_block = lambda *shape: pl.BlockSpec((1,) + shape, lambda h: (h, 0, 0))
+    anywhere = pl.BlockSpec(memory_space=pl.ANY)
     return pl.pallas_call(
         functools.partial(backward_kernel, key_block=256),
         grid=(heads,),
@@ -717,14 +758,14 @@
             whole(rows, width),
             whole(*weight.shape),
         ]
-        + [whole(own_rows, head_cols)] * 4
+        + [whole(*block.shape) for block in blocks]
         + [whole(*ffn_grads.shape), whole(*out_grads.shape), whole(*small.shape)],
         out_specs=[
-            whole(ffn_rows, width),
-            whole(late_rows, width),
+            anywhere,
+            anywhere,
             whole(16, width),
-            whole(own_rows, width),
-            whole(own_rows, width),
+            anywhere,
+            anywhere,
         ],
         out_shape=[
             array((ffn_rows, width), BF16),
@@ -757,6 +798,7 @@
             pltpu.VMEM((own_rows, width), BF16),
             pltpu.SemaphoreType.DMA((transfers,)),
             pltpu.SemaphoreType.DMA((transfers,)),
+            pltpu.SemaphoreType.DMA((4,)),
         ],
         compiler_params=pltpu.CompilerParams(
             collective_id=4, has_side_effects=True, vmem_limit_bytes=62 * 2**20
@@ -770,13 +812,22 @@
     )(*qkv, context, source, weight, *blocks, ffn_grads, out_grads, small)
 
 
+def stacked(block):
+    half = block.shape[0] // 2
+    return jnp.concatenate([block[:half], block[half:]], axis=1)
+
+
+def side_by_side(block):
+    return jnp.concatenate([block[:, :HEAD_DIM], block[:, HEAD_DIM:]], axis=0)
+
+
 (OUT_BIAS, GAIN_1, SHIFT_1, DOWN_BIAS, GAIN_2, SHIFT_2, UP_BIAS) = range(7)
 T_VECTORS = 7
 LOSS_ROW, UP_ROW = 6, 7
 
 
 def middle_kernel(
-    x_ref, ca0, ca1, ca2, ca3, tc_ref, outs0, outs1, outs2, outs3, w_up, s_down, vec,
+    x_ref, ca0, ca1, ca2, ca3, tc_ref, ta0, ta1, ta2, ta3, outs0, outs1, outs2, outs3, w_up, s_down, vec,
     pack_own, pack_near, piece_a, piece_b, piece_c, next_a, sums_ref,
     out_ref, gh_ref, kept_ref, outg_ref, g0_ref, g1_ref, g2_ref, g3_ref, small_ref, piece_d, next_b, next_c, next_d,
     tc1, tc2, tcf, tc3, y_all, g_all, slope, hid, gu_all, t_out, first, normed, two, inv,
@@ -797,9 +848,8 @@
     row = lambda index: vec[index : index + 1, :]
 
     place = lax.axis_index("dp")
-    first_bits = [order[0] for order in dp_bits()]
     others = [{"tensor": near_id}, {"tensor": far_id}]
-    others += [{"dp": in_pair(place, bit)[0]} for bit in first_bits]
+    others += [{"dp": in_pair(place, bit)[0]} for bit in dp_bits()[0][:2]]
     greet(others)
 
     count = [0]
@@ -918,9 +968,9 @@
             copies.append(put(send1.at[rows], near0.at[rows], near_id))
         return copies
 
-    def far_blocks(block, work, sent):
+    def far_blocks(block, work, sent, between=()):
         copies = []
-        for rows, (_, far) in zip(chunks, sent):
+        for c, (rows, (_, far)) in enumerate(zip(chunks, sent)):
             far.wait_recv()
             passed = put(block.at[2, rows], block.at[3, rows], near_id)
             part2[rows, :] = work(2, rows)
@@ -930,6 +980,8 @@
             met.wait_recv()
             send2[rows, :] = (part2[rows, :] + near2[rows, :].astype(F32)).astype(BF16)
             copies.append(put(send2.at[rows], far0.at[rows], far_id))
+            if between:
+                between[c]()
         return copies
 
     def summed(rows, near, far):
@@ -944,38 +996,47 @@
     t_near.wait_recv()
     t_far.wait_recv()
     t_row = lambda index: row(T_VECTORS + index)
-    t_attn = dot(tc_ref[0], tw_out(0)) + dot(tc1[...], tw_out(1)) + dot(tc2[...], tw_out(2))
     t_last.wait_recv()
-    t_attn += dot(tc3[...], tw_out(3))
+    t_attn = None
+    for j, (wide, last) in enumerate(zip((ta0, ta1, ta2, ta3), (tc_ref.at[0], tc1, tc2, tc3))):
+        both = jnp.concatenate([wide[...], side_by_side(last[...])], axis=1)
+        step = dot(both, tw_out(j))
+        t_attn = step if t_attn is None else t_attn + step
     t_one, _, _ = norm_forward(x_ref[...].astype(F32) + t_attn + t_row(0), t_row(1), t_row(2))
     two[...] = t_one
     t_out[...] = t_one + t_row(3)
     half = hidden // 2
     t_in = t_one.astype(BF16)
-    for index in range(len(pack_refs)):
-        slot = index % 2
-        if index == 4:
-            next_copies[0].wait_recv()
-            next_copies[1].wait_recv()
-            next_copies.append(put(next_b, next_d, near_id))
-        if index == 6:
-            next_copies[2].wait_recv()
-            next_copies[3].wait_recv()
-        if index + 1 < len(pack_refs):
-            start_pack(index + 1)
-        for copy in load_pack(index):
-            copy.wait()
-        upward = dot_cols(t_in, packs[slot, :half, :])
-        upward = upward + packs[slot, hidden : hidden + 1, :half].astype(F32)
-        act = (upward * normal_parts(upward)[0]).astype(BF16)
-        t_out[...] += dot(act, packs[slot, half:hidden, :])
+
+    def teacher_packs(first, last):
+        for index in range(first, last):
+            slot = index % 2
+            if index == 4:
+                next_copies[0].wait_recv()
+                next_copies[1].wait_recv()
+                next_copies.append(put(next_b, next_d, near_id))
+            if index == 6:
+                next_copies[2].wait_recv()
+                next_copies[3].wait_recv()
+            if index + 1 < len(pack_refs):
+                start_pack(index + 1)
+            for copy in load_pack(index):
+                copy.wait()
+            upward = dot_cols(t_in, packs[slot, :half, :])
+            upward = upward + packs[slot, hidden : hidden + 1, :half].astype(F32)
+            act = (upward * normal_parts(upward)[0]).astype(BF16)
+            t_out[...] += dot(act, packs[slot, half:hidden, :])
+
+    middle_pack = len(pack_refs) // 2
+    between = [
+        functools.partial(teacher_packs, 0, middle_pack),
+        functools.partial(teacher_packs, middle_pack, len(pack_refs)),
+    ]
+    y_far = far_blocks(y_all, forward_block, y_sent, between)
     t_out[...] = norm_forward(t_out[...], t_row(4), t_row(5))[0]
 
-    y_far = far_blocks(y_all, forward_block, y_sent)
-
     g_sent = []
-    for copy in started:
-        copy.wait_send()
+    earlier = list(started)
     started.clear()
     for rows, near, far in zip(chunks, y_near, y_far):
         ffn = summed(rows, near, far)
@@ -994,20 +1055,25 @@
         g_all[0, rows, :] = grad_ffn
         g_sent.append(share(g_all, rows))
 
+    for copy in earlier:
+        copy.wait_send()
     g_near = near_blocks(backward_block, g_sent)
     g_far = far_blocks(g_all, backward_block, g_sent)
     flat = lambda block: block[...].reshape(4 * own_rows, block.shape[2])
-    ffn_ref[:width, :] = dot_rows(flat(y_all), flat(gu_all)).astype(BF16)
-    ffn_ref[width:, :] = dot_rows(flat(hid), flat(g_all)).astype(BF16)
-    halves, taken = [], 0
-    for (low, size), bit in zip(split_rows(0, width + hidden), first_bits):
-        partner, digit = in_pair(place, bit)
-        size = size // 2
-        give = ffn_ref.at[pl.ds(pl.multiple_of(low + (1 - digit) * size, 16), size)]
-        keep = pl.multiple_of(low + digit * size, 16)
-        land = slice(taken, taken + size)
-        halves.append((put(give, ffn_land.at[land], partner, "dp"), keep, land))
-        taken += size
+
+    def weight_gradients():
+        ffn_ref[:width, :] = dot_rows(flat(y_all), flat(gu_all)).astype(BF16)
+        ffn_ref[width:, :] = dot_rows(flat(hid), flat(g_all)).astype(BF16)
+        sent, taken = [], 0
+        for (low, count), order in zip(split_rows(0, width + hidden), dp_bits()):
+            partner, digit = in_pair(place, order[0])
+            count = count // 2
+            give = ffn_ref.at[pl.ds(pl.multiple_of(low + (1 - digit) * count, 16), count)]
+            keep = pl.multiple_of(low + digit * count, 16)
+            land = ffn_land.at[taken : taken + count]
+            sent.append((put(give, land, partner, "dp"), (keep, count)))
+            taken += count
+        return sent
 
     passes = []
     for c, (rows, near, far) in enumerate(zip(chunks, g_near, g_far)):
@@ -1024,53 +1090,61 @@
             act = ca[...]
             level = act.astype(F32) * (1.0 / CLIP_RANGE)
             grad = dot_cols(grad_attn, w_out(j)) * (1.0 - level * level)
-            gs[j, rows, :] = grad.astype(BF16)
+            grad = grad.astype(BF16)
+            gs[j, c, :size, :] = grad[:, :LANES]
+            gs[j, c, size:, :] = stacked(grad[:, LANES:])
             step = dot_rows(act, grad_attn)
             if c:
                 step = step + part2[group(j), :]
             part2[group(j), :] = step
         passes.append(
             (
-                put(gs.at[3, rows], gr.at[3, rows], far_id),
-                put(gs.at[2, rows], gr.at[1, rows], far_id),
-                put(gs.at[1, rows], gr.at[0, rows], near_id),
+                put(gs.at[3, c], gr.at[3, c], far_id),
+                put(gs.at[2, c], gr.at[1, c], far_id),
+                put(gs.at[1, c], gr.at[0, c], near_id),
             )
         )
+        if c == 0:
+            halves = weight_gradients()
     g0_ref[...] = gs[0]
     for j in range(4):
         outg_ref[j] = part2[group(j), :].astype(BF16)
     lasts = []
-    for rows, (passing, _, _) in zip(chunks, passes):
+    for c, (passing, _, _) in enumerate(passes):
         passing.wait_recv()
-        lasts.append(put(gr.at[3, rows], gr.at[2, rows], near_id))
-    for rows, (_, far, near), last in zip(chunks, passes, lasts):
+        lasts.append(put(gr.at[3, c], gr.at[2, c], near_id))
+    for c, ((_, far, near), last) in enumerate(zip(passes, lasts)):
         near.wait_recv()
-        g1_ref[rows, :] = gr[0, rows, :]
+        g1_ref[c] = gr[0, c]
         far.wait_recv()
-        g2_ref[rows, :] = gr[1, rows, :]
+        g2_ref[c] = gr[1, c]
         last.wait_recv()
-        g3_ref[rows, :] = gr[2, rows, :]
-    for copy, keep, land in halves:
+        g3_ref[c] = gr[2, c]
+    taken = 0
+    for copy, (keep, part_size) in halves:
         copy.wait_recv()
-        mine = ffn_ref[pl.ds(keep, land.stop - land.start), :].astype(F32)
+        land = slice(taken, taken + part_size)
+        mine = ffn_ref[pl.ds(keep, part_size), :].astype(F32)
         kept_ref[land, :] = (mine + ffn_land[land, :].astype(F32)).astype(BF16)
+        taken += part_size
     for copy in started:
         copy.wait_send()
 
 
-def middle(x_own, cas, tc, outs, w_up, s_down, vectors, packs, sums):
+def middle(x_own, cas, tcs, outs, w_up, s_down, vectors, packs, sums):
     own_rows, width = x_own.shape
     hidden = s_down.shape[0]
     head_cols = cas[0].shape[1]
     array = jax.ShapeDtypeStruct
     vmem = pl.BlockSpec(memory_space=pltpu.VMEM)
     transfers = 8 + 4 * 3 * CHUNKS + 4 * CHUNKS + 2
+    packed = (CHUNKS, own_rows // CHUNKS * 3 // 2, LANES)
     four_outs = pltpu.VMEM((4, head_cols, width), BF16)
     square = lambda kind: pltpu.VMEM((own_rows, width), kind)
     four = lambda cols, kind: pltpu.VMEM((4, own_rows, cols), kind)
     return pl.pallas_call(
         middle_kernel,
-        in_specs=[vmem] * 13 + [pl.BlockSpec(memory_space=pl.ANY)] * 6 + [vmem],
+        in_specs=[vmem] * 17 + [pl.BlockSpec(memory_space=pl.ANY)] * 6 + [vmem],
         out_specs=[vmem] * 9 + [pl.BlockSpec(memory_space=pl.ANY)] * 4,
         out_shape=[
             array((own_rows, width), BF16),
@@ -1078,17 +1152,17 @@
             array(((width + hidden) // 2, width), BF16),
             array((4, head_cols, width), BF16),
         ]
-        + [array((own_rows, head_cols), BF16)] * 4
+        + [array(packed, BF16)] * 4
         + [array((8, width), F32)]
         + [array(packs[2].shape, BF16)] * 4,
-        scratch_shapes=[pltpu.VMEM((own_rows, head_cols), BF16)] * 4
+        scratch_shapes=[pltpu.VMEM(tcs[0].shape[1:], BF16)] * 4
         + [four(width, BF16), four(width, BF16), four(hidden, F32), four(hidden, BF16)]
         + [four(hidden, BF16)]
         + [square(F32)] * 4
         + [pltpu.VMEM((own_rows, LANES), F32)]
         + [square(F32), pltpu.VMEM((4 * max(own_rows // 4, head_cols), width), F32)]
         + [square(BF16)] * 6
-        + [four(head_cols, BF16), four(head_cols, BF16)]
+        + [pltpu.VMEM((4,) + packed, BF16)] * 2
         + [
             pltpu.VMEM(packs[0].shape, BF16),
             pltpu.VMEM((width + hidden, width), BF16),
@@ -1106,7 +1180,7 @@
             flops=120 * own_rows * width * hidden, bytes_accessed=2**25, transcendentals=2**22
         ),
         name="middle",
-    )(x_own, *cas, tc, *outs, w_up, s_down, vectors, *packs, sums)
+    )(x_own, *cas, *tcs, *outs, w_up, s_down, vectors, *packs, sums)
 
 
 def projection(weight, bias):
@@ -1167,14 +1241,14 @@
     *qkv, context, x_in_all, ca_own, ca_near, ca_far, sums, pack_near, piece_a, outs1, outs2 = attend_forward(
         base, blocks, w_three, b_three, *tables, [pack, outs, sums], True
     )
-    t_context, ca1, ca2, _, ca3, outs3, next_a, piece_b, piece_c = attend_forward(
+    t_last, ta0, ca1, ca2, _, ca3, ta1, ta2, _, ta3, outs3, next_a, piece_b, piece_c = attend_forward(
         base, blocks, *projection(teacher_qkv, teacher_qv_bias), *tables,
         [ca_near, ca_far, outs2, piece_a], False,
     )
     cas, outs = [ca_own, ca1, ca2, ca3], [outs, outs1, outs2, outs3]
     packs = [pack, pack_near, piece_a, piece_b, piece_c, next_a]
     out_own, grad_h, ffn_grads, out_grads, g0, g1, g2, g3, small, *_ = middle(
-        tokens, cas, t_context, outs, w_up, s_down, vectors, packs, sums
+        tokens, cas, [t_last, ta0, ta1, ta2, ta3], outs, w_up, s_down, vectors, packs, sums
     )
     ffn_grads, late, small, gx_own, gx_far = attend_backward(
         qkv, context, x_in_all, w_three, [g0, g1, g2, g3], ffn_grads, out_grads, small

time: 309 us -> 297 us (0.961)
  Pallas kernels: 270 us -> 258 us
    pallas_call x1, Pallas kernels: 105 us -> 93.5 us  [middle(): pl.pallas_call(middle_kernel, in_specs=[vmem] * 17 + [pl.BlockSpec(memory...]
where the time goes in v5:
time: 297 us; the launch traced here: 292 us
  Pallas kernels  258 us (87%)
  local copies, waits for them, and re-layouts  16.2 us (5%)
  other arithmetic  11.1 us (4%)
  starting transfers between devices  3.04 us (1%)
    pallas_call x1, Pallas kernels, middle(): pl.pallas_call(middle_kernel, in_specs=[vmem] * 17 + [pl.BlockSpec(memory...  93.5 us
    pallas_call x1, Pallas kernels, attend_backward(): pl.pallas_call(functools.partial(backward_kernel, key_block=256), grid=(h...  92.9 us
    pallas_call x2, Pallas kernels, attend_forward(): pl.pallas_call(functools.partial(forward_kernel, student=student), grid=(...  63.8 us
    pallas_call x1, Pallas kernels, prepare(): pl.pallas_call(prepare_kernel, out_shape=[array((2 * out_latent.shape[0],...  7.23 us
    unnamed x21, local copies, waits for them, and re-layouts  7.02 us
  transfers between devices with their start and end apart: 3, of which 1 were waited for; matrix products, arithmetic and copies ran while one was open for 4% of the time, Pallas kernels for 2%

profile of v5, /device:TPU:0, one launch (start us, length us, event | category | flops | bytes accessed | tf_op | source)
XLA Modules:
  0.0 291.6 jit_solution(4754949399196843976)
XLA Ops:
  0.6 3.0 %collective-permute-start.1 = (bf16[512,768]{1,0:T(8,128)(2,1)}, bf16[512,768]{1,0:T(8,128)(2,1)S(1)}, u32[]{:S(2)}, u32[]{:S(2)}) collective-permute-start(bf16[512,768]{1,0:T(8,128)(2,1)} %x_ref.1), channel_id=1, source_target_pairs={{0,2},{1,3},{2,0},{3,1},{4,6},{5,7},{6,4},{7,5},{8,10},{9,11},{10,... | collective-permute-start | bytes 2359304 | tf_op jit(solution)/shard_map/ppermute | solution.py:74
  3.7 0.8 select_reduce_fusion.1
  4.5 0.7 bitcast_add_fusion
  5.1 0.8 fusion.10
  5.9 0.8 fusion.9
  6.6 2.3 copy.43
  9.0 1.9 copy.42
  11.0 0.7 pad.23.seg_ref
  11.7 7.2 %prepare.1 = (bf16[384,768]{1,0:T(8,128)(2,1)}, bf16[768,768]{1,0:T(8,128)(2,1)}, bf16[768,768]{1,0:T(8,128)(2,1)}, bf16[2,800,768]{2,1,0:T(8,128)(2,1)}, f32[8,768]{1,0:T(8,128)}, /*index=5*/f32[16,768]{1,0:T(8,128)}) custom-call(f32[192,768]{1,0:T(8,128)} %out_ref.1, bf16[192,768]{1,0:T(8,128)(2,1)} %t_out_ref.1, f32[768,768]{1,0:T(8,128)} %up_ref.1, ...), custom_call_target="tpu_custom_call" | custom-call | tf_op jit(solution)/shard_map/prepare/pallas_call | solution.py:139
  19.0 0.6 pad_convert_fusion.1
  19.6 0.2 select_reduce_fusion
  19.8 0.7 pad_convert_fusion.blocked_ref
  20.5 0.9 collective-permute-done.1.x2
  21.4 0.7 pad_add_fusion.1.base_ref
  22.1 0.2 abs_reduce_fusion
  22.3 1.7 fusion.w_ref
  24.0 0.9 copy-done.8
  24.9 33.9 %student_attention.1 = (bf16[3,2048,128]{2,1,0:T(8,128)(2,1)}, bf16[3,2048,128]{2,1,0:T(8,128)(2,1)}, bf16[3,2048,128]{2,1,0:T(8,128)(2,1)}, f32[3,2048,64]{2,1,...) custom-call(s32[4]{0:T(128)} %pad_add_fusion.1.base_ref, ...), custom_call_target="tpu_custom_call" | custom-call | flops 12884901888 | bytes 12582912 | tf_op jit(solution)/shard_map/student_attention/pallas_call | solution.py:437
  58.8 29.9 %teacher_attention.1 = (bf16[4,256,128]{2,1,0:T(8,128)(2,1)}, bf16[512,128]{1,0:T(8,128)(2,1)}, bf16[512,192]{1,0:T(8,128)(2,1)}, bf16[512,192]{1,0:T(8,128)(2,1...) custom-call(s32[4]{0:T(128)} %pad_add_fusion.1.base_ref, ...), custom_call_target="tpu_custom_call" | custom-call | flops 12884901888 | bytes 12582912 | tf_op jit(solution)/shard_map/teacher_attention/pallas_call | solution.py:437
  88.8 93.5 %middle.1 = (bf16[512,768]{1,0:T(8,128)(2,1)}, f32[512,768]{1,0:T(8,128)}, bf16[768,768]{1,0:T(8,128)(2,1)}, bf16[4,192,768]{2,1,0:T(8,128)(2,1)}, bf16[2,384,12...) custom-call(bf16[512,768]{1,0:T(8,128)(2,1)} %x_ref.1, ...), custom_call_target="tpu_custom_call" | custom-call | flops 36238786560 | bytes 33554432 | tf_op jit(solution)/shard_map/middle/pallas_call | solution.py:1145
  182.3 92.9 %attention_backward.1 = (bf16[1536,768]{1,0:T(8,128)(2,1)}, bf16[768,768]{1,0:T(8,128)(2,1)}, f32[16,768]{1,0:T(8,128)}, f32[512,768]{1,0:T(8,128)}, bf16[512,768]{1,0:T(8,128)(2,1)}) custom-call(bf16[3,2048,128]{2,1,0:T(8,128)(2,1)} %get-tuple-element.87.q_ref, bf16[3,2048,128]{2,1,0:T(8,128)(2,1)} %get-tuple-element.88.k_ref, ...), custom_call_target="tpu_custom_call" | custom-call | flops 48318382080 | bytes 15728640 | tf_op jit(solution)/shard_map/attention_backward/pallas_call | solution.py:750
  275.3 0.8 slice.74
  276.1 1.7 slice_reduce_fusion
  277.8 1.1 slice.90
  278.9 0.9 fusion.8
  280.0 0.1 pad_maximum_fusion
  280.2 1.3 copy.44
  281.5 1.0 copy-done
  282.5 2.6 fusion.7
  285.7 0.6 pad_maximum_fusion.3
  286.3 3.0 %multiply_add_fusion = f32[512,768]{1,0:T(8,128)} fusion(f32[512,768]{1,0:T(8,128)S(1)} %copy-done.3, bf16[512,768]{1,0:T(8,128)(2,1)} %x_ref.1, f32[512,768]{1,0:T(8,128)S(1)} %copy-done.4, bf16[512,768]{1,0:T(8,128)(2,1)} %get-tuple-element.102), kind=kLoop, calls=%fused_computation.3 | loop fusion | flops 3145728 | bytes 6291456 | tf_op jit(solution)/shard_map/add | solution.py:1257
  289.4 0.9 copy.46
  (30 shorter events, 0.5 us)
Async XLA Ops:
  0.6 20.8 %collective-permute-start.1 = (bf16[512,768]{1,0:T(8,128)(2,1)}, bf16[512,768]{1,0:T(8,128)(2,1)S(1)}, u32[]{:S(2)}, u32[]{:S(2)}) collective-permute-start(bf16[512,768]{1,0:T(8,128)(2,1)} %x_ref.1), channel_id=1, source_target_pairs={{0,2},{1,3},{2,0},{3,1},{4,6},{5,7},{6,4},{7,5},{8,10},{9,11},{10,... | collective-permute-start | bytes 2359304 | tf_op jit(solution)/shard_map/ppermute | solution.py:74
  3.7 20.3 %collective-permute-start = (bf16[512,768]{1,0:T(8,128)(2,1)}, bf16[512,768]{1,0:T(8,128)(2,1)}, u32[]{:S(2)}, u32[]{:S(2)}) collective-permute-start(bf16[512,768]{1,0:T(8,128)(2,1)} %x_ref.1), channel_id=1, source_target_pairs={{0,1},{1,0},{2,3},{3,2},{4,5},{5,4},{6,7},{7,6},{8,9},{9,8},{10,11... | collective-permute-start | bytes 2359304 | tf_op jit(solution)/shard_map/ppermute | solution.py:74
  11.6 7.9 %copy-start.6 = (s32[1,13]{1,0:T(1,128)S(1)}, s32[1,13]{1,0:T(1,128)}, u32[]{:S(2)}) copy-start(s32[1,13]{1,0:T(1,128)} %param.29) | copy-start | bytes 160
  11.7 10.5 %copy-start.1 = (f32[768,3,192]{0,2,1:T(8,128)S(1)}, f32[768,3,192]{0,2,1:T(8,128)}, u32[]{:S(2)}) copy-start(f32[768,3,192]{0,2,1:T(8,128)} %param.30) | copy-start | bytes 5308420
  21.4 2.6 copy-start.7
  21.4 2.6 collective-permute-start.2
  24.0 0.9 copy-start.8
  275.2 3.7 %copy-start.2 = (bf16[768,768]{1,0:T(8,128)(2,1)S(1)}, bf16[768,768]{1,0:T(8,128)(2,1)}, u32[]{:S(2)}) copy-start(bf16[768,768]{1,0:T(8,128)(2,1)} %get-tuple-element.103) | copy-start | bytes 3538948
  280.1 2.3 copy-start
  282.5 3.9 %copy-start.3 = (f32[512,768]{1,0:T(8,128)S(1)}, f32[512,768]{1,0:T(8,128)}, u32[]{:S(2)}) copy-start(f32[512,768]{1,0:T(8,128)} %get-tuple-element.100) | copy-start | bytes 4718596
  282.5 3.9 %copy-start.4 = (f32[512,768]{1,0:T(8,128)S(1)}, f32[512,768]{1,0:T(8,128)}, u32[]{:S(2)}) copy-start(f32[512,768]{1,0:T(8,128)} %get-tuple-element.101) | copy-start | bytes 4718596
  286.3 3.1 %copy-start.5 = (bf16[512,768]{1,0:T(8,128)(2,1)S(1)}, bf16[512,768]{1,0:T(8,128)(2,1)}, u32[]{:S(2)}) copy-start(bf16[512,768]{1,0:T(8,128)(2,1)} %get-tuple-element.142) | copy-start | bytes 2359300

commit v6 on v5

--- a/solution.py
+++ b/solution.py
@@ -105,15 +105,19 @@
 
 
 def prepare_kernel(
-    out_ref, t_out_ref, up_ref, down_ref, t_up_ref, t_down_ref, t_bias_ref, *rest
+    qkv_ref, out_ref, t_out_ref, up_ref, down_ref, t_up_ref, t_down_ref, t_bias_ref, *rest
 ):
-    *vectors, outs_ref, w_up_ref, s_down_ref, pack_ref, sums_ref, vec_ref = rest
+    *vectors, w_qkv_ref, outs_ref, w_up_ref, s_down_ref, pack_ref, sums_ref, vec_ref = rest
     vec_ref[...] = jnp.zeros_like(vec_ref)
     for index, vector in enumerate(vectors):
         vec_ref[index : index + 1, :] = vector[...].astype(F32).reshape(1, -1)
     hidden, width = down_ref.shape
     half = hidden // 2
     rows = out_ref.shape[0]
+    for c in range(3):
+        latent = qkv_ref[c]
+        scale = jnp.sum(jnp.abs(latent), axis=1, keepdims=True) * (1.0 / width)
+        w_qkv_ref[c] = (scale * sign_of(latent)).astype(BF16)
     total = lambda ref: jnp.sum(jnp.abs(ref[...]), axis=0, keepdims=True)
     sums_ref[...] = jnp.zeros_like(sums_ref)
     sums_ref[0:1, :] = total(out_ref)
@@ -134,11 +138,12 @@
 
 def prepare(latents, vectors):
     array = jax.ShapeDtypeStruct
-    out_latent, _, up_latent, down_latent, *_ = latents
+    qkv_latent, out_latent, _, up_latent, down_latent, *_ = latents
     hidden, width = down_latent.shape
     return pl.pallas_call(
         prepare_kernel,
         out_shape=[
+            array(qkv_latent.shape, BF16),
             array((2 * out_latent.shape[0], width), BF16),
             array(up_latent.shape, BF16),
             array(down_latent.shape, BF16),
@@ -147,6 +152,9 @@
             array((16, width), F32),
         ],
         compiler_params=pltpu.CompilerParams(vmem_limit_bytes=58 * 2**20),
+        cost_estimate=pl.CostEstimate(
+            flops=16 * 10**9, bytes_accessed=24 * width * hidden, transcendentals=0
+        ),
         name="prepare",
     )(*latents, *vectors)
 
@@ -193,7 +201,7 @@
     return me + 1 - 2 * lax.rem(me, 2), lax.rem(me + 2, lax.axis_size("tensor"))
 
 
-def forward_kernel(base_ref, x0, x1, x2, x3, w_ref, b_ref, seg_ref, blocked_ref, *rest, student):
+def forward_kernel(base_ref, x0, x1, x2, w_ref, b_ref, seg_ref, blocked_ref, *rest, student):
     if student:
         pack_ref, outs, sums_ref, *rest = rest
         q_ref, k_ref, v_ref, ctx_ref, source, own, near, far, *rest = rest
@@ -202,7 +210,7 @@
         ca_near, ca_far, outs2, piece_a, *rest = rest
         sent, ta0, ca1, ca2, ca_pass, ca3, ta1, ta2, ta_pass, ta3, *rest = rest
         outs3, next_a, piece_b, piece_c, source, send_a, *rest = rest
-    joined, queries, keys, vals_t, send_sem, recv_sem = rest
+    x3, joined, queries, keys, vals_t, send_sem, recv_sem = rest
     blocks = (x0, x1, x2, x3)
     own_rows = x0.shape[0]
     rows = own_rows * len(blocks)
@@ -264,6 +272,8 @@
         ]
         a_last = copy_to(ta_pass, ta3, "tensor", near_id)
 
+    last_block = copy_to(x2, x3, "tensor", near_id)
+
     def run_stage(index):
         before, copies = stages[index]
         for copy in before:
@@ -276,10 +286,13 @@
         if student:
             sums[0] = sums_ref[...]
         greet(others)
+        last_block().start()
         run_stage(0)
         lane = lax.broadcasted_iota(jnp.int32, (own_rows, LANES), 1)
         ones = (lane >= ROW_TERM) & (lane < ROW_TERM + 3)
         for j, block in enumerate(blocks):
+            if j == 3:
+                last_block().wait()
             part = slice(j * own_rows, (j + 1) * own_rows)
             if student:
                 source[part, :] = clip_act(block[...].astype(F32)).astype(BF16)
@@ -294,7 +307,9 @@
                 jnp.where(ones, 1.0, 0.0).astype(BF16),
             )
             for c, (scale, extra) in enumerate(zip((0.125, 1.0, 1.0), extras)):
-                proj = dot(source[part, :], w_ref[c]) + b_ref[c : c + 1, :]
+                proj = dot_cols(source[part, :], w_ref[c])
+                if c != 1:
+                    proj = proj + b_ref[c // 2 : c // 2 + 1, :].astype(F32)
                 proj = proj.astype(BF16)
                 for h in range(heads):
                     one = proj[:, h * HEAD_DIM : (h + 1) * HEAD_DIM] * scale
@@ -391,8 +406,9 @@
 
 def attend_forward(base, blocks, weight, bias, seg_lanes, blocked, moved, student):
     own_rows, width = blocks[0].shape
-    rows = own_rows * len(blocks)
-    head_cols = weight.shape[2]
+    group = len(blocks) + 1
+    rows = own_rows * group
+    head_cols = weight.shape[1]
     heads = head_cols // HEAD_DIM
     whole = lambda *shape: pl.BlockSpec(shape, lambda h: (0,) * len(shape))
     anywhere = pl.BlockSpec(memory_space=pl.ANY)
@@ -415,18 +431,19 @@
         ]
         outs += [(anywhere, array(piece, BF16))]
         outs += [(anywhere, array(out_weights.shape, BF16))] * 2
-        scratch, transfers = [pltpu.VMEM((4,) + sums.shape, F32)], 7
+        scratch, transfers = [pltpu.VMEM((4,) + sums.shape, F32)], 8
     else:
         ca_near, ca_far, out_weights, piece = moved
-        last = (len(blocks), own_rows // 2, LANES)
+        last = (group, own_rows // 2, LANES)
         pair = array((own_rows, LANES), BF16)
         outs = [(whole(*last), array(last, BF16)), (whole(*pair.shape), pair)]
         outs += [(anywhere, array(ca_near.shape, BF16))] * 4 + [(anywhere, pair)] * 4
         outs += [(anywhere, array(out_weights.shape, BF16))]
         outs += [(anywhere, array(piece.shape, BF16))] * 3
-        scratch, transfers = [pltpu.VMEM((rows, width), BF16)], 12
-        scratch.append(pltpu.VMEM((len(blocks),) + pair.shape, BF16))
+        scratch, transfers = [pltpu.VMEM((rows, width), BF16)], 13
+        scratch.append(pltpu.VMEM((group,) + pair.shape, BF16))
     scratch += [
+        pltpu.VMEM((own_rows, width), BF16),
         pltpu.VMEM((heads, rows, HEAD_DIM), F32),
         pltpu.VMEM((heads, rows, LANES), BF16),
         pltpu.VMEM((heads, rows, LANES), BF16),
@@ -438,7 +455,7 @@
         functools.partial(forward_kernel, student=student),
         grid=(heads,),
         in_specs=[pl.BlockSpec(memory_space=pltpu.SMEM)]
-        + [whole(own_rows, width)] * 4
+        + [whole(own_rows, width)] * 3
         + [whole(*a.shape) for a in (weight, bias, seg_lanes, blocked)]
         + [whole(*a.shape) if a.dtype == F32 else anywhere for a in moved],
         out_specs=[spec for spec, _ in outs],
@@ -565,7 +582,8 @@
         over_tensor(out_far, out_far_land, far_id),
     ]
     gx_steps = [
-        over_tensor(gx_near, gx_near_land, near_id),
+        over_tensor(gx_near.at[1], gx_near_land.at[1], near_id),
+        over_tensor(gx_near.at[0], gx_near_land.at[0], near_id),
         over_tensor(gx_far, gx_far_land, far_id),
     ]
 
@@ -592,8 +610,8 @@
         wide[...] = jnp.zeros_like(wide)
         for h in range(heads):
             for c, scale in enumerate((0.125, 1.0, 1.0)):
-                one = w_ref[c, :, h * HEAD_DIM : (h + 1) * HEAD_DIM] * scale
-                wide[h, :, c * LANES : c * LANES + HEAD_DIM] = one
+                one = w_ref[c, h * HEAD_DIM : (h + 1) * HEAD_DIM, :] * scale
+                wide[h, c * LANES : c * LANES + HEAD_DIM, :] = one
 
     queries = q_ref[0]
     slopes = grads[head]
@@ -686,19 +704,23 @@
             small_in[0, 8 + h : 9 + h, : 3 * LANES] = small[4 + h, 0:1, : 3 * LANES]
         small_steps[0]().start()
 
-    for j in (1, 3, 2, 0):
-        step = dot_cols(packed[part(j), :], wide[head])
+    for j in (3, 2, 1, 0):
+        step = dot(packed[part(j), :], wide[head])
         total[part(j), :] = jnp.where(head == 0, step, total[part(j), :] + step)
+        if j % 2:
+
+            @pl.when(head == heads - 1)
+            def _(j=j):
+                gx_near[j // 2] = total[part(j), :].astype(BF16)
+                gx_steps[1 - j // 2]().start()
 
     @pl.when(head == heads - 1)
     def _():
-        gx_near[0] = total[part(1), :].astype(BF16)
-        gx_near[1] = total[part(3), :].astype(BF16)
-        gx_steps[0]().start()
         run_step(last_plans, 1)
         gx_steps[0]().wait_recv()
         gx_far[...] = (total[part(2), :] + gx_near_land[1].astype(F32)).astype(BF16)
-        gx_steps[1]().start()
+        gx_steps[2]().start()
+        gx_steps[1]().wait_recv()
         total[part(0), :] = total[part(0), :] + gx_near_land[0].astype(F32)
         gx_write = pltpu.make_async_copy(total.at[part(0)], gx_out, write_sem.at[0])
         gx_write.start()
@@ -723,7 +745,7 @@
         ffn_write.start()
         late_write = pltpu.make_async_copy(late, late_out, write_sem.at[2])
         late_write.start()
-        gx_steps[1]().wait_recv()
+        gx_steps[2]().wait_recv()
         far_write = pltpu.make_async_copy(gx_far_land, gxfar_out, write_sem.at[3])
         far_write.start()
         shared = small[2, LOSS_ROW : LOSS_ROW + 1, :] + small[3, LOSS_ROW : LOSS_ROW + 1, :]
@@ -736,13 +758,13 @@
 
 def attend_backward(qkv, context, source, weight, blocks, ffn_grads, out_grads, small):
     rows, width = source.shape
-    own_rows, head_cols = rows // len(blocks), weight.shape[2]
+    own_rows, head_cols = rows // len(blocks), weight.shape[1]
     cols = 3 * LANES
     heads = head_cols // HEAD_DIM
     levels = (lax.axis_size("dp") - 1).bit_length()
     ffn_rows, late_rows = 2 * ffn_grads.shape[0], (heads + 1) * head_cols
     landing = ffn_rows + late_rows + 8 * 48 * levels
-    transfers = 2 * 4 * 2 * levels + levels + 6
+    transfers = 2 * 4 * 2 * levels + levels + 7
     array = jax.ShapeDtypeStruct
     whole = lambda *shape: pl.BlockSpec(shape, lambda h: (0,) * len(shape))
     head_block = lambda *shape: pl.BlockSpec((1,) + shape, lambda h: (h, 0, 0))
@@ -776,7 +798,7 @@
         ],
         scratch_shapes=[
             pltpu.VMEM((heads, rows, LANES), BF16),
-            pltpu.VMEM((heads, width, cols), BF16),
+            pltpu.VMEM((heads, cols, width), BF16),
             pltpu.VMEM((rows, cols), BF16),
             pltpu.VMEM((LANES, rows), BF16),
             pltpu.VMEM((rows, width), F32),
@@ -1183,9 +1205,75 @@
     )(x_own, *cas, *tcs, *outs, w_up, s_down, vectors, *packs, sums)
 
 
-def projection(weight, bias):
-    rows = jnp.stack([bias[0], jnp.zeros_like(bias[0]), bias[1]]).astype(F32)
-    return weight.transpose(1, 0, 2), jnp.pad(rows, ((0, 5), (0, 0)))
+def finish_kernel(
+    ffn_ref, late_ref, small_ref, gx_ref, gx_far_ref, gh_ref, x_ref, y_ref,
+    up_ref, down_ref, qkv_ref, out_ref, input_ref, y_out, bias_ref, loss_ref, *vectors, tokens
+):
+    up_ref[...] = ffn_ref[0].astype(F32)
+    down_ref[...] = ffn_ref[1].astype(F32)
+    grad = gx_ref[...] + gx_far_ref[...].astype(F32)
+    input_ref[...] = gh_ref[...] + grad * clip_slope(x_ref[...].astype(F32))
+    y_out[...] = y_ref[...]
+
+    @pl.when(pl.program_id(0) == 0)
+    def _():
+        cols = out_ref.shape[0]
+        heads = cols // HEAD_DIM
+        out_ref[...] = late_ref[cols : 2 * cols, :].astype(F32)
+        for h in range(heads):
+            first = 0 if h == 0 else cols + h * cols
+            for c in range(3):
+                rows = slice(first + c * HEAD_DIM, first + (c + 1) * HEAD_DIM)
+                qkv_ref[c, h * HEAD_DIM : (h + 1) * HEAD_DIM, :] = late_ref[rows, :].astype(F32)
+        for index, (lane, factor) in enumerate(((0, 0.125), (2 * LANES, 1.0))):
+            parts = [small_ref[8 + h : 9 + h, lane : lane + HEAD_DIM] for h in range(heads)]
+            bias_ref[index : index + 1, :] = jnp.concatenate(parts, axis=1) * factor
+        for row, vector in zip((0, 1, 2, UP_ROW, 3, 4, 5), vectors):
+            vector[...] = small_ref[row : row + 1, :].reshape(vector.shape)
+        loss_ref[0] = jnp.sum(small_ref[LOSS_ROW : LOSS_ROW + 1, :]) * (1.0 / tokens)
+
+
+def finish(ffn, late, small, gx, gx_far, grad_h, x_own, out_own, head_cols, tokens):
+    own_rows, width = x_own.shape
+    steps = 4
+    array = jax.ShapeDtypeStruct
+    whole = lambda *shape: pl.BlockSpec(shape, lambda i: (0,) * len(shape))
+    by_rows = lambda rows: pl.BlockSpec((rows // steps, width), lambda i: (i, 0))
+    hidden = ffn.shape[0] // 2
+    return pl.pallas_call(
+        functools.partial(finish_kernel, tokens=tokens),
+        grid=(steps,),
+        in_specs=[
+            pl.BlockSpec((2, hidden // steps, width), lambda i: (0, i, 0)),
+            whole(*late.shape),
+            whole(*small.shape),
+        ]
+        + [by_rows(own_rows)] * 5,
+        out_specs=[
+            by_rows(hidden),
+            by_rows(hidden),
+            whole(3, head_cols, width),
+            whole(head_cols, width),
+            by_rows(own_rows),
+            by_rows(own_rows),
+            whole(2, head_cols),
+            pl.BlockSpec(memory_space=pltpu.SMEM),
+        ]
+        + [whole(width)] * 7,
+        out_shape=[
+            array((hidden, width), F32),
+            array((hidden, width), F32),
+            array((3, head_cols, width), F32),
+            array((head_cols, width), F32),
+            array((own_rows, width), F32),
+            array((own_rows, width), BF16),
+            array((2, head_cols), F32),
+            array((1,), F32),
+        ]
+        + [array((width,), F32)] * 7,
+        compiler_params=pltpu.CompilerParams(vmem_limit_bytes=58 * 2**20),
+        name="finish",
+    )(ffn.reshape(2, hidden, width), late, small, gx, gx_far, grad_h, x_own, out_own)
 
 
 def body(
@@ -1222,27 +1310,23 @@
     me = lax.axis_index("tensor")
     all_rows = own_rows * group
     local_cols = qkv_latent.shape[2]
-    local_heads = local_cols // HEAD_DIM
-    near_x = swap(tokens, 1)
-    far_x = swap(tokens, 2)
-    blocks = [tokens, near_x, far_x, swap(far_x, 1)]
-    latents = [out_latent, teacher_out, up_latent, down_latent]
+    blocks = [tokens, swap(tokens, 1), swap(tokens, 2)]
+    qkv_latent, teacher_qkv = qkv_latent.transpose(1, 2, 0), teacher_qkv.transpose(1, 2, 0)
+    latents = [qkv_latent, out_latent, teacher_out, up_latent, down_latent]
     latents += [teacher_up, teacher_down, teacher_up_bias]
     vectors = [out_bias, norm1_gain, norm1_shift, down_bias, norm2_gain, norm2_shift, up_bias]
     vectors += [teacher_out_bias, teacher_norm1_gain, teacher_norm1_shift]
     vectors += [teacher_down_bias, teacher_norm2_gain, teacher_norm2_shift]
-    outs, w_up, s_down, pack, sums, vectors = prepare(latents, vectors)
-    w_qkv = (jnp.mean(jnp.abs(qkv_latent), axis=0) * jnp.sign(qkv_latent)).astype(BF16)
+    w_qkv, outs, w_up, s_down, pack, sums, vectors = prepare(latents, vectors)
     seg_lanes, blocked = segment_tables(seg_lengths[0], parents[0])
     base = jnp.stack([(me ^ j) * own_rows for j in range(group)]).astype(jnp.int32)
 
-    w_three, b_three = projection(w_qkv, qv_bias)
     tables = (seg_lanes, blocked)
     *qkv, context, x_in_all, ca_own, ca_near, ca_far, sums, pack_near, piece_a, outs1, outs2 = attend_forward(
-        base, blocks, w_three, b_three, *tables, [pack, outs, sums], True
+        base, blocks, w_qkv, qv_bias, *tables, [pack, outs, sums], True
     )
     t_last, ta0, ca1, ca2, _, ca3, ta1, ta2, _, ta3, outs3, next_a, piece_b, piece_c = attend_forward(
-        base, blocks, *projection(teacher_qkv, teacher_qv_bias), *tables,
+        base, blocks, teacher_qkv, teacher_qv_bias, *tables,
         [ca_near, ca_far, outs2, piece_a], False,
     )
     cas, outs = [ca_own, ca1, ca2, ca3], [outs, outs1, outs2, outs3]
@@ -1251,35 +1335,24 @@
         tokens, cas, [t_last, ta0, ta1, ta2, ta3], outs, w_up, s_down, vectors, packs, sums
     )
     ffn_grads, late, small, gx_own, gx_far = attend_backward(
-        qkv, context, x_in_all, w_three, [g0, g1, g2, g3], ffn_grads, out_grads, small
+        qkv, context, x_in_all, w_qkv, [g0, g1, g2, g3], ffn_grads, out_grads, small
     )
-    grad_x_in = gx_own + gx_far.astype(F32)
-    input_grad = grad_h + grad_x_in * clip_slope(tokens.astype(F32))
-    ffn_grads = ffn_grads.astype(F32)
-    tree_loss = jnp.sum(small[LOSS_ROW])[None] / (all_rows * model_width)
-    proj_bias_grad = small[8 : 8 + local_heads, : 3 * LANES].reshape(local_heads, 3, LANES)
-    proj_bias_grad = proj_bias_grad[:, :, :HEAD_DIM].transpose(1, 0, 2).reshape(3, local_cols)
-    proj_bias_grad = jnp.stack([proj_bias_grad[0] * 0.125, proj_bias_grad[2]])
-    late = late.astype(F32)
-    qkv_grad = jnp.concatenate([late[:local_cols], late[2 * local_cols :]])
-    qkv_grad = qkv_grad.reshape(local_heads, 3, HEAD_DIM, model_width)
-    qkv_grad = qkv_grad.transpose(3, 1, 0, 2).reshape(model_width, 3, local_cols)
+    up_grad, down_grad, qkv_grad, out_grad, input_grad, out_own, bias_grad, loss, *vectors = finish(
+        ffn_grads, late, small, gx_own, gx_far, grad_h, tokens, out_own, local_cols,
+        all_rows * model_width,
+    )
     return (
         out_own,
-        tree_loss,
+        loss,
         input_grad,
-        qkv_grad,
-        proj_bias_grad,
-        late[local_cols : 2 * local_cols],
-        small[0],
-        small[1],
-        small[2],
-        ffn_grads[:model_width],
-        small[7],
-        ffn_grads[model_width:],
-        small[3],
-        small[4],
-        small[5],
+        qkv_grad.transpose(2, 0, 1),
+        bias_grad,
+        out_grad,
+        *vectors[:3],
+        up_grad,
+        vectors[3],
+        down_grad,
+        *vectors[4:],
     )
 
 

time: 297 us -> 285 us (0.960)
  local copies, waits for them, and re-layouts: 16.2 us -> 1.81 us
  Pallas kernels: 258 us -> 267 us
  other arithmetic: 11.1 us -> 2.32 us
  waiting for transfers between devices: 0.9 us -> 6.25 us
    pallas_call x1 -> x2, Pallas kernels: 7.23 us -> 16.4 us  [the longest x1 8.46 us: prepare(): pl.pallas_call(prepare_kernel, out_shape=[array(qkv_latent.shape, BF16),...]
    slice x7 -> x0, local copies, waits for them, and re-layouts: 7.06 us -> none  [the longest x1 2.62 us: body(): ffn_grads[model_width:]]
    unnamed x21 -> x8, local copies, waits for them, and re-layouts: 7.02 us -> 1.14 us
    ppermute x3 -> x2, waiting for transfers between devices: 0.9 us -> 6.25 us  [swap(): return lax.ppermute(array, 'tensor', [(i, i ^ bit) for i in range(size)])]
    add x1 -> x0, other arithmetic: 3.05 us -> none  [body(): input_grad = grad_h + grad_x_in * clip_slope(tokens.astype(F32))]
  transfers between devices with their start and end apart: 3 -> 2, of which waited for: 1 -> 1; matrix products, arithmetic and copies ran while one was open for 4% -> 1% of each run, Pallas kernels for 2% -> 3%
where the time goes in v6:
time: 285 us; the launch traced here: 281 us
  Pallas kernels  267 us (94%)
  waiting for transfers between devices  6.25 us (2%)
  starting transfers between devices  3.03 us (1%)
    pallas_call x1, Pallas kernels, middle(): pl.pallas_call(middle_kernel, in_specs=[vmem] * 17 + [pl.BlockSpec(memory...  93.8 us
    pallas_call x1, Pallas kernels, attend_backward(): pl.pallas_call(functools.partial(backward_kernel, key_block=256), grid=(h...  93.4 us
    pallas_call x2, Pallas kernels, attend_forward(): pl.pallas_call(functools.partial(forward_kernel, student=student), grid=(...  63.4 us
    pallas_call x1, Pallas kernels, prepare(): pl.pallas_call(prepare_kernel, out_shape=[array(qkv_latent.shape, BF16),...  8.46 us
    pallas_call x1, Pallas kernels, finish(): pl.pallas_call(functools.partial(finish_kernel, tokens=tokens), grid=(ste...  7.93 us
    ppermute x2, waiting for transfers between devices, swap(): return lax.ppermute(array, 'tensor', [(i, i ^ bit) for i in range(size)])  6.25 us
  transfers between devices with their start and end apart: 2, of which 1 were waited for; matrix products, arithmetic and copies ran while one was open for 1% of the time, Pallas kernels for 3%

profile of v6, /device:TPU:0, one launch (start us, length us, event | category | flops | bytes accessed | tf_op | source)
XLA Modules:
  0.0 281.4 jit_solution(2474348625723799531)
XLA Ops:
  0.6 3.0 %collective-permute-start.1 = (bf16[512,768]{1,0:T(8,128)(2,1)}, bf16[512,768]{1,0:T(8,128)(2,1)S(1)}, u32[]{:S(2)}, u32[]{:S(2)}) collective-permute-start(bf16[512,768]{1,0:T(8,128)(2,1)} %x_ref.3), channel_id=1, source_target_pairs={{0,2},{1,3},{2,0},{3,1},{4,6},{5,7},{6,4},{7,5},{8,10},{9,11},{10,... | collective-permute-start | bytes 2359304 | tf_op jit(solution)/shard_map/ppermute | solution.py:74
  3.7 0.0 collective-permute-start
  3.7 0.8 select_reduce_fusion.1
  4.5 0.0 copy-start.3
  4.5 0.0 copy-start
  4.5 8.5 %prepare.1 = (bf16[3,192,768]{2,1,0:T(8,128)(2,1)}, bf16[384,768]{1,0:T(8,128)(2,1)}, bf16[768,768]{1,0:T(8,128)(2,1)}, bf16[768,768]{1,0:T(8,128)(2,1)}, bf16[2...) custom-call(f32[3,192,768]{2,1,0:T(8,128)} %bitcast.16, f32[192,768]{1,0:T(8,128)} %out_ref.1, ...), custom_call_target="tpu_custom_call" | custom-call | flops 16000000000 | bytes 14155776 | tf_op jit(solution)/shard_map/prepare/pallas_call | solution.py:143
  12.9 0.0 copy-done.3
  13.0 0.7 pad.10.seg_ref
  13.6 0.6 pad_add_fusion.1.base_ref
  14.2 0.0 copy-done
  14.2 0.2 select_reduce_fusion
  14.4 0.1 fusion.4
  14.5 0.7 pad_convert_fusion.blocked_ref
  15.2 6.2 %collective-permute-done.1.x2 = bf16[512,768]{1,0:T(8,128)(2,1)S(1)} collective-permute-done((bf16[512,768]{1,0:T(8,128)(2,1)}, bf16[512,768]{1,0:T(8,128)(2,1)S(1)}, u32[]{:S(2)}, u32[]{:S(2)}) %collective-permute-start.1) | collective-permute-done | bytes 786464 | tf_op jit(solution)/shard_map/ppermute | solution.py:74
  21.4 0.0 copy-start.1
  21.4 0.0 collective-permute-done.x1
  21.4 0.0 copy-start.2
  21.4 0.9 copy-done.1
  22.3 0.3 copy-done.2
  22.6 32.4 %student_attention.1 = (bf16[3,2048,128]{2,1,0:T(8,128)(2,1)}, bf16[3,2048,128]{2,1,0:T(8,128)(2,1)}, bf16[3,2048,128]{2,1,0:T(8,128)(2,1)}, f32[3,2048,64]{2,1,...) custom-call(s32[4]{0:T(128)} %pad_add_fusion.1.base_ref, ...), custom_call_target="tpu_custom_call" | custom-call | flops 12884901888 | bytes 12582912 | tf_op jit(solution)/shard_map/student_attention/pallas_call | solution.py:454
  55.0 31.1 %teacher_attention.1 = (bf16[4,256,128]{2,1,0:T(8,128)(2,1)}, bf16[512,128]{1,0:T(8,128)(2,1)}, bf16[512,192]{1,0:T(8,128)(2,1)}, bf16[512,192]{1,0:T(8,128)(2,1...) custom-call(s32[4]{0:T(128)} %pad_add_fusion.1.base_ref, ...), custom_call_target="tpu_custom_call" | custom-call | flops 12884901888 | bytes 12582912 | tf_op jit(solution)/shard_map/teacher_attention/pallas_call | solution.py:454
  86.0 93.8 %middle.1 = (bf16[512,768]{1,0:T(8,128)(2,1)}, f32[512,768]{1,0:T(8,128)}, bf16[768,768]{1,0:T(8,128)(2,1)}, bf16[4,192,768]{2,1,0:T(8,128)(2,1)}, bf16[2,384,12...) custom-call(bf16[512,768]{1,0:T(8,128)(2,1)} %x_ref.3, ...), custom_call_target="tpu_custom_call" | custom-call | flops 36238786560 | bytes 33554432 | tf_op jit(solution)/shard_map/middle/pallas_call | solution.py:1167
  179.9 93.4 %attention_backward.1 = (bf16[1536,768]{1,0:T(8,128)(2,1)}, bf16[768,768]{1,0:T(8,128)(2,1)}, f32[16,768]{1,0:T(8,128)}, f32[512,768]{1,0:T(8,128)}, bf16[512,768]{1,0:T(8,128)(2,1)}) custom-call(bf16[3,2048,128]{2,1,0:T(8,128)(2,1)} %get-tuple-element.80.q_ref, bf16[3,2048,128]{2,1,0:T(8,128)(2,1)} %get-tuple-element.81.k_ref, ...), custom_call_target="tpu_custom_call" | custom-call | flops 48318382080 | bytes 15728640 | tf_op jit(solution)/shard_map/attention_backward/pallas_call | solution.py:772
  273.3 7.9 %finish.1 = (f32[768,768]{1,0:T(8,128)}, f32[768,768]{1,0:T(8,128)}, f32[3,192,768]{2,1,0:T(8,128)}, f32[192,768]{1,0:T(8,128)}, f32[512,768]{1,0:T(8,128)}, /*i...) custom-call(bf16[2,768,768]{2,1,0:T(8,128)(2,1)} %bitcast.12, ...), custom_call_target="tpu_custom_call" | custom-call | tf_op jit(solution)/shard_map/finish/pallas_call | solution.py:1243
  (2 shorter events, 0.0 us)
Async XLA Ops:
  0.6 20.8 %collective-permute-start.1 = (bf16[512,768]{1,0:T(8,128)(2,1)}, bf16[512,768]{1,0:T(8,128)(2,1)S(1)}, u32[]{:S(2)}, u32[]{:S(2)}) collective-permute-start(bf16[512,768]{1,0:T(8,128)(2,1)} %x_ref.3), channel_id=1, source_target_pairs={{0,2},{1,3},{2,0},{3,1},{4,6},{5,7},{6,4},{7,5},{8,10},{9,11},{10,... | collective-permute-start | bytes 2359304 | tf_op jit(solution)/shard_map/ppermute | solution.py:74
  3.7 17.8 %collective-permute-start = (bf16[512,768]{1,0:T(8,128)(2,1)}, bf16[512,768]{1,0:T(8,128)(2,1)S(1)}, u32[]{:S(2)}, u32[]{:S(2)}) collective-permute-start(bf16[512,768]{1,0:T(8,128)(2,1)} %x_ref.3), channel_id=1, source_target_pairs={{0,1},{1,0},{2,3},{3,2},{4,5},{5,4},{6,7},{7,6},{8,9},{9,8},{10,11... | collective-permute-start | bytes 2359304 | tf_op jit(solution)/shard_map/ppermute | solution.py:74
  4.5 8.5 %copy-start.3 = (s32[1,13]{1,0:T(1,128)S(1)}, s32[1,13]{1,0:T(1,128)}, u32[]{:S(2)}) copy-start(s32[1,13]{1,0:T(1,128)} %param.28) | copy-start | bytes 160
  4.5 9.8 %copy-start = (s32[1,13]{1,0:T(1,128)S(1)}, s32[1,13]{1,0:T(1,128)}, u32[]{:S(2)}) copy-start(s32[1,13]{1,0:T(1,128)} %param.29) | copy-start | bytes 160
  21.4 0.9 copy-start.1
  21.4 1.1 copy-start.2

commit v7 on v6

--- a/solution.py
+++ b/solution.py
@@ -530,11 +530,11 @@
 
 
 def backward_kernel(
-    q_ref, k_ref, v_ref, ctx_ref, x_ref, w_ref, g0, g1, g2, g3, ffn_ref, outg_ref, small_ref,
+    q_ref, k_ref, v_ref, ctx_ref, x_hbm, w_ref, g0, g1, g2, g3, ffn_hbm, outg_ref, small_ref,
     ffn_out, late_out, small_out, gx_out, gxfar_out,
     grads, wide, packed, keys_t, total, ffn_part, ffn, late_in, late, small, small_in, landing, small_land,
     out_near, out_near_land, out_far, out_far_land, gx_near, gx_near_land, gx_far, gx_far_land,
-    send_sem, recv_sem, write_sem, *, key_block,
+    x_ref, send_sem, recv_sem, write_sem, *, key_block,
 ):
     blocks = (g0, g1, g2, g3)
     rows = x_ref.shape[0]
@@ -587,11 +587,16 @@
         over_tensor(gx_far, gx_far_land, far_id),
     ]
 
+    load_ffn = lambda: pltpu.make_async_copy(ffn_hbm, ffn_part, write_sem.at[1])
+    load_x = lambda: pltpu.make_async_copy(x_hbm, x_ref, write_sem.at[2])
+
     @pl.when(head == 0)
     def _():
+        load_ffn().start()
+        load_x().start()
         others = [{"tensor": near_id}, {"tensor": far_id}]
         greet(others + [{"dp": in_pair(place, bit)[0]} for bit in bits])
-        ffn_part[...] = ffn_ref[...]
+        load_ffn().wait()
         run_step(ffn_plans, 0)
         out_near[0] = outg_ref[1]
         out_near[1] = outg_ref[3]
@@ -647,6 +652,7 @@
 
     @at(0)
     def _():
+        load_x().wait()
         run_step(ffn_plans, 1)
         out_steps[0]().wait_recv()
         out_far[...] = (outg_ref[2].astype(F32) + out_near_land[1].astype(F32)).astype(BF16)
@@ -777,11 +783,11 @@
             head_block(rows, LANES),
             head_block(rows, LANES),
             head_block(rows, HEAD_DIM),
-            whole(rows, width),
+            anywhere,
             whole(*weight.shape),
         ]
         + [whole(*block.shape) for block in blocks]
-        + [whole(*ffn_grads.shape), whole(*out_grads.shape), whole(*small.shape)],
+        + [anywhere, whole(*out_grads.shape), whole(*small.shape)],
         out_specs=[
             anywhere,
             anywhere,
@@ -818,6 +824,7 @@
             pltpu.VMEM((2, own_rows, width), BF16),
             pltpu.VMEM((own_rows, width), BF16),
             pltpu.VMEM((own_rows, width), BF16),
+            pltpu.VMEM((rows, width), BF16),
             pltpu.SemaphoreType.DMA((transfers,)),
             pltpu.SemaphoreType.DMA((transfers,)),
             pltpu.SemaphoreType.DMA((4,)),

time: 285 us -> 283 us (level)
  no operation moved by 1% of the time
where the time goes in v7:
time: 283 us; the launch traced here: 279 us
  Pallas kernels  265 us (94%)
  waiting for transfers between devices  6.25 us (2%)
  starting transfers between devices  3.03 us (1%)
    pallas_call x1, Pallas kernels, middle(): pl.pallas_call(middle_kernel, in_specs=[vmem] * 17 + [pl.BlockSpec(memory...  93.8 us
    pallas_call x1, Pallas kernels, attend_backward(): pl.pallas_call(functools.partial(backward_kernel, key_block=256), grid=(h...  91.4 us
    pallas_call x2, Pallas kernels, attend_forward(): pl.pallas_call(functools.partial(forward_kernel, student=student), grid=(...  63.4 us
    pallas_call x1, Pallas kernels, prepare(): pl.pallas_call(prepare_kernel, out_shape=[array(qkv_latent.shape, BF16),...  8.46 us
    pallas_call x1, Pallas kernels, finish(): pl.pallas_call(functools.partial(finish_kernel, tokens=tokens), grid=(ste...  7.93 us
    ppermute x2, waiting for transfers between devices, swap(): return lax.ppermute(array, 'tensor', [(i, i ^ bit) for i in range(size)])  6.25 us
  transfers between devices with their start and end apart: 2, of which 1 were waited for; matrix products, arithmetic and copies ran while one was open for 1% of the time, Pallas kernels for 3%

profile of v7, /device:TPU:0, one launch (start us, length us, event | category | flops | bytes accessed | tf_op | source)
XLA Modules:
  0.0 279.4 jit_solution(14905308746327826755)
XLA Ops:
  0.6 3.0 %collective-permute-start.1 = (bf16[512,768]{1,0:T(8,128)(2,1)}, bf16[512,768]{1,0:T(8,128)(2,1)S(1)}, u32[]{:S(2)}, u32[]{:S(2)}) collective-permute-start(bf16[512,768]{1,0:T(8,128)(2,1)} %x_ref.3), channel_id=1, source_target_pairs={{0,2},{1,3},{2,0},{3,1},{4,6},{5,7},{6,4},{7,5},{8,10},{9,11},{10,... | collective-permute-start | bytes 2359304 | tf_op jit(solution)/shard_map/ppermute | solution.py:74
  3.7 0.0 collective-permute-start
  3.7 0.8 select_reduce_fusion.1
  4.5 0.0 copy-start.3
  4.5 0.0 copy-start
  4.5 8.5 %prepare.1 = (bf16[3,192,768]{2,1,0:T(8,128)(2,1)}, bf16[384,768]{1,0:T(8,128)(2,1)}, bf16[768,768]{1,0:T(8,128)(2,1)}, bf16[768,768]{1,0:T(8,128)(2,1)}, bf16[2...) custom-call(f32[3,192,768]{2,1,0:T(8,128)} %bitcast.16, f32[192,768]{1,0:T(8,128)} %out_ref.1, ...), custom_call_target="tpu_custom_call" | custom-call | flops 16000000000 | bytes 14155776 | tf_op jit(solution)/shard_map/prepare/pallas_call | solution.py:143
  12.9 0.0 copy-done.3
  13.0 0.7 pad.10.seg_ref
  13.6 0.6 pad_add_fusion.1.base_ref
  14.2 0.0 copy-done
  14.2 0.2 select_reduce_fusion
  14.4 0.1 fusion.4
  14.5 0.7 pad_convert_fusion.blocked_ref
  15.2 6.2 %collective-permute-done.1.x2 = bf16[512,768]{1,0:T(8,128)(2,1)S(1)} collective-permute-done((bf16[512,768]{1,0:T(8,128)(2,1)}, bf16[512,768]{1,0:T(8,128)(2,1)S(1)}, u32[]{:S(2)}, u32[]{:S(2)}) %collective-permute-start.1) | collective-permute-done | bytes 786464 | tf_op jit(solution)/shard_map/ppermute | solution.py:74
  21.4 0.0 copy-start.1
  21.4 0.0 collective-permute-done.x1
  21.4 0.0 copy-start.2
  21.4 0.9 copy-done.1
  22.3 0.3 copy-done.2
  22.6 32.4 %student_attention.1 = (bf16[3,2048,128]{2,1,0:T(8,128)(2,1)}, bf16[3,2048,128]{2,1,0:T(8,128)(2,1)}, bf16[3,2048,128]{2,1,0:T(8,128)(2,1)}, f32[3,2048,64]{2,1,...) custom-call(s32[4]{0:T(128)} %pad_add_fusion.1.base_ref, ...), custom_call_target="tpu_custom_call" | custom-call | flops 12884901888 | bytes 12582912 | tf_op jit(solution)/shard_map/student_attention/pallas_call | solution.py:454
  55.0 31.1 %teacher_attention.1 = (bf16[4,256,128]{2,1,0:T(8,128)(2,1)}, bf16[512,128]{1,0:T(8,128)(2,1)}, bf16[512,192]{1,0:T(8,128)(2,1)}, bf16[512,192]{1,0:T(8,128)(2,1...) custom-call(s32[4]{0:T(128)} %pad_add_fusion.1.base_ref, ...), custom_call_target="tpu_custom_call" | custom-call | flops 12884901888 | bytes 12582912 | tf_op jit(solution)/shard_map/teacher_attention/pallas_call | solution.py:454
  86.0 93.8 %middle.1 = (bf16[512,768]{1,0:T(8,128)(2,1)}, f32[512,768]{1,0:T(8,128)}, bf16[768,768]{1,0:T(8,128)(2,1)}, bf16[4,192,768]{2,1,0:T(8,128)(2,1)}, bf16[2,384,12...) custom-call(bf16[512,768]{1,0:T(8,128)(2,1)} %x_ref.3, ...), custom_call_target="tpu_custom_call" | custom-call | flops 36238786560 | bytes 33554432 | tf_op jit(solution)/shard_map/middle/pallas_call | solution.py:1174
  179.9 91.4 %attention_backward.1 = (bf16[1536,768]{1,0:T(8,128)(2,1)}, bf16[768,768]{1,0:T(8,128)(2,1)}, f32[16,768]{1,0:T(8,128)}, f32[512,768]{1,0:T(8,128)}, bf16[512,768]{1,0:T(8,128)(2,1)}) custom-call(bf16[3,2048,128]{2,1,0:T(8,128)(2,1)} %get-tuple-element.80.q_ref, bf16[3,2048,128]{2,1,0:T(8,128)(2,1)} %get-tuple-element.81.k_ref, ...), custom_call_target="tpu_custom_call" | custom-call | flops 48318382080 | bytes 15728640 | tf_op jit(solution)/shard_map/attention_backward/pallas_call | solution.py:778
  271.2 7.9 %finish.1 = (f32[768,768]{1,0:T(8,128)}, f32[768,768]{1,0:T(8,128)}, f32[3,192,768]{2,1,0:T(8,128)}, f32[192,768]{1,0:T(8,128)}, f32[512,768]{1,0:T(8,128)}, /*i...) custom-call(bf16[2,768,768]{2,1,0:T(8,128)(2,1)} %bitcast.12, ...), custom_call_target="tpu_custom_call" | custom-call | tf_op jit(solution)/shard_map/finish/pallas_call | solution.py:1250
  (2 shorter events, 0.0 us)
Async XLA Ops:
  0.6 20.8 %collective-permute-start.1 = (bf16[512,768]{1,0:T(8,128)(2,1)}, bf16[512,768]{1,0:T(8,128)(2,1)S(1)}, u32[]{:S(2)}, u32[]{:S(2)}) collective-permute-start(bf16[512,768]{1,0:T(8,128)(2,1)} %x_ref.3), channel_id=1, source_target_pairs={{0,2},{1,3},{2,0},{3,1},{4,6},{5,7},{6,4},{7,5},{8,10},{9,11},{10,... | collective-permute-start | bytes 2359304 | tf_op jit(solution)/shard_map/ppermute | solution.py:74
  3.7 17.8 %collective-permute-start = (bf16[512,768]{1,0:T(8,128)(2,1)}, bf16[512,768]{1,0:T(8,128)(2,1)S(1)}, u32[]{:S(2)}, u32[]{:S(2)}) collective-permute-start(bf16[512,768]{1,0:T(8,128)(2,1)} %x_ref.3), channel_id=1, source_target_pairs={{0,1},{1,0},{2,3},{3,2},{4,5},{5,4},{6,7},{7,6},{8,9},{9,8},{10,11... | collective-permute-start | bytes 2359304 | tf_op jit(solution)/shard_map/ppermute | solution.py:74
  4.5 8.5 %copy-start.3 = (s32[1,13]{1,0:T(1,128)S(1)}, s32[1,13]{1,0:T(1,128)}, u32[]{:S(2)}) copy-start(s32[1,13]{1,0:T(1,128)} %param.28) | copy-start | bytes 160
  4.5 9.8 %copy-start = (s32[1,13]{1,0:T(1,128)S(1)}, s32[1,13]{1,0:T(1,128)}, u32[]{:S(2)}) copy-start(s32[1,13]{1,0:T(1,128)} %param.29) | copy-start | bytes 160
  21.4 0.9 copy-start.1
  21.4 1.1 copy-start.2
